TPU v7x, 128 devices: a whole 4x4x4 slice. The times are simulated.
128 devices in a mesh: shard: 32 (over z, x_hi, y), rep: 4 (over x_lo, core).
Axes of the slice: x: 4 (x_hi: 2, x_lo: 2; x = x_hi * 2 + x_lo), y: 4, z: 4, core: 2. Of those that a mesh axis runs over, the one named last changes fastest.
Arguments:
- weights: bfloat16 [6144, 196608], P('rep', 'shard'), may hold values from -12 to 12
- keep_mask: int32 [48, 1536], P('rep', 'shard'), may hold values from 0 to 1, as said below
- test_matrix: bfloat16 [196608, 128], P('shard'), may hold values from -6 to 6
Outputs:
- range_basis: float32 [6144, 128], P('rep')
- projection: float32 [196608, 128], P(('shard', 'rep'))
Inputs may be any that keep to these rules, and one draw needn't show every extreme that they name: `keep_mask`: each device's 12 x 48 blocks hold at most 144 kept blocks, and some device holds exactly 144; every device holds at least one; all devices of one column shard hold equally many.
All inputs are finite; a program needn't handle non-finite values.
Results may differ from a plain program's by a relative error of at most 0.0028.
Values sent between devices are 32-bit elements; how exact they have to be, the bound alone decides.
No kernel may reach another device: no remote copies, remote signals or barrier semaphores. Data moves between devices by JAX's collectives and lax.ppermute only.
A program may use at most 128 MiB of HBM per device.

v0:
```python
import math

import jax
import jax.numpy as jnp
from jax import lax
from jax.sharding import PartitionSpec as P

D = 6144
BLOCK = 128


def gram_of(rows_part):
    return lax.dot_general(
        rows_part, rows_part, (((0,), (0,)), ((), ())), precision=lax.Precision.HIGHEST
    )


def orthonormal(sketch_part, gram_matrix):
    factor = jnp.linalg.cholesky(gram_matrix)
    return lax.linalg.triangular_solve(
        factor, sketch_part, left_side=False, lower=True, transpose_a=True
    )


def shards(weights, keep_mask, test_matrix):
    row_blocks, col_blocks = keep_mask.shape
    local_rows, width = weights.shape
    quad = weights.reshape(row_blocks, BLOCK, col_blocks, BLOCK)
    masked = (quad * keep_mask[:, None, :, None].astype(weights.dtype)).reshape(local_rows, width)
    partial_sketch = jnp.dot(masked, test_matrix, preferred_element_type=jnp.float32)
    sketch = lax.psum(partial_sketch, "shard")
    gram_matrix = lax.psum(gram_of(sketch), "rep")
    basis = orthonormal(sketch, gram_matrix)
    projection = lax.psum_scatter(
        lax.dot_general(
            masked,
            basis.astype(jnp.bfloat16),
            (((0,), (0,)), ((), ())),
            preferred_element_type=jnp.float32,
        ),
        "rep",
        scatter_dimension=0,
        tiled=True,
    )
    return (basis * math.sqrt(D), projection)


def solution(mesh):
    placed = (P("rep", "shard"), P("rep", "shard"), P("shard", None))
    return jax.shard_map(
        shards,
        mesh=mesh,
        in_specs=placed,
        out_specs=(P("rep", None), P(("shard", "rep"), None)),
        check_vma=False,
    )
```

profile of v0, /device:TPU:1, one launch (start us, length us, event | category | flops | bytes accessed | tf_op | source)
XLA Modules:
  0.0 517.5 jit_solution(3500606130979041880)
XLA Ops:
  7.2 0.0 copy-start
  7.2 0.0 all-reduce.3.cloned.1.call-start
  7.2 0.8 convert_element_type.7
  8.0 7.0 %mul.17 = bf16[12,128,48,128]{3,2,1,0:T(8,128)(2,1)} broadcast(bf16[12,48]{1,0:T(8,128)(2,1)S(1)} %convert_element_type.7), dimensions={0,2} | broadcast | bytes 18875520 | tf_op jit(solution)/shard_map/mul | solution.py:29
  15.0 0.0 copy-done
  15.0 16.4 %fusion.1 = f32[1536,128]{1,0:T(8,128)} fusion(bf16[6144,128]{1,0:T(8,128)(2,1)S(1)} %copy-done, bf16[1536,6144]{1,0:T(8,128)(2,1)} %param.3, bf16[192,8,48,128]{3,2,1,0:T(8,128)(2,1)} %bitcast.22), kind=kOutput, calls=%fused_computation.2 | convolution fusion | flops 2425356288 | bytes 40108032 | tf_op jit(solution)/shard_map/dot_general | solution.py:30
  31.4 0.0 all-reduce.3.cloned.1.call-update
  31.4 0.0 all-reduce.5.cloned.1.call-start
  31.5 333.8 %all-reduce.3.cloned.1.call-done = f32[1536,128]{1,0:T(8,128)} async-done(((f32[1536,128]{1,0:T(8,128)}), f32[1536,128]{1,0:T(8,128)}) %all-reduce.3.cloned.1.call-update) | async-done | bytes 786448 | tf_op jit(solution)/shard_map/psum | solution.py:31
  365.3 3.4 fusion.7
  368.8 0.0 all-reduce.5.cloned.1.call-update
  368.8 0.2 reduce-scatter.2.cloned.1.call-start
  369.0 57.7 %all-reduce.5.cloned.1.call-done = f32[128,128]{0,1:T(8,128)} async-done(((f32[128,128]{0,1:T(8,128)}), f32[128,128]{0,1:T(8,128)}) %all-reduce.5.cloned.1.call-update) | async-done | bytes 65552 | tf_op jit(solution)/shard_map/psum | solution.py:32
  426.7 0.9 copy.6
  427.6 0.9 fusion.6
  428.5 11.7 %cholesky.16 = f32[128,128]{1,0:T(8,128)S(1)} custom-call(f32[128,128]{1,0:T(8,128)S(1)} %fusion.6), custom_call_target="Cholesky" | custom-call | tf_op jit(solution)/shard_map/jit(cholesky)/cholesky | solution.py:19
  440.2 0.6 compare_reduce_fusion
  440.9 0.7 fusion.3
  441.5 9.8 %custom-call.6 = f32[1,128,128]{1,2,0:T(8,128)S(1)} custom-call(f32[1,128,128]{2,1,0:T(8,128)S(1)} %fusion.3), custom_call_target="InvertDiagBlocksLowerTriangular" | custom-call | tf_op jit(solution)/shard_map/triangular_solve | solution.py:20
  451.4 2.8 broadcast_multiply_fusion
  454.1 19.1 %fusion = f32[6144,128]{1,0:T(8,128)} fusion(bf16[1536,6144]{1,0:T(8,128)(2,1)} %param.3, bf16[192,8,48,128]{3,2,1,0:T(8,128)(2,1)} %bitcast.23, bf16[1536,128]{1,0:T(8,128)(2,1)S(1)} %get-tuple-element.3), kind=kOutput, calls=%fused_computation.1 | convolution fusion | flops 2425356288 | bytes 41287680 | tf_op jit(solution)/shard_map/dot_general | solution.py:35
  473.3 0.0 reduce-scatter.2.cloned.1.call-update
  473.3 37.7 %reduce-scatter.2.cloned.1.call-done = f32[1536,128]{1,0:T(8,128)} async-done(((f32[6144,128]{1,0:T(8,128)}), f32[1536,128]{1,0:T(8,128)}) %reduce-scatter.2.cloned.1.call-update) | async-done | bytes 786448 | tf_op jit(solution)/shard_map/reduce_scatter | solution.py:34
  (1 shorter events, 0.0 us)
Async XLA Ops:
  7.2 7.8 %copy-start = (bf16[6144,128]{1,0:T(8,128)(2,1)S(1)}, bf16[6144,128]{1,0:T(8,128)(2,1)}, u32[]{:S(2)}) copy-start(bf16[6144,128]{1,0:T(8,128)(2,1)} %param.5) | copy-start | bytes 4718596
  7.2 358.2 %all-reduce.3.cloned.1.call-start = ((), (), s32[]{:S(2)}) async-start(), calls=%async_computation.1 | async-start | bytes 1572864 | tf_op jit(solution)/shard_map/psum | solution.py:31
  31.4 395.3 %all-reduce.5.cloned.1.call-start = ((), (), s32[]{:S(2)}) async-start(), calls=%async_computation.2 | async-start | bytes 131072 | tf_op jit(solution)/shard_map/psum | solution.py:32
  368.8 142.2 %reduce-scatter.2.cloned.1.call-start = ((), (), s32[]{:S(2)}) async-start(), calls=%async_computation.3 | async-start | bytes 3932160 | tf_op jit(solution)/shard_map/reduce_scatter | solution.py:34
Sparse Core Ops, SparseCore 0:
  31.6 333.7 all-reduce.2
  368.9 57.7 all-reduce.4
  473.4 37.5 reduce-scatter.1
where the time goes:
time: 518 us
  waiting for transfers between devices  429 us (83%)
  matrix products  41.8 us (8%)
  other arithmetic  24.5 us (5%)
  between operations  13.8 us (3%)
  local copies, waits for them, and re-layouts  7.9 us (2%)
    psum x1, waiting for transfers between devices, shards(): sketch = lax.psum(partial_sketch, 'shard')  334 us
    psum x1, waiting for transfers between devices, shards(): gram_matrix = lax.psum(gram_of(sketch), 'rep')  57.7 us
    reduce_scatter x1, waiting for transfers between devices, shards(): lax.psum_scatter(lax.dot_general(masked, basis.astype(jnp.bfloat16), (((0...  37.7 us
    dot_general x1, matrix products, shards(): lax.dot_general(masked, basis.astype(jnp.bfloat16), (((0,), (0,)), ((), (...  19.1 us
    dot_general x1, matrix products, shards(): jnp.dot(masked, test_matrix, preferred_element_type=jnp.float32)  16.4 us
    another operation x3, other arithmetic, orthonormal(): factor = jnp.linalg.cholesky(gram_matrix)  12.4 us
    another operation x2, other arithmetic, orthonormal(): lax.linalg.triangular_solve(factor, sketch_part, left_side=False, lower=T...  10.5 us
  transfers between devices with their start and end apart: 3, of which 3 were waited for; matrix products, arithmetic and copies ran while one was open for 0% of the time, Pallas kernels for 0%

commit v1 on v0

v1 whole, which is shorter than its diff:
```python
import itertools
import math

import jax
import jax.numpy as jnp
from jax import lax
from jax.experimental import pallas as pl
from jax.experimental.pallas import tpu as pltpu
from jax.sharding import PartitionSpec as P

D = 6144
K = 128
BLOCK = 128
ROWS = 1536
WIDTH = 6144
QUARTER = ROWS // 4
SUB = QUARTER // 4
PANEL = 1536
TILE = 256
AXES = ("shard", "rep")
HIGHEST = lax.Precision.HIGHEST

FOLD_A, FOLD_B = (1, 0, 3, 2), (3, 2, 1, 0)
LABEL_A, LABEL_B = (0, 1, 1, 0), (0, 0, 1, 1)


def device(z, x_hi, y, x_lo, core):
    return ((z * 2 + x_hi) * 4 + y) * 4 + x_lo * 2 + core


PLACES = list(itertools.product(range(4), range(2), range(4), range(2), range(2)))


def pairs(partner):
    return [(device(*place), device(*partner(*place))) for place in PLACES]


def square(first, bits):
    def partner(z, x_hi, y, x_lo, core):
        fold = FOLD_A if (core == 0) == first else FOLD_B
        return (fold[z] if bits & 1 else z, x_hi, fold[y] if bits & 2 else y, x_lo, core)

    return pairs(partner)


ACROSS = pairs(lambda z, x_hi, y, x_lo, core: (z, 1 - x_hi, y, x_lo, core))
CORES = pairs(lambda z, x_hi, y, x_lo, core: (z, x_hi, y, x_lo, 1 - core))
CHIPS = pairs(lambda z, x_hi, y, x_lo, core: (z, x_hi, y, 1 - x_lo, core))


def swap(value, perm):
    return lax.ppermute(value, AXES, perm)


def label(table, place):
    return sum(jnp.where(place == i, v, 0) for i, v in enumerate(table) if v)


def position():
    shard, rep = lax.axis_index("shard"), lax.axis_index("rep")
    y, z = lax.rem(shard, 4), shard // 8
    core, x_lo = lax.rem(rep, 2), rep // 2
    a = 2 * label(LABEL_A, y) + label(LABEL_A, z)
    b = 2 * label(LABEL_B, y) + label(LABEL_B, z)
    return jnp.stack([jnp.where(core == 0, a, b), jnp.where(core == 0, b, a), x_lo, core]).astype(jnp.int32)


def masked(tile, keep, row_block, col_block):
    rows, cols = tile.shape
    return jnp.concatenate(
        [
            jnp.concatenate(
                [
                    tile[r * BLOCK : (r + 1) * BLOCK, c * BLOCK : (c + 1) * BLOCK]
                    * keep[row_block + r, col_block + c].astype(jnp.float32).astype(tile.dtype)
                    for c in range(cols // BLOCK)
                ],
                axis=1,
            )
            for r in range(rows // BLOCK)
        ],
        axis=0,
    )


def sketch_kernel(first, place, keep, weights, test, *rest):
    outs, total = rest[:2], rest[2]
    panel, which = pl.program_id(0), pl.program_id(1)
    quarter = place[0] ^ (first + which)
    tile = masked(weights[...], keep, quarter * (QUARTER // BLOCK), panel * (PANEL // BLOCK))
    part = jnp.dot(tile, test[...], preferred_element_type=jnp.float32)

    @pl.when(panel == 0)
    def _():
        total[which] = part

    @pl.when(panel > 0)
    def _():
        total[which] += part

    @pl.when(panel == WIDTH // PANEL - 1)
    def _():
        for i, out in enumerate(outs):

            @pl.when(which == i)
            def _():
                for m in range(4):
                    start = pl.multiple_of((place[1] ^ m) * SUB, 8)
                    out[m * SUB : (m + 1) * SUB, :] = total[i, pl.ds(start, SUB), :]


def sketch_parts(first, place, keep_mask, weights, test_matrix):
    return pl.pallas_call(
        lambda *refs: sketch_kernel(first, *refs),
        grid_spec=pltpu.PrefetchScalarGridSpec(
            num_scalar_prefetch=2,
            grid=(WIDTH // PANEL, 2),
            in_specs=[
                pl.BlockSpec((QUARTER, PANEL), lambda j, k, place, keep: (place[0] ^ (first + k), j)),
                pl.BlockSpec((PANEL, K), lambda j, k, place, keep: (j, 0)),
            ],
            out_specs=[pl.BlockSpec((QUARTER, K), lambda j, k, place, keep: (0, 0))] * 2,
            scratch_shapes=[pltpu.VMEM((2, QUARTER, K), jnp.float32)],
        ),
        out_shape=[jax.ShapeDtypeStruct((QUARTER, K), jnp.float32)] * 2,
        compiler_params=pltpu.CompilerParams(vmem_limit_bytes=32 * 2**20),
        cost_estimate=pl.CostEstimate(flops=2 * 2 * QUARTER * WIDTH * K, bytes_accessed=2 * QUARTER * WIDTH * 2, transcendentals=0),
        name="sketch",
    )(place, keep_mask, weights, test_matrix)


def turn_kernel(place, *refs):
    parts, out, rows = refs[:4], refs[4], refs[5]
    for m in range(4):
        rows[pl.ds(pl.multiple_of((place[1] ^ m) * SUB, 8), SUB), :] = parts[m][...]
    out[...] = rows[...].T


def turn(place, parts):
    return pl.pallas_call(
        turn_kernel,
        in_specs=[pl.BlockSpec(memory_space=pltpu.SMEM)] + [pl.BlockSpec(memory_space=pltpu.VMEM)] * 4,
        out_specs=pl.BlockSpec(memory_space=pltpu.VMEM),
        out_shape=jax.ShapeDtypeStruct((K, QUARTER), jnp.float32),
        scratch_shapes=[pltpu.VMEM((QUARTER, K), jnp.float32)],
        name="turn",
    )(place, *parts)


def gram_kernel(place, *refs):
    parts, out, whole = refs[:4], refs[4], refs[5]
    for k in range(4):
        whole[:, pl.ds(pl.multiple_of((place[0] ^ k) * QUARTER, BLOCK), QUARTER)] = parts[k][...]
    out[...] = lax.dot_general(
        whole[...], whole[...], (((1,), (1,)), ((), ())), precision=HIGHEST, preferred_element_type=jnp.float32
    )


def gram_of(place, parts):
    return pl.pallas_call(
        gram_kernel,
        in_specs=[pl.BlockSpec(memory_space=pltpu.SMEM)] + [pl.BlockSpec(memory_space=pltpu.VMEM)] * 4,
        out_specs=pl.BlockSpec(memory_space=pltpu.VMEM),
        out_shape=jax.ShapeDtypeStruct((K, K), jnp.float32),
        scratch_shapes=[pltpu.VMEM((K, ROWS), jnp.float32)],
        cost_estimate=pl.CostEstimate(flops=12 * ROWS * K * K, bytes_accessed=4 * ROWS * K, transcendentals=0),
        name="gram",
    )(place, *parts)


def inverse_factor_kernel(mine, theirs, out, step=4):
    gram = mine[...] + theirs[...]
    lanes = lax.broadcasted_iota(jnp.int32, (K, K), 1)
    rows = lax.broadcasted_iota(jnp.int32, (K, K), 0)
    unit = jnp.where(lanes == rows, 1.0, 0.0).astype(jnp.float32)
    for top in range(0, K, step):
        left = K - top
        column = [jnp.broadcast_to(gram[:, top + i : top + i + 1], (left, K)) for i in range(step)]
        row = [gram[i : i + 1, :] for i in range(step)]
        side = [unit[i : i + 1, :] for i in range(step)]
        for i in range(step):
            pivot = column[i][i : i + 1, :]
            inverse = 1.0 / pivot
            for m in range(i + 1, step):
                factor = column[i][m : m + 1, :] * inverse
                column[m] = column[m] - column[i] * factor
                row[m] = row[m] - row[i] * factor
                side[m] = side[m] - side[i] * factor
            out[top + i : top + i + 1, :] = side[i] * lax.rsqrt(pivot)
            row[i] = row[i] * inverse
            side[i] = side[i] * inverse
        if left > step:
            gram, unit = gram[step:], unit[step:]
            for i in range(step):
                gram = gram - column[i][step:] * row[i]
                unit = unit - column[i][step:] * side[i]


def inverse_factor(mine, theirs):
    return pl.pallas_call(
        inverse_factor_kernel,
        in_specs=[pl.BlockSpec(memory_space=pltpu.VMEM)] * 2,
        out_specs=pl.BlockSpec(memory_space=pltpu.VMEM),
        out_shape=jax.ShapeDtypeStruct((K, K), jnp.float32),
        cost_estimate=pl.CostEstimate(flops=10**9, bytes_accessed=2 * 10**7, transcendentals=0),
        name="inverse_factor",
    )(mine, theirs)


def projection_kernel(place, keep, first, tiles, *refs):
    parts, weights, outs, sketch = refs[:4], refs[4], refs[5:7], refs[7]
    t = pl.program_id(0)

    @pl.when(t == 0)
    def _():
        for k in range(4):
            at = pl.ds(pl.multiple_of((place[0] ^ k) * QUARTER, BLOCK), QUARTER)
            high = parts[k][...].astype(jnp.bfloat16)
            sketch[0:K, at] = high
            sketch[K : 2 * K, at] = (parts[k][...] - high.astype(jnp.float32)).astype(jnp.bfloat16)

    tile = masked(weights[...], keep, 0, first(t, place) * (TILE // BLOCK))
    both = jnp.dot(sketch[...], tile, preferred_element_type=jnp.float32)
    total = both[:K] + both[K:]
    for i, out in enumerate(outs):

        @pl.when(t // tiles == i)
        def _():
            out[...] = total


def projection_parts(place, keep_mask, weights, parts, near, offset, count):
    tiles = count // TILE

    def first(t, place):
        chip = place[2] if near else 1 - place[2]
        core = jnp.where(t < tiles, 1 - place[3], place[3])
        return (chip * 2 + core) * (WIDTH // 4 // TILE) + offset // TILE + lax.rem(t, tiles)

    return pl.pallas_call(
        lambda place, keep, *refs: projection_kernel(place, keep, first, tiles, *refs),
        grid_spec=pltpu.PrefetchScalarGridSpec(
            num_scalar_prefetch=2,
            grid=(2 * tiles,),
            in_specs=[pl.BlockSpec((K, QUARTER), lambda t, place, keep: (0, 0))] * 4
            + [pl.BlockSpec((ROWS, TILE), lambda t, place, keep: (0, first(t, place)))],
            out_specs=[
                pl.BlockSpec((K, TILE), lambda t, place, keep: (0, jnp.minimum(t, tiles - 1))),
                pl.BlockSpec((K, TILE), lambda t, place, keep: (0, jnp.maximum(t - tiles, 0))),
            ],
            scratch_shapes=[pltpu.VMEM((2 * K, ROWS), jnp.bfloat16)],
        ),
        out_shape=[jax.ShapeDtypeStruct((K, count), jnp.float32)] * 2,
        compiler_params=pltpu.CompilerParams(vmem_limit_bytes=32 * 2**20),
        cost_estimate=pl.CostEstimate(flops=8 * ROWS * K * count, bytes_accessed=4 * ROWS * count, transcendentals=0),
        name="project",
    )(place, keep_mask, *parts, weights)


def basis_kernel(place, inverse, *refs):
    parts, out = refs[:4], refs[4]
    t = pl.program_id(0)
    for k in range(4):

        @pl.when((place[0] ^ k) == t)
        def _():
            turned = jnp.dot(inverse[...], parts[k][...], precision=HIGHEST, preferred_element_type=jnp.float32)
            out[...] = (turned * math.sqrt(D)).T


def range_basis_of(place, inverse, parts):
    return pl.pallas_call(
        basis_kernel,
        grid_spec=pltpu.PrefetchScalarGridSpec(
            num_scalar_prefetch=1,
            grid=(4,),
            in_specs=[pl.BlockSpec((K, K), lambda t, place: (0, 0))]
            + [pl.BlockSpec((K, QUARTER), lambda t, place: (0, 0))] * 4,
            out_specs=pl.BlockSpec((QUARTER, K), lambda t, place: (t, 0)),
        ),
        out_shape=jax.ShapeDtypeStruct((ROWS, K), jnp.float32),
        cost_estimate=pl.CostEstimate(flops=12 * ROWS * K * K, bytes_accessed=8 * ROWS * K, transcendentals=0),
        name="basis",
    )(place, inverse, *parts)


def finish_kernel(inverse, here, core, far_a, far_b, out):
    t = pl.program_id(0)
    for i, far in enumerate((far_a, far_b)):

        @pl.when(t // 2 == i)
        def _():
            total = here[...] + core[...] + far[...]
            out[...] = jnp.dot(inverse[...], total, precision=HIGHEST, preferred_element_type=jnp.float32).T


def finish(inverse, here, core, far_a, far_b):
    half = pl.BlockSpec((K, QUARTER), lambda t: (0, t))
    return pl.pallas_call(
        finish_kernel,
        grid=(4,),
        in_specs=[
            pl.BlockSpec((K, K), lambda t: (0, 0)),
            half,
            half,
            pl.BlockSpec((K, QUARTER), lambda t: (0, jnp.minimum(t, 1))),
            pl.BlockSpec((K, QUARTER), lambda t: (0, jnp.maximum(t - 2, 0))),
        ],
        out_specs=pl.BlockSpec((QUARTER, K), lambda t: (t, 0)),
        out_shape=jax.ShapeDtypeStruct((ROWS, K), jnp.float32),
        cost_estimate=pl.CostEstimate(flops=12 * ROWS * K * K, bytes_accessed=16 * ROWS * K, transcendentals=0),
        name="finish",
    )(inverse, here, core, far_a, far_b)


def shards(weights, keep_mask, test_matrix):
    place = position()

    three = sketch_parts(2, place, keep_mask, weights, test_matrix)
    got3, got2 = swap(three[1], square(True, 3)), swap(three[0], square(True, 2))
    own = sketch_parts(0, place, keep_mask, weights, test_matrix)
    got1 = swap(own[1], square(True, 1))
    quarter = own[0] + got1 + got2 + got3
    piece = [quarter[m * SUB : (m + 1) * SUB] for m in range(4)]
    got = [swap(piece[m], square(False, m)) for m in (3, 2, 1)]
    sub = piece[0] + got[2] + got[1] + got[0]
    sub = sub + swap(sub, ACROSS)

    got = {m: swap(sub, square(False, m)) for m in (3, 2, 1)}
    mine = turn(place, (sub, got[1], got[2], got[3]))
    got = {k: swap(mine, square(True, k)) for k in (3, 2, 1)}
    parts = (mine, got[1], got[2], got[3])

    half = WIDTH // 8
    far = []
    for i in range(2):
        send, stay = projection_parts(place, keep_mask, weights, parts, False, i * half, half)
        far.append(swap(stay + swap(send, CORES), CHIPS))
    send, here = projection_parts(place, keep_mask, weights, parts, True, 0, 2 * half)
    core = swap(send, CORES)

    gram = gram_of(place, parts)
    gram = gram + swap(gram, CORES)
    inverse = inverse_factor(gram, swap(gram, CHIPS))
    return range_basis_of(place, inverse, parts), finish(inverse, here, core, *far)


def solution(mesh):
    placed = (P("rep", "shard"), P("rep", "shard"), P("shard", None))
    return jax.shard_map(
        shards,
        mesh=mesh,
        in_specs=placed,
        out_specs=(P("rep", None), P(("shard", "rep"), None)),
        check_vma=False,
    )
```

time: 518 us -> 136 us (0.26)
  waiting for transfers between devices: 429 us -> 34.1 us
  Pallas kernels: 0 us -> 47 us
  matrix products: 41.8 us -> 0 us
  starting transfers between devices: 0.3 us -> 32.8 us
  other arithmetic: 24.5 us -> 1.13 us
  between operations: 13.8 us -> 0.86 us
  local copies, waits for them, and re-layouts: 7.9 us -> 19.7 us
    psum x2 -> x0, waiting for transfers between devices: 392 us -> none  [the longest x1 334 us: shards(): sketch = lax.psum(partial_sketch, 'shard')]
    pallas_call x0 -> x10, Pallas kernels: none -> 47 us  [the longest x3 16.4 us: projection_parts(): pl.pallas_call(lambda place, keep, *refs: projection_kernel(place, keep,...]
    dot_general x3 -> x0, matrix products: 39 us -> none  [the longest x1 19.1 us: shards(): lax.dot_general(masked, basis.astype(jnp.bfloat16), (((0,), (0,)), ((), (...]
    reduce_scatter x1 -> x0, waiting for transfers between devices: 37.7 us -> none  [shards(): lax.psum_scatter(lax.dot_general(masked, basis.astype(jnp.bfloat16), (((0...]
    ppermute x0 -> x20, waiting for transfers between devices: none -> 34.1 us  [swap(): return lax.ppermute(value, AXES, perm)]
    ppermute x0 -> x20, starting transfers between devices: none -> 32.8 us  [swap(): return lax.ppermute(value, AXES, perm)]
    another operation x5 -> x1, other arithmetic: 22.9 us -> 0.08 us  [position(): jnp.stack([jnp.where(core == 0, a, b), jnp.where(core == 0, b, a), x_lo,...]
    unnamed x2 -> x44, local copies, waits for them, and re-layouts: 0.01 us -> 19.7 us
  transfers between devices with their start and end apart: 3 -> 20, of which waited for: 3 -> 14; matrix products, arithmetic and copies ran while one was open for 0% -> 1% of each run, Pallas kernels for 0% -> 23%
where the time goes in v1:
time: 136 us
  Pallas kernels  47 us (35%)
  waiting for transfers between devices  34.1 us (25%)
  starting transfers between devices  32.8 us (24%)
  local copies, waits for them, and re-layouts  19.7 us (14%)
    ppermute x20, waiting for transfers between devices, swap(): return lax.ppermute(value, AXES, perm)  34.1 us
    ppermute x20, starting transfers between devices, swap(): return lax.ppermute(value, AXES, perm)  32.8 us
    unnamed x44, local copies, waits for them, and re-layouts  19.7 us
    pallas_call x3, Pallas kernels, projection_parts(): pl.pallas_call(lambda place, keep, *refs: projection_kernel(place, keep,...  16.4 us
    pallas_call x2, Pallas kernels, sketch_parts(): pl.pallas_call(lambda *refs: sketch_kernel(first, *refs), grid_spec=pltpu...  11.1 us
    pallas_call x1, Pallas kernels, inverse_factor(): pl.pallas_call(inverse_factor_kernel, in_specs=[pl.BlockSpec(memory_space...  5.85 us
    pallas_call x1, Pallas kernels, finish(): pl.pallas_call(finish_kernel, grid=(4,), in_specs=[pl.BlockSpec((K, K), l...  4.66 us
    pallas_call x1, Pallas kernels, range_basis_of(): pl.pallas_call(basis_kernel, grid_spec=pltpu.PrefetchScalarGridSpec(num_s...  4.64 us
  transfers between devices with their start and end apart: 20, of which 14 were waited for; matrix products, arithmetic and copies ran while one was open for 1% of the time, Pallas kernels for 23%

profile of v1, /device:TPU:1, one launch (start us, length us, event | category | flops | bytes accessed | tf_op | source)
XLA Modules:
  0.0 135.6 jit_solution(10632634085782282941)
XLA Ops:
  0.8 6.4 %copy-done = bf16[1536,6144]{1,0:T(8,128)(2,1)S(1)} copy-done((bf16[1536,6144]{1,0:T(8,128)(2,1)S(1)}, bf16[1536,6144]{1,0:T(8,128)(2,1)}, u32[]{:S(2)}) %copy-start) | copy-done | bytes 18874392
  9.2 5.5 %sketch.2 = (f32[384,128]{1,0:T(8,128)S(1)}, f32[384,128]{1,0:T(8,128)S(1)}) custom-call(s32[4]{0:T(128)S(1)} %pad_add_fusion.refs_0_.place, s32[12,48]{1,0:T(8,128)S(1)} %copy-done.9, bf16[1536,6144]{1,0:T(8,128)(2,1)S(1)} %copy-done, bf16[6144,128]{1,0:T(8,128)(2,1)S(1)} %copy-done.2), custom_call_target="tpu_custom_call" | custom-call | flops 1207959552 | bytes 9437184 | tf_op jit(solution)/shard_map/sketch/pallas_call | solution.py:113
  14.8 4.7 %collective-permute-start = (f32[384,128]{1,0:T(8,128)S(1)}, f32[384,128]{1,0:T(8,128)S(1)}, u32[]{:S(2)}, u32[]{:S(2)}) collective-permute-start(f32[384,128]{1,0:T(8,128)S(1)} %get-tuple-element.13), channel_id=1, source_target_pairs={{0,32},{1,97},{2,34},{3,99},{4,36},{5,101},{6,38},{7,103},{8,40},{... | collective-permute-start | bytes 589832 | tf_op jit(solution)/shard_map/ppermute | solution.py:52
  19.5 5.5 %sketch.3 = (f32[384,128]{1,0:T(8,128)S(1)}, f32[384,128]{1,0:T(8,128)S(1)}) custom-call(s32[4]{0:T(128)S(1)} %pad_add_fusion.refs_0_.place, s32[12,48]{1,0:T(8,128)S(1)} %copy-done.9, bf16[1536,6144]{1,0:T(8,128)(2,1)S(1)} %copy-done, bf16[6144,128]{1,0:T(8,128)(2,1)S(1)} %copy-done.2), custom_call_target="tpu_custom_call" | custom-call | flops 1207959552 | bytes 9437184 | tf_op jit(solution)/shard_map/sketch/pallas_call | solution.py:113
  25.0 2.8 %collective-permute-start.1 = (f32[384,128]{1,0:T(8,128)S(1)}, f32[384,128]{1,0:T(8,128)S(1)}, u32[]{:S(2)}, u32[]{:S(2)}) collective-permute-start(f32[384,128]{1,0:T(8,128)S(1)} %get-tuple-element.14), channel_id=1, source_target_pairs={{0,4},{1,13},{2,6},{3,15},{4,0},{5,9},{6,2},{7,11},{8,12},{9,5},{1... | collective-permute-start | bytes 589832 | tf_op jit(solution)/shard_map/ppermute | solution.py:52
  27.8 3.2 %collective-permute-done.1 = f32[384,128]{1,0:T(8,128)S(1)} collective-permute-done((f32[384,128]{1,0:T(8,128)S(1)}, f32[384,128]{1,0:T(8,128)S(1)}, u32[]{:S(2)}, u32[]{:S(2)}) %collective-permute-start.1) | collective-permute-done | bytes 196640 | tf_op jit(solution)/shard_map/ppermute | solution.py:52
  31.0 4.6 %collective-permute-done.2 = f32[384,128]{1,0:T(8,128)S(1)} collective-permute-done((f32[384,128]{1,0:T(8,128)S(1)}, f32[384,128]{1,0:T(8,128)S(1)}, u32[]{:S(2)}, u32[]{:S(2)}) %collective-permute-start.2) | collective-permute-done | bytes 196640 | tf_op jit(solution)/shard_map/ppermute | solution.py:52
  35.9 2.5 %collective-permute-start.5 = (f32[96,128]{1,0:T(8,128)S(1)}, f32[96,128]{1,0:T(8,128)S(1)}, u32[]{:S(2)}, u32[]{:S(2)}) collective-permute-start(f32[96,128]{1,0:T(8,128)S(1)} %get-tuple-element.23), channel_id=1, source_target_pairs={{0,108},{1,37},{2,110},{3,39},{4,104},{5,33},{6,106},{7,35},{8,100... | collective-permute-start | bytes 147464 | tf_op jit(solution)/shard_map/ppermute | solution.py:52
  40.5 2.8 %collective-permute-start.6 = (f32[96,128]{1,0:T(8,128)S(1)}, f32[96,128]{1,0:T(8,128)S(1)}, u32[]{:S(2)}, u32[]{:S(2)}) collective-permute-start(f32[96,128]{1,0:T(8,128)S(1)} %fusion.1), channel_id=1, source_target_pairs={{0,16},{1,17},{2,18},{3,19},{4,20},{5,21},{6,22},{7,23},{8,24},{9,... | collective-permute-start | bytes 147464 | tf_op jit(solution)/shard_map/ppermute | solution.py:52
  43.3 2.0 %collective-permute-done.6 = f32[96,128]{1,0:T(8,128)S(1)} collective-permute-done((f32[96,128]{1,0:T(8,128)S(1)}, f32[96,128]{1,0:T(8,128)S(1)}, u32[]{:S(2)}, u32[]{:S(2)}) %collective-permute-start.6) | collective-permute-done | bytes 49184 | tf_op jit(solution)/shard_map/ppermute | solution.py:52
  48.8 2.4 %collective-permute-done.9.refs_3_ = f32[96,128]{1,0:T(8,128)S(1)} collective-permute-done((f32[96,128]{1,0:T(8,128)S(1)}, f32[96,128]{1,0:T(8,128)S(1)}, u32[]{:S(2)}, u32[]{:S(2)}) %collective-permute-start.9) | collective-permute-done | bytes 49184 | tf_op jit(solution)/shard_map/ppermute | solution.py:52
  53.7 2.6 %collective-permute-start.11 = (f32[128,384]{1,0:T(8,128)}, f32[128,384]{1,0:T(8,128)S(1)}, u32[]{:S(2)}, u32[]{:S(2)}) collective-permute-start(f32[128,384]{1,0:T(8,128)} %turn.1.refs_0_), channel_id=1, source_target_pairs={{0,4},{1,13},{2,6},{3,15},{4,0},{5,9},{6,2},{7,11},{8,12},{9,5},{1... | collective-permute-start | bytes 589832 | tf_op jit(solution)/shard_map/ppermute | solution.py:52
  56.3 2.2 %collective-permute-start.12 = (f32[128,384]{1,0:T(8,128)}, f32[128,384]{1,0:T(8,128)S(1)}, u32[]{:S(2)}, u32[]{:S(2)}) collective-permute-start(f32[128,384]{1,0:T(8,128)} %turn.1.refs_0_), channel_id=1, source_target_pairs={{0,36},{1,109},{2,38},{3,111},{4,32},{5,105},{6,34},{7,107},{8,44}... | collective-permute-start | bytes 589832 | tf_op jit(solution)/shard_map/ppermute | solution.py:52
  60.2 4.2 %collective-permute-done.12.refs_3_ = f32[128,384]{1,0:T(8,128)S(1)} collective-permute-done((f32[128,384]{1,0:T(8,128)}, f32[128,384]{1,0:T(8,128)S(1)}, u32[]{:S(2)}, u32[]{:S(2)}) %collective-permute-start.12) | collective-permute-done | bytes 196640 | tf_op jit(solution)/shard_map/ppermute | solution.py:52
  64.4 6.4 %copy-done.1 = bf16[1536,6144]{1,0:T(8,128)(2,1)S(1)} copy-done((bf16[1536,6144]{1,0:T(8,128)(2,1)S(1)}, bf16[1536,6144]{1,0:T(8,128)(2,1)}, u32[]{:S(2)}) %copy-start.1) | copy-done | bytes 18874392
  72.3 4.3 %project.5 = (f32[128,768]{1,0:T(8,128)S(1)}, f32[128,768]{1,0:T(8,128)S(1)}) custom-call(s32[4]{0:T(128)S(1)} %copy-done.12, s32[12,48]{1,0:T(8,128)S(1)} %copy-done.10, f32[128,384]{1,0:T(8,128)S(1)} %copy-done.3, f32[128,384]{1,0:T(8,128)S(1)} %collective-permute-done.10.refs_1_, f32[128,384]{1,0:T(8,128)S(1)} %collective-permute-done.11.refs_2_, ...), custom_call_target="tpu_custom_call" | custom-call | flops 1207959552 | bytes 4718592 | tf_op jit(solution)/shard_map/project/pallas_call | solution.py:240
  76.7 7.8 %collective-permute-start.18 = (f32[128,768]{1,0:T(8,128)S(1)}, f32[128,768]{1,0:T(8,128)S(1)}, u32[]{:S(2)}, u32[]{:S(2)}) collective-permute-start(f32[128,768]{1,0:T(8,128)S(1)} %get-tuple-element.21), channel_id=1, source_target_pairs={{0,1},{1,0},{2,3},{3,2},{4,5},{5,4},{6,7},{7,6},{8,9},{9,8},{10,11... | collective-permute-start | bytes 1179656 | tf_op jit(solution)/shard_map/ppermute | solution.py:52
  84.4 4.3 %project.4 = (f32[128,768]{1,0:T(8,128)S(1)}, f32[128,768]{1,0:T(8,128)S(1)}) custom-call(s32[4]{0:T(128)S(1)} %copy-done.12, s32[12,48]{1,0:T(8,128)S(1)} %copy-done.10, f32[128,384]{1,0:T(8,128)S(1)} %copy-done.3, f32[128,384]{1,0:T(8,128)S(1)} %collective-permute-done.10.refs_1_, f32[128,384]{1,0:T(8,128)S(1)} %collective-permute-done.11.refs_2_, ...), custom_call_target="tpu_custom_call" | custom-call | flops 1207959552 | bytes 4718592 | tf_op jit(solution)/shard_map/project/pallas_call | solution.py:240
  88.9 7.8 %project.3 = (f32[128,1536]{1,0:T(8,128)S(1)}, f32[128,1536]{1,0:T(8,128)S(1)}) custom-call(s32[4]{0:T(128)S(1)} %copy-done.12, s32[12,48]{1,0:T(8,128)S(1)} %copy-done.10, f32[128,384]{1,0:T(8,128)S(1)} %copy-done.4, f32[128,384]{1,0:T(8,128)S(1)} %collective-permute-done.10.refs_1_, f32[128,384]{1,0:T(8,128)S(1)} %collective-permute-done.11.refs_2_, ...), custom_call_target="tpu_custom_call" | custom-call | flops 2415919104 | bytes 9437184 | tf_op jit(solution)/shard_map/project/pallas_call | solution.py:240
  99.8 2.7 %gram.1 = f32[128,128]{1,0:T(8,128)} custom-call(s32[4]{0:T(128)} %copy-done.11, f32[128,384]{1,0:T(8,128)} %turn.1.refs_0_, f32[128,384]{1,0:T(8,128)} %copy-done.5, f32[128,384]{1,0:T(8,128)} %copy-done.6, f32[128,384]{1,0:T(8,128)} %copy-done.7), custom_call_target="tpu_custom_call" | custom-call | flops 301989888 | bytes 786432 | tf_op jit(solution)/shard_map/gram/pallas_call | solution.py:160
  106.5 12.2 %collective-permute-done.14.theirs = f32[128,128]{1,0:T(8,128)S(1)} collective-permute-done((f32[128,128]{1,0:T(8,128)S(1)}, f32[128,128]{1,0:T(8,128)S(1)}, u32[]{:S(2)}, u32[]{:S(2)}) %collective-permute-start.14) | collective-permute-done | bytes 65568 | tf_op jit(solution)/shard_map/ppermute | solution.py:52
  119.3 5.9 %inverse_factor.1.inverse = f32[128,128]{1,0:T(8,128)} custom-call(f32[128,128]{1,0:T(8,128)} %copy-done.17, f32[128,128]{1,0:T(8,128)} %copy-done.21), custom_call_target="tpu_custom_call" | custom-call | flops 1000000000 | bytes 20000000 | tf_op jit(solution)/shard_map/inverse_factor/pallas_call | solution.py:200
  125.2 4.6 %basis.1 = f32[1536,128]{1,0:T(8,128)} custom-call(s32[4]{0:T(128)} %copy-done.11, f32[128,128]{1,0:T(8,128)} %inverse_factor.1.inverse, f32[128,384]{1,0:T(8,128)} %turn.1.refs_0_, f32[128,384]{1,0:T(8,128)} %copy-done.5, f32[128,384]{1,0:T(8,128)} %copy-done.6, f32[128,384]{1,0:T(8,128)} %copy-done.7), custom_call_target="tpu_custom_call" | custom-call | flops 301989888 | bytes 1572864 | tf_op jit(solution)/shard_map/basis/pallas_call | solution.py:272
  130.9 4.7 %finish.1 = f32[1536,128]{1,0:T(8,128)} custom-call(f32[128,128]{1,0:T(8,128)} %inverse_factor.1.inverse, f32[128,1536]{1,0:T(8,128)} %copy-done.8, f32[128,1536]{1,0:T(8,128)} %copy-done.13, f32[128,768]{1,0:T(8,128)} %copy-done.15, f32[128,768]{1,0:T(8,128)} %copy-done.14), custom_call_target="tpu_custom_call" | custom-call | flops 301989888 | bytes 3145728 | tf_op jit(solution)/shard_map/finish/pallas_call | solution.py:299
  (78 shorter events, 22.6 us)
Async XLA Ops:
  9.2 55.1 %copy-start.10 = (s32[12,48]{1,0:T(8,128)S(1)}, s32[12,48]{1,0:T(8,128)}, u32[]{:S(2)}) copy-start(s32[12,48]{1,0:T(8,128)} %keep.5) | copy-start | bytes 6916
  14.8 13.0 %collective-permute-start = (f32[384,128]{1,0:T(8,128)S(1)}, f32[384,128]{1,0:T(8,128)S(1)}, u32[]{:S(2)}, u32[]{:S(2)}) collective-permute-start(f32[384,128]{1,0:T(8,128)S(1)} %get-tuple-element.13), channel_id=1, source_target_pairs={{0,32},{1,97},{2,34},{3,99},{4,36},{5,101},{6,38},{7,103},{8,40},{... | collective-permute-start | bytes 589832 | tf_op jit(solution)/shard_map/ppermute | solution.py:52
  25.0 6.0 %collective-permute-start.1 = (f32[384,128]{1,0:T(8,128)S(1)}, f32[384,128]{1,0:T(8,128)S(1)}, u32[]{:S(2)}, u32[]{:S(2)}) collective-permute-start(f32[384,128]{1,0:T(8,128)S(1)} %get-tuple-element.14), channel_id=1, source_target_pairs={{0,4},{1,13},{2,6},{3,15},{4,0},{5,9},{6,2},{7,11},{8,12},{9,5},{1... | collective-permute-start | bytes 589832 | tf_op jit(solution)/shard_map/ppermute | solution.py:52
  27.8 7.8 %collective-permute-start.2 = (f32[384,128]{1,0:T(8,128)S(1)}, f32[384,128]{1,0:T(8,128)S(1)}, u32[]{:S(2)}, u32[]{:S(2)}) collective-permute-start(f32[384,128]{1,0:T(8,128)S(1)} %get-tuple-element.15), channel_id=1, source_target_pairs={{0,36},{1,109},{2,38},{3,111},{4,32},{5,105},{6,34},{7,107},{8,44}... | collective-permute-start | bytes 589832 | tf_op jit(solution)/shard_map/ppermute | solution.py:52
  35.7 3.0 %collective-permute-start.3 = (f32[96,128]{1,0:T(8,128)S(1)}, f32[96,128]{1,0:T(8,128)S(1)}, u32[]{:S(2)}, u32[]{:S(2)}) collective-permute-start(f32[96,128]{1,0:T(8,128)S(1)} %get-tuple-element.22), channel_id=1, source_target_pairs={{0,96},{1,33},{2,98},{3,35},{4,100},{5,37},{6,102},{7,39},{8,104},... | collective-permute-start | bytes 147464 | tf_op jit(solution)/shard_map/ppermute | solution.py:52
  35.8 3.0 %collective-permute-start.4 = (f32[96,128]{1,0:T(8,128)S(1)}, f32[96,128]{1,0:T(8,128)S(1)}, u32[]{:S(2)}, u32[]{:S(2)}) collective-permute-start(f32[96,128]{1,0:T(8,128)S(1)} %get-tuple-element.24), channel_id=1, source_target_pairs={{0,12},{1,5},{2,14},{3,7},{4,8},{5,1},{6,10},{7,3},{8,4},{9,13},{1... | collective-permute-start | bytes 147464 | tf_op jit(solution)/shard_map/ppermute | solution.py:52
  35.9 4.5 %collective-permute-start.5 = (f32[96,128]{1,0:T(8,128)S(1)}, f32[96,128]{1,0:T(8,128)S(1)}, u32[]{:S(2)}, u32[]{:S(2)}) collective-permute-start(f32[96,128]{1,0:T(8,128)S(1)} %get-tuple-element.23), channel_id=1, source_target_pairs={{0,108},{1,37},{2,110},{3,39},{4,104},{5,33},{6,106},{7,35},{8,100... | collective-permute-start | bytes 147464 | tf_op jit(solution)/shard_map/ppermute | solution.py:52
  40.5 4.8 %collective-permute-start.6 = (f32[96,128]{1,0:T(8,128)S(1)}, f32[96,128]{1,0:T(8,128)S(1)}, u32[]{:S(2)}, u32[]{:S(2)}) collective-permute-start(f32[96,128]{1,0:T(8,128)S(1)} %fusion.1), channel_id=1, source_target_pairs={{0,16},{1,17},{2,18},{3,19},{4,20},{5,21},{6,22},{7,23},{8,24},{9,... | collective-permute-start | bytes 147464 | tf_op jit(solution)/shard_map/ppermute | solution.py:52
  45.3 3.0 %collective-permute-start.7 = (f32[96,128]{1,0:T(8,128)S(1)}, f32[96,128]{1,0:T(8,128)S(1)}, u32[]{:S(2)}, u32[]{:S(2)}) collective-permute-start(f32[96,128]{1,0:T(8,128)S(1)} %add.62.refs_0_), channel_id=1, source_target_pairs={{0,96},{1,33},{2,98},{3,35},{4,100},{5,37},{6,102},{7,39},{8,104},... | collective-permute-start | bytes 147464 | tf_op jit(solution)/shard_map/ppermute | solution.py:52
  45.8 3.0 %collective-permute-start.8 = (f32[96,128]{1,0:T(8,128)S(1)}, f32[96,128]{1,0:T(8,128)S(1)}, u32[]{:S(2)}, u32[]{:S(2)}) collective-permute-start(f32[96,128]{1,0:T(8,128)S(1)} %add.62.refs_0_), channel_id=1, source_target_pairs={{0,12},{1,5},{2,14},{3,7},{4,8},{5,1},{6,10},{7,3},{8,4},{9,13},{1... | collective-permute-start | bytes 147464 | tf_op jit(solution)/shard_map/ppermute | solution.py:52
  47.3 3.9 %collective-permute-start.9 = (f32[96,128]{1,0:T(8,128)S(1)}, f32[96,128]{1,0:T(8,128)S(1)}, u32[]{:S(2)}, u32[]{:S(2)}) collective-permute-start(f32[96,128]{1,0:T(8,128)S(1)} %add.62.refs_0_), channel_id=1, source_target_pairs={{0,108},{1,37},{2,110},{3,39},{4,104},{5,33},{6,106},{7,35},{8,100... | collective-permute-start | bytes 147464 | tf_op jit(solution)/shard_map/ppermute | solution.py:52
  53.5 6.5 %collective-permute-start.10 = (f32[128,384]{1,0:T(8,128)}, f32[128,384]{1,0:T(8,128)S(1)}, u32[]{:S(2)}, u32[]{:S(2)}) collective-permute-start(f32[128,384]{1,0:T(8,128)} %turn.1.refs_0_), channel_id=1, source_target_pairs={{0,32},{1,97},{2,34},{3,99},{4,36},{5,101},{6,38},{7,103},{8,40},{... | collective-permute-start | bytes 589832 | tf_op jit(solution)/shard_map/ppermute | solution.py:52
  53.7 6.5 %collective-permute-start.11 = (f32[128,384]{1,0:T(8,128)}, f32[128,384]{1,0:T(8,128)S(1)}, u32[]{:S(2)}, u32[]{:S(2)}) collective-permute-start(f32[128,384]{1,0:T(8,128)} %turn.1.refs_0_), channel_id=1, source_target_pairs={{0,4},{1,13},{2,6},{3,15},{4,0},{5,9},{6,2},{7,11},{8,12},{9,5},{1... | collective-permute-start | bytes 589832 | tf_op jit(solution)/shard_map/ppermute | solution.py:52
  56.3 8.1 %collective-permute-start.12 = (f32[128,384]{1,0:T(8,128)}, f32[128,384]{1,0:T(8,128)S(1)}, u32[]{:S(2)}, u32[]{:S(2)}) collective-permute-start(f32[128,384]{1,0:T(8,128)} %turn.1.refs_0_), channel_id=1, source_target_pairs={{0,36},{1,109},{2,38},{3,111},{4,32},{5,105},{6,34},{7,107},{8,44}... | collective-permute-start | bytes 589832 | tf_op jit(solution)/shard_map/ppermute | solution.py:52
  60.0 28.9 %copy-start.5 = (f32[128,384]{1,0:T(8,128)}, f32[128,384]{1,0:T(8,128)S(1)}, u32[]{:S(2)}) copy-start(f32[128,384]{1,0:T(8,128)S(1)} %collective-permute-done.10.refs_1_) | copy-start | bytes 589828
  60.2 28.7 %copy-start.6 = (f32[128,384]{1,0:T(8,128)}, f32[128,384]{1,0:T(8,128)S(1)}, u32[]{:S(2)}) copy-start(f32[128,384]{1,0:T(8,128)S(1)} %collective-permute-done.11.refs_2_) | copy-start | bytes 589828
  72.3 16.5 %copy-start.4 = (f32[128,384]{1,0:T(8,128)S(1)}, f32[128,384]{1,0:T(8,128)}, u32[]{:S(2)}) copy-start(f32[128,384]{1,0:T(8,128)} %turn.1.refs_0_) | copy-start | bytes 589828
  76.7 21.4 %collective-permute-start.18 = (f32[128,768]{1,0:T(8,128)S(1)}, f32[128,768]{1,0:T(8,128)S(1)}, u32[]{:S(2)}, u32[]{:S(2)}) collective-permute-start(f32[128,768]{1,0:T(8,128)S(1)} %get-tuple-element.21), channel_id=1, source_target_pairs={{0,1},{1,0},{2,3},{3,2},{4,5},{5,4},{6,7},{7,6},{8,9},{9,8},{10,11... | collective-permute-start | bytes 1179656 | tf_op jit(solution)/shard_map/ppermute | solution.py:52
  88.7 10.7 %collective-permute-start.16 = (f32[128,768]{1,0:T(8,128)S(1)}, f32[128,768]{1,0:T(8,128)S(1)}, u32[]{:S(2)}, u32[]{:S(2)}) collective-permute-start(f32[128,768]{1,0:T(8,128)S(1)} %get-tuple-element.19), channel_id=1, source_target_pairs={{0,1},{1,0},{2,3},{3,2},{4,5},{5,4},{6,7},{7,6},{8,9},{9,8},{10,11... | collective-permute-start | bytes 1179656 | tf_op jit(solution)/shard_map/ppermute | solution.py:52
  97.6 32.3 %collective-permute-start.15 = (f32[128,1536]{1,0:T(8,128)S(1)}, f32[128,1536]{1,0:T(8,128)S(1)}, u32[]{:S(2)}, u32[]{:S(2)}) collective-permute-start(f32[128,1536]{1,0:T(8,128)S(1)} %get-tuple-element.17), channel_id=1, source_target_pairs={{0,1},{1,0},{2,3},{3,2},{4,5},{5,4},{6,7},{7,6},{8,9},{9,8},{10,11... | collective-permute-start | bytes 2359304 | tf_op jit(solution)/shard_map/ppermute | solution.py:52
  98.1 31.7 %collective-permute-start.19 = (f32[128,768]{1,0:T(8,128)S(1)}, f32[128,768]{1,0:T(8,128)S(1)}, u32[]{:S(2)}, u32[]{:S(2)}) collective-permute-start(f32[128,768]{1,0:T(8,128)S(1)} %add.65), channel_id=1, source_target_pairs={{0,2},{1,3},{2,0},{3,1},{4,6},{5,7},{6,4},{7,5},{8,10},{9,11},{10,... | collective-permute-start | bytes 1179656 | tf_op jit(solution)/shard_map/ppermute | solution.py:52
  99.4 30.4 %collective-permute-start.17 = (f32[128,768]{1,0:T(8,128)S(1)}, f32[128,768]{1,0:T(8,128)S(1)}, u32[]{:S(2)}, u32[]{:S(2)}) collective-permute-start(f32[128,768]{1,0:T(8,128)S(1)} %add.64), channel_id=1, source_target_pairs={{0,2},{1,3},{2,0},{3,1},{4,6},{5,7},{6,4},{7,5},{8,10},{9,11},{10,... | collective-permute-start | bytes 1179656 | tf_op jit(solution)/shard_map/ppermute | solution.py:52
  102.5 1.7 %collective-permute-start.13 = (f32[128,128]{1,0:T(8,128)}, f32[128,128]{1,0:T(8,128)S(1)}, u32[]{:S(2)}, u32[]{:S(2)}) collective-permute-start(f32[128,128]{1,0:T(8,128)} %gram.1), channel_id=1, source_target_pairs={{0,1},{1,0},{2,3},{3,2},{4,5},{5,4},{6,7},{7,6},{8,9},{9,8},{10,11... | collective-permute-start | bytes 196616 | tf_op jit(solution)/shard_map/ppermute | solution.py:52
  105.1 13.6 %collective-permute-start.14 = (f32[128,128]{1,0:T(8,128)S(1)}, f32[128,128]{1,0:T(8,128)S(1)}, u32[]{:S(2)}, u32[]{:S(2)}) collective-permute-start(f32[128,128]{1,0:T(8,128)S(1)} %add.63.mine), channel_id=1, source_target_pairs={{0,2},{1,3},{2,0},{3,1},{4,6},{5,7},{6,4},{7,5},{8,10},{9,11},{10,... | collective-permute-start | bytes 196616 | tf_op jit(solution)/shard_map/ppermute | solution.py:52
  (18 other events, 78.3 us)

commit v2 on v0

v2 whole, which is shorter than its diff:
```python
import itertools
import math

import jax
import jax.numpy as jnp
from jax import lax
from jax.experimental import pallas as pl
from jax.experimental.pallas import tpu as pltpu
from jax.sharding import PartitionSpec as P

D = 6144
K = 128
BLOCK = 128
ROWS = 1536
WIDTH = 6144
QUARTER = ROWS // 4
SUB = QUARTER // 4
PANEL = 1536
PANELS = WIDTH // PANEL
TILE = 384
TILES = WIDTH // 2 // TILE
MIB = 2**20
AXES = ("shard", "rep")
HIGHEST = lax.Precision.HIGHEST
SCALARS = pl.BlockSpec(memory_space=pltpu.SMEM)
WHOLE = pl.BlockSpec(memory_space=pltpu.VMEM)
ANYWHERE = pl.BlockSpec(memory_space=pl.ANY)
SMALL = pl.CostEstimate(flops=10**6, bytes_accessed=10**5, transcendentals=0)

FOLD_A, FOLD_B = (1, 0, 3, 2), (3, 2, 1, 0)
LABEL_A, LABEL_B = (0, 1, 1, 0), (0, 0, 1, 1)


def device(z, x_hi, y, x_lo, core):
    return ((z * 2 + x_hi) * 4 + y) * 4 + x_lo * 2 + core


PLACES = list(itertools.product(range(4), range(2), range(4), range(2), range(2)))


def pairs(partner):
    return [(device(*place), device(*partner(*place))) for place in PLACES]


def square(first, bits):
    def partner(z, x_hi, y, x_lo, core):
        fold = FOLD_A if (core == 0) == first else FOLD_B
        return (fold[z] if bits & 1 else z, x_hi, fold[y] if bits & 2 else y, x_lo, core)

    return pairs(partner)


ACROSS = pairs(lambda z, x_hi, y, x_lo, core: (z, 1 - x_hi, y, x_lo, core))
CORES = pairs(lambda z, x_hi, y, x_lo, core: (z, x_hi, y, x_lo, 1 - core))
CHIPS = pairs(lambda z, x_hi, y, x_lo, core: (z, x_hi, y, 1 - x_lo, core))


def swap(value, perm):
    return lax.ppermute(value, AXES, perm)


def label(table, place):
    return sum(jnp.where(place == i, v, 0) for i, v in enumerate(table) if v)


def position():
    shard, rep = lax.axis_index("shard"), lax.axis_index("rep")
    y, z = lax.rem(shard, 4), shard // 8
    core, x_lo = lax.rem(rep, 2), rep // 2
    a = 2 * label(LABEL_A, y) + label(LABEL_A, z)
    b = 2 * label(LABEL_B, y) + label(LABEL_B, z)
    return jnp.stack([jnp.where(core == 0, a, b), jnp.where(core == 0, b, a), x_lo, core]).astype(jnp.int32)


def masked(tile, keep, row_block, col_block):
    rows, cols = tile.shape
    return jnp.concatenate(
        [
            jnp.concatenate(
                [
                    tile[r * BLOCK : (r + 1) * BLOCK, c * BLOCK : (c + 1) * BLOCK]
                    * keep[row_block + r, col_block + c].astype(jnp.float32).astype(tile.dtype)
                    for c in range(cols // BLOCK)
                ],
                axis=1,
            )
            for r in range(rows // BLOCK)
        ],
        axis=0,
    )


def sketch_kernel(place, keep, weights, test, *refs):
    outs, tiles, right, total, tile_sems, test_sems = refs[:4], *refs[4:]

    def test_copy(p):
        at = pl.ds(p * PANEL, PANEL)
        return pltpu.make_async_copy(test.at[at, :], right.at[at, :], test_sems.at[p])

    def tile_copy(p, k):
        rows = pl.ds(pl.multiple_of((place[0] ^ k) * QUARTER, QUARTER), QUARTER)
        return pltpu.make_async_copy(weights.at[rows, pl.ds(p * PANEL, PANEL)], tiles.at[p, k], tile_sems.at[p, k])

    for p in range(PANELS):
        test_copy(p).start()
        for k in range(4):
            tile_copy(p, k).start()
    for p in range(PANELS):
        test_copy(p).wait()
        for k in range(4):
            tile_copy(p, k).wait()
            tile = masked(tiles[p, k], keep, (place[0] ^ k) * (QUARTER // BLOCK), p * (PANEL // BLOCK))
            part = jnp.dot(tile, right[p * PANEL : (p + 1) * PANEL, :], preferred_element_type=jnp.float32)
            total[k] = part if p == 0 else total[k] + part
    for k in range(4):
        for m in range(4):
            start = pl.multiple_of((place[1] ^ m) * SUB, 8)
            outs[k][m * SUB : (m + 1) * SUB, :] = total[k, pl.ds(start, SUB), :]


def sketch_parts(place, keep_mask, weights, test_matrix):
    return pl.pallas_call(
        sketch_kernel,
        in_specs=[SCALARS, SCALARS, ANYWHERE, ANYWHERE],
        out_specs=[WHOLE] * 4,
        scratch_shapes=[
            pltpu.VMEM((PANELS, 4, QUARTER, PANEL), jnp.bfloat16),
            pltpu.VMEM((WIDTH, K), jnp.bfloat16),
            pltpu.VMEM((4, QUARTER, K), jnp.float32),
            pltpu.SemaphoreType.DMA((PANELS, 4)),
            pltpu.SemaphoreType.DMA((PANELS,)),
        ],
        out_shape=[jax.ShapeDtypeStruct((QUARTER, K), jnp.float32)] * 4,
        compiler_params=pltpu.CompilerParams(vmem_limit_bytes=48 * MIB),
        cost_estimate=SMALL,
        name="sketch",
    )(place, keep_mask, weights, test_matrix)


def turn_kernel(place, *refs):
    parts, out, rows = refs[:4], refs[4], refs[5]
    for m in range(4):
        rows[pl.ds(pl.multiple_of((place[1] ^ m) * SUB, 8), SUB), :] = parts[m][...]
    out[...] = rows[...].T


def turn(place, parts):
    return pl.pallas_call(
        turn_kernel,
        in_specs=[SCALARS] + [WHOLE] * 4,
        out_specs=WHOLE,
        out_shape=jax.ShapeDtypeStruct((K, QUARTER), jnp.float32),
        scratch_shapes=[pltpu.VMEM((QUARTER, K), jnp.float32)],
        compiler_params=pltpu.CompilerParams(vmem_limit_bytes=4 * MIB),
        cost_estimate=SMALL,
        name="turn",
    )(place, *parts)


def gram_kernel(*refs):
    first, second, more, out = refs[0], refs[1], refs[2:-1], refs[-1]

    def square_of(piece):
        return lax.dot_general(
            piece[...], piece[...], (((1,), (1,)), ((), ())), precision=HIGHEST, preferred_element_type=jnp.float32
        )

    total = square_of(first) + square_of(second)
    for before in more:
        total = total + before[...]
    out[...] = total


def gram_of(*parts):
    return pl.pallas_call(
        gram_kernel,
        in_specs=[WHOLE] * len(parts),
        out_specs=WHOLE,
        out_shape=jax.ShapeDtypeStruct((K, K), jnp.float32),
        compiler_params=pltpu.CompilerParams(vmem_limit_bytes=8 * MIB),
        cost_estimate=SMALL,
        name="gram",
    )(*parts)


def inverse_factor_kernel(mine, theirs, out, step=4):
    gram = mine[...] + theirs[...]
    lanes = lax.broadcasted_iota(jnp.int32, (K, K), 1)
    rows = lax.broadcasted_iota(jnp.int32, (K, K), 0)
    unit = jnp.where(lanes == rows, 1.0, 0.0).astype(jnp.float32)
    for top in range(0, K, step):
        left = K - top
        column = [jnp.broadcast_to(gram[:, top + i : top + i + 1], (left, K)) for i in range(step)]
        row = [gram[i : i + 1, :] for i in range(step)]
        side = [unit[i : i + 1, :] for i in range(step)]
        for i in range(step):
            pivot = column[i][i : i + 1, :]
            inverse = 1.0 / pivot
            for m in range(i + 1, step):
                factor = column[i][m : m + 1, :] * inverse
                column[m] = column[m] - column[i] * factor
                row[m] = row[m] - row[i] * factor
                side[m] = side[m] - side[i] * factor
            out[top + i : top + i + 1, :] = side[i] * lax.rsqrt(pivot)
            row[i] = row[i] * inverse
            side[i] = side[i] * inverse
        if left > step:
            gram, unit = gram[step:], unit[step:]
            for i in range(step):
                gram = gram - column[i][step:] * row[i]
                unit = unit - column[i][step:] * side[i]


def inverse_factor(mine, theirs):
    return pl.pallas_call(
        inverse_factor_kernel,
        in_specs=[WHOLE] * 2,
        out_specs=WHOLE,
        out_shape=jax.ShapeDtypeStruct((K, K), jnp.float32),
        compiler_params=pltpu.CompilerParams(vmem_limit_bytes=8 * MIB),
        cost_estimate=SMALL,
        name="inverse_factor",
    )(mine, theirs)


def tile_columns(place, near, t):
    core = 1 - place[3] if t < TILES // 2 else place[3]
    chip = place[2] if near else 1 - place[2]
    return (chip * 2 + core) * (WIDTH // 4 // BLOCK) + t % (TILES // 2) * (TILE // BLOCK)


def tile_copy(place, near, t, weights, tiles, sems):
    columns = pl.ds(pl.multiple_of(tile_columns(place, near, t) * BLOCK, BLOCK), TILE)
    return pltpu.make_async_copy(weights.at[:, columns], tiles.at[t], sems.at[t])


def stage_kernel(place, weights, ready, tiles, sems):
    copies = [tile_copy(place, False, t, weights, tiles, sems) for t in range(TILES)]
    for copy in copies:
        copy.start()
    for copy in copies:
        copy.wait()


def stage(place, weights, ready):
    return pl.pallas_call(
        stage_kernel,
        in_specs=[SCALARS, ANYWHERE, ANYWHERE],
        out_specs=WHOLE,
        out_shape=jax.ShapeDtypeStruct((TILES, ROWS, TILE), jnp.bfloat16),
        scratch_shapes=[pltpu.SemaphoreType.DMA((TILES,))],
        compiler_params=pltpu.CompilerParams(vmem_limit_bytes=44 * MIB),
        cost_estimate=SMALL,
        name="stage",
    )(place, weights, ready)


def project(place, keep, near, parts, write, sketch, tile):
    for k in range(4):
        at = pl.ds(pl.multiple_of((place[0] ^ k) * QUARTER, BLOCK), QUARTER)
        high = parts[k][...].astype(jnp.bfloat16)
        sketch[0:K, at] = high
        sketch[K : 2 * K, at] = (parts[k][...] - high.astype(jnp.float32)).astype(jnp.bfloat16)
    for t in range(TILES):
        both = jnp.dot(
            sketch[...], masked(tile(t), keep, 0, tile_columns(place, near, t)), preferred_element_type=jnp.float32
        )
        write(t, both[:K] + both[K:])


def far_kernel(place, keep, *refs):
    parts, tiles, outs, sketch = refs[:4], refs[4], refs[5:-1], refs[-1]

    def write(t, value):
        outs[t // (TILES // 2)][:, t % (TILES // 2) * TILE : (t % (TILES // 2) + 1) * TILE] = value

    project(place, keep, False, parts, write, sketch, lambda t: tiles[t])


def near_kernel(place, keep, *refs):
    parts, weights, outs, tiles, sketch, sems = refs[:4], refs[4], refs[5:-3], *refs[-3:]
    copies = [tile_copy(place, True, t, weights, tiles, sems) for t in range(TILES)]
    for copy in copies:
        copy.start()

    def tile(t):
        copies[t].wait()
        return tiles[t]

    def write(t, value):
        outs[t][...] = value

    project(place, keep, True, parts, write, sketch, tile)


def far_terms(place, keep_mask, parts, tiles):
    return pl.pallas_call(
        far_kernel,
        in_specs=[SCALARS, SCALARS] + [WHOLE] * 5,
        out_specs=[WHOLE] * 2,
        scratch_shapes=[pltpu.VMEM((2 * K, ROWS), jnp.bfloat16)],
        out_shape=[jax.ShapeDtypeStruct((K, WIDTH // 4), jnp.float32)] * 2,
        compiler_params=pltpu.CompilerParams(vmem_limit_bytes=32 * MIB),
        cost_estimate=SMALL,
        name="far",
    )(place, keep_mask, *parts, tiles)


def near_terms(place, keep_mask, parts, weights):
    return pl.pallas_call(
        near_kernel,
        in_specs=[SCALARS, SCALARS] + [WHOLE] * 4 + [ANYWHERE],
        out_specs=[WHOLE] * TILES,
        scratch_shapes=[
            pltpu.VMEM((TILES, ROWS, TILE), jnp.bfloat16),
            pltpu.VMEM((2 * K, ROWS), jnp.bfloat16),
            pltpu.SemaphoreType.DMA((TILES,)),
        ],
        out_shape=[jax.ShapeDtypeStruct((K, TILE), jnp.float32)] * TILES,
        compiler_params=pltpu.CompilerParams(vmem_limit_bytes=48 * MIB),
        cost_estimate=SMALL,
        name="near",
    )(place, keep_mask, *parts, weights)


def dot_split(left, right):
    def terms(x):
        high = x.astype(jnp.bfloat16)
        return high, (x - high.astype(jnp.float32)).astype(jnp.bfloat16)

    (a, b), (c, d) = terms(left), terms(right)
    return jnp.dot(
        jnp.concatenate([a, a, b], axis=1), jnp.concatenate([c, d, c], axis=0), preferred_element_type=jnp.float32
    )


def write_turned(inverse, columns, scale, out, held, sems):
    copies = []
    for t in range(4):
        value, place = columns(t)
        held[t] = (dot_split(inverse, value) * scale).T
        rows = pl.ds(pl.multiple_of(place * QUARTER, QUARTER), QUARTER)
        copies.append(pltpu.make_async_copy(held.at[t], out.at[rows, :], sems.at[t]))
        copies[-1].start()
    for copy in copies:
        copy.wait()


TURNED = dict(
    out_specs=pl.BlockSpec(memory_space=pl.ANY),
    out_shape=jax.ShapeDtypeStruct((ROWS, K), jnp.float32),
    scratch_shapes=[pltpu.VMEM((4, QUARTER, K), jnp.float32), pltpu.SemaphoreType.DMA((4,))],
    compiler_params=pltpu.CompilerParams(vmem_limit_bytes=16 * MIB),
    cost_estimate=SMALL,
)


def basis_kernel(place, inverse, *refs):
    parts, out, held, sems = refs[:4], *refs[4:]
    write_turned(inverse[...], lambda k: (parts[k][...], place[0] ^ k), math.sqrt(D), out, held, sems)


def range_basis_of(place, inverse, parts):
    return pl.pallas_call(basis_kernel, in_specs=[SCALARS] + [WHOLE] * 5, name="basis", **TURNED)(place, inverse, *parts)


def finish_kernel(inverse, far, *refs):
    terms, out, held, sems = refs[:8], *refs[8:]

    def columns(t):
        return terms[t][...] + terms[t + 4][...] + far[:, t * TILE : (t + 1) * TILE], t

    write_turned(inverse[...], columns, 1.0, out, held, sems)


def finish(inverse, far, here, core):
    return pl.pallas_call(finish_kernel, in_specs=[WHOLE] * 10, name="finish", **TURNED)(inverse, far, *here, *core)


def shards(weights, keep_mask, test_matrix):
    place = position()

    own = sketch_parts(place, keep_mask, weights, test_matrix)
    got = [swap(own[k], square(True, k)) for k in (3, 2, 1)]
    quarter = own[0] + got[2] + got[1] + got[0]
    piece = [quarter[m * SUB : (m + 1) * SUB] for m in range(4)]
    got = [swap(piece[m], square(False, m)) for m in (3, 2, 1)]
    sub = piece[0] + got[2] + got[1] + got[0]
    sub = sub + swap(sub, ACROSS)

    got = {m: swap(sub, square(False, m)) for m in (3, 2, 1)}
    mine = turn(place, (sub, got[1], got[2], got[3]))
    got = {k: swap(mine, square(True, k)) for k in (3, 2, 1)}
    parts = (mine, got[1], got[2], got[3])
    tiles = stage(place, weights, mine)

    gram = gram_of(got[2], got[3], gram_of(mine, got[1]))
    gram, parts = lax.optimization_barrier((gram, parts))
    send, stay = far_terms(place, keep_mask, parts, tiles)
    gram = gram + swap(gram, CORES)
    stay, gram = lax.optimization_barrier((stay + swap(send, CORES), gram))
    far_gram = swap(gram, CHIPS)
    far = swap(stay, CHIPS)
    terms = near_terms(place, keep_mask, parts, weights)
    core = [swap(term, CORES) for term in terms[:4]]
    inverse = inverse_factor(gram, far_gram)
    return range_basis_of(place, inverse, parts), finish(inverse, far, terms[4:], core)


def solution(mesh):
    placed = (P("rep", "shard"), P("rep", "shard"), P("shard", None))
    return jax.shard_map(
        shards,
        mesh=mesh,
        in_specs=placed,
        out_specs=(P("rep", None), P(("shard", "rep"), None)),
        check_vma=False,
    )
```

time: 518 us -> 103 us (0.20)
  waiting for transfers between devices: 429 us -> 28.2 us
  matrix products: 41.8 us -> 0 us
  Pallas kernels: 0 us -> 38.2 us
  starting transfers between devices: 0.3 us -> 33.2 us
  other arithmetic: 24.5 us -> 0.23 us
  between operations: 13.8 us -> 1.07 us
  local copies, waits for them, and re-layouts: 7.9 us -> 2.12 us
    psum x2 -> x0, waiting for transfers between devices: 392 us -> none  [the longest x1 334 us: shards(): sketch = lax.psum(partial_sketch, 'shard')]
    dot_general x3 -> x0, matrix products: 39 us -> none  [the longest x1 19.1 us: shards(): lax.dot_general(masked, basis.astype(jnp.bfloat16), (((0,), (0,)), ((), (...]
    pallas_call x0 -> x10, Pallas kernels: none -> 38.2 us  [the longest x1 13.1 us: sketch_parts(): pl.pallas_call(sketch_kernel, in_specs=[SCALARS, SCALARS, ANYWHERE, ANYWH...]
    reduce_scatter x1 -> x0, waiting for transfers between devices: 37.7 us -> none  [shards(): lax.psum_scatter(lax.dot_general(masked, basis.astype(jnp.bfloat16), (((0...]
    ppermute x0 -> x21, starting transfers between devices: none -> 33.2 us  [swap(): return lax.ppermute(value, AXES, perm)]
    ppermute x0 -> x21, waiting for transfers between devices: none -> 28.2 us  [swap(): return lax.ppermute(value, AXES, perm)]
    another operation x5 -> x1, other arithmetic: 22.9 us -> 0.08 us  [position(): jnp.stack([jnp.where(core == 0, a, b), jnp.where(core == 0, b, a), x_lo,...]
    mul x1 -> x0, local copies, waits for them, and re-layouts: 6.96 us -> none  [shards(): quad * keep_mask[:, None, :, None].astype(weights.dtype)]
  transfers between devices with their start and end apart: 3 -> 21, of which waited for: 3 -> 13; matrix products, arithmetic and copies ran while one was open for 0% -> 0% of each run, Pallas kernels for 0% -> 18%
where the time goes in v2:
time: 103 us
  Pallas kernels  38.2 us (37%)
  starting transfers between devices  33.2 us (32%)
  waiting for transfers between devices  28.2 us (27%)
  local copies, waits for them, and re-layouts  2.12 us (2%)
  between operations  1.07 us (1%)
    ppermute x21, starting transfers between devices, swap(): return lax.ppermute(value, AXES, perm)  33.2 us
    ppermute x21, waiting for transfers between devices, swap(): return lax.ppermute(value, AXES, perm)  28.2 us
    pallas_call x1, Pallas kernels, sketch_parts(): pl.pallas_call(sketch_kernel, in_specs=[SCALARS, SCALARS, ANYWHERE, ANYWH...  13.1 us
    pallas_call x1, Pallas kernels, near_terms(): pl.pallas_call(near_kernel, in_specs=[SCALARS, SCALARS] + [WHOLE] * 4 + [...  7.03 us
    pallas_call x1, Pallas kernels, far_terms(): pl.pallas_call(far_kernel, in_specs=[SCALARS, SCALARS] + [WHOLE] * 5, out...  4.43 us
    pallas_call x1, Pallas kernels, stage(): pl.pallas_call(stage_kernel, in_specs=[SCALARS, ANYWHERE, ANYWHERE], out_...  4.41 us
    pallas_call x1, Pallas kernels, inverse_factor(): pl.pallas_call(inverse_factor_kernel, in_specs=[WHOLE] * 2, out_specs=WHO...  4.34 us
    unnamed x6, local copies, waits for them, and re-layouts  2.11 us
  transfers between devices with their start and end apart: 21, of which 13 were waited for; matrix products, arithmetic and copies ran while one was open for 0% of the time, Pallas kernels for 18%

profile of v2, /device:TPU:1, one launch (start us, length us, event | category | flops | bytes accessed | tf_op | source)
XLA Modules:
  0.0 103.0 jit_solution(5519799109388821843)
XLA Ops:
  0.8 1.4 %copy-done = bf16[6144,128]{1,0:T(8,128)(2,1)S(1)} copy-done((bf16[6144,128]{1,0:T(8,128)(2,1)S(1)}, bf16[6144,128]{1,0:T(8,128)(2,1)}, u32[]{:S(2)}) %copy-start) | copy-done | bytes 1572888
  2.9 13.1 %sketch.1 = (f32[384,128]{1,0:T(8,128)S(1)}, f32[384,128]{1,0:T(8,128)S(1)}, f32[384,128]{1,0:T(8,128)S(1)}, f32[384,128]{1,0:T(8,128)S(1)}) custom-call(s32[4]{0:T(128)S(1)} %pad_add_fusion.place, s32[12,48]{1,0:T(8,128)S(1)} %copy-done.1, bf16[1536,6144]{1,0:T(8,128)(2,1)} %refs_4_.1, bf16[6144,128]{1,0:T(8,128)(2,1)S(1)} %copy-done), custom_call_target="tpu_custom_call" | custom-call | flops 1000000 | bytes 100000 | tf_op jit(solution)/shard_map/sketch/pallas_call | solution.py:122
  16.0 4.7 %collective-permute-start = (f32[384,128]{1,0:T(8,128)S(1)}, f32[384,128]{1,0:T(8,128)S(1)}, u32[]{:S(2)}, u32[]{:S(2)}) collective-permute-start(f32[384,128]{1,0:T(8,128)S(1)} %get-tuple-element.24), channel_id=1, source_target_pairs={{0,32},{1,97},{2,34},{3,99},{4,36},{5,101},{6,38},{7,103},{8,40},{... | collective-permute-start | bytes 589832 | tf_op jit(solution)/shard_map/ppermute | solution.py:59
  20.6 2.7 %collective-permute-start.1 = (f32[384,128]{1,0:T(8,128)S(1)}, f32[384,128]{1,0:T(8,128)S(1)}, u32[]{:S(2)}, u32[]{:S(2)}) collective-permute-start(f32[384,128]{1,0:T(8,128)S(1)} %get-tuple-element.25), channel_id=1, source_target_pairs={{0,4},{1,13},{2,6},{3,15},{4,0},{5,9},{6,2},{7,11},{8,12},{9,5},{1... | collective-permute-start | bytes 589832 | tf_op jit(solution)/shard_map/ppermute | solution.py:59
  23.7 2.9 %collective-permute-done.1 = f32[384,128]{1,0:T(8,128)S(1)} collective-permute-done((f32[384,128]{1,0:T(8,128)S(1)}, f32[384,128]{1,0:T(8,128)S(1)}, u32[]{:S(2)}, u32[]{:S(2)}) %collective-permute-start.1) | collective-permute-done | bytes 196640 | tf_op jit(solution)/shard_map/ppermute | solution.py:59
  26.6 4.6 %collective-permute-done.2 = f32[384,128]{1,0:T(8,128)S(1)} collective-permute-done((f32[384,128]{1,0:T(8,128)S(1)}, f32[384,128]{1,0:T(8,128)S(1)}, u32[]{:S(2)}, u32[]{:S(2)}) %collective-permute-start.2) | collective-permute-done | bytes 196640 | tf_op jit(solution)/shard_map/ppermute | solution.py:59
  31.4 2.5 %collective-permute-start.5 = (f32[96,128]{1,0:T(8,128)S(1)}, f32[96,128]{1,0:T(8,128)S(1)}, u32[]{:S(2)}, u32[]{:S(2)}) collective-permute-start(f32[96,128]{1,0:T(8,128)S(1)} %get-tuple-element.45), channel_id=1, source_target_pairs={{0,108},{1,37},{2,110},{3,39},{4,104},{5,33},{6,106},{7,35},{8,100... | collective-permute-start | bytes 147464 | tf_op jit(solution)/shard_map/ppermute | solution.py:59
  34.4 1.6 %collective-permute-done.5 = f32[96,128]{1,0:T(8,128)S(1)} collective-permute-done((f32[96,128]{1,0:T(8,128)S(1)}, f32[96,128]{1,0:T(8,128)S(1)}, u32[]{:S(2)}, u32[]{:S(2)}) %collective-permute-start.5) | collective-permute-done | bytes 49184 | tf_op jit(solution)/shard_map/ppermute | solution.py:59
  36.0 2.8 %collective-permute-start.6 = (f32[96,128]{1,0:T(8,128)S(1)}, f32[96,128]{1,0:T(8,128)S(1)}, u32[]{:S(2)}, u32[]{:S(2)}) collective-permute-start(f32[96,128]{1,0:T(8,128)S(1)} %fusion.1), channel_id=1, source_target_pairs={{0,16},{1,17},{2,18},{3,19},{4,20},{5,21},{6,22},{7,23},{8,24},{9,... | collective-permute-start | bytes 147464 | tf_op jit(solution)/shard_map/ppermute | solution.py:59
  38.8 2.0 %collective-permute-done.6 = f32[96,128]{1,0:T(8,128)S(1)} collective-permute-done((f32[96,128]{1,0:T(8,128)S(1)}, f32[96,128]{1,0:T(8,128)S(1)}, u32[]{:S(2)}, u32[]{:S(2)}) %collective-permute-start.6) | collective-permute-done | bytes 49184 | tf_op jit(solution)/shard_map/ppermute | solution.py:59
  41.3 1.5 %collective-permute-start.8 = (f32[96,128]{1,0:T(8,128)S(1)}, f32[96,128]{1,0:T(8,128)S(1)}, u32[]{:S(2)}, u32[]{:S(2)}) collective-permute-start(f32[96,128]{1,0:T(8,128)S(1)} %add.59.refs_0_), channel_id=1, source_target_pairs={{0,12},{1,5},{2,14},{3,7},{4,8},{5,1},{6,10},{7,3},{8,4},{9,13},{1... | collective-permute-start | bytes 147464 | tf_op jit(solution)/shard_map/ppermute | solution.py:59
  44.3 2.4 %collective-permute-done.9.refs_3_ = f32[96,128]{1,0:T(8,128)S(1)} collective-permute-done((f32[96,128]{1,0:T(8,128)S(1)}, f32[96,128]{1,0:T(8,128)S(1)}, u32[]{:S(2)}, u32[]{:S(2)}) %collective-permute-start.9) | collective-permute-done | bytes 49184 | tf_op jit(solution)/shard_map/ppermute | solution.py:59
  47.7 2.5 %collective-permute-start.10 = (f32[128,384]{1,0:T(8,128)S(1)}, f32[128,384]{1,0:T(8,128)S(1)}, u32[]{:S(2)}, u32[]{:S(2)}) collective-permute-start(f32[128,384]{1,0:T(8,128)S(1)} %turn.1.refs_0_.ready), channel_id=1, source_target_pairs={{0,4},{1,13},{2,6},{3,15},{4,0},{5,9},{6,2},{7,11},{8,12},{9,5},{1... | collective-permute-start | bytes 589832 | tf_op jit(solution)/shard_map/ppermute | solution.py:59
  50.3 2.2 %collective-permute-start.11 = (f32[128,384]{1,0:T(8,128)S(1)}, f32[128,384]{1,0:T(8,128)S(1)}, u32[]{:S(2)}, u32[]{:S(2)}) collective-permute-start(f32[128,384]{1,0:T(8,128)S(1)} %turn.1.refs_0_.ready), channel_id=1, source_target_pairs={{0,36},{1,109},{2,38},{3,111},{4,32},{5,105},{6,34},{7,107},{8,44}... | collective-permute-start | bytes 589832 | tf_op jit(solution)/shard_map/ppermute | solution.py:59
  52.5 4.4 %stage.1.refs_4_ = bf16[8,1536,384]{2,1,0:T(8,128)(2,1)S(1)} custom-call(s32[4]{0:T(128)S(1)} %pad_add_fusion.place, bf16[1536,6144]{1,0:T(8,128)(2,1)} %refs_4_.1, f32[128,384]{1,0:T(8,128)S(1)} %turn.1.refs_0_.ready), custom_call_target="tpu_custom_call" | custom-call | flops 1000000 | bytes 100000 | tf_op jit(solution)/shard_map/stage/pallas_call | solution.py:246
  59.3 4.4 %far.1 = (f32[128,1536]{1,0:T(8,128)S(1)}, f32[128,1536]{1,0:T(8,128)S(1)}) custom-call(s32[4]{0:T(128)S(1)} %pad_add_fusion.place, s32[12,48]{1,0:T(8,128)S(1)} %copy-done.2, f32[128,384]{1,0:T(8,128)S(1)} %turn.1.refs_0_.ready, f32[128,384]{1,0:T(8,128)S(1)} %collective-permute-done.12.refs_1_, f32[128,384]{1,0:T(8,128)S(1)} %collective-permute-done.10.refs_0_.refs_2_, ...), custom_call_target="tpu_custom_call" | custom-call | flops 1000000 | bytes 100000 | tf_op jit(solution)/shard_map/far/pallas_call | solution.py:297
  63.7 8.0 %collective-permute-start.13 = (f32[128,1536]{1,0:T(8,128)S(1)}, f32[128,1536]{1,0:T(8,128)S(1)}, u32[]{:S(2)}, u32[]{:S(2)}) collective-permute-start(f32[128,1536]{1,0:T(8,128)S(1)} %get-tuple-element.32), channel_id=1, source_target_pairs={{0,1},{1,0},{2,3},{3,2},{4,5},{5,4},{6,7},{7,6},{8,9},{9,8},{10,11... | collective-permute-start | bytes 2359304 | tf_op jit(solution)/shard_map/ppermute | solution.py:59
  71.8 1.9 %collective-permute-done.14 = f32[128,128]{1,0:T(8,128)S(1)} collective-permute-done((f32[128,128]{1,0:T(8,128)S(1)}, f32[128,128]{1,0:T(8,128)S(1)}, u32[]{:S(2)}, u32[]{:S(2)}) %collective-permute-start.14) | collective-permute-done | bytes 65568 | tf_op jit(solution)/shard_map/ppermute | solution.py:59
  73.9 1.3 %collective-permute-start.16 = (f32[128,1536]{1,0:T(8,128)S(1)}, f32[128,1536]{1,0:T(8,128)S(1)}, u32[]{:S(2)}, u32[]{:S(2)}) collective-permute-start(f32[128,1536]{1,0:T(8,128)S(1)} %add.60), channel_id=1, source_target_pairs={{0,2},{1,3},{2,0},{3,1},{4,6},{5,7},{6,4},{7,5},{8,10},{9,11},{10,... | collective-permute-start | bytes 2359304 | tf_op jit(solution)/shard_map/ppermute | solution.py:59
  75.4 7.0 %near.1 = (f32[128,384]{1,0:T(8,128)S(1)}, f32[128,384]{1,0:T(8,128)S(1)}, f32[128,384]{1,0:T(8,128)S(1)}, f32[128,384]{1,0:T(8,128)S(1)}, f32[128,384]{1,0:T(8,...) custom-call(s32[4]{0:T(128)S(1)} %pad_add_fusion.place, s32[12,48]{1,0:T(8,128)S(1)} %copy-done.2, ...), custom_call_target="tpu_custom_call" | custom-call | flops 1000000 | bytes 100000 | tf_op jit(solution)/shard_map/near/pallas_call | solution.py:310
  84.0 10.1 %collective-permute-done.15.theirs = f32[128,128]{1,0:T(8,128)S(1)} collective-permute-done((f32[128,128]{1,0:T(8,128)S(1)}, f32[128,128]{1,0:T(8,128)S(1)}, u32[]{:S(2)}, u32[]{:S(2)}) %collective-permute-start.15) | collective-permute-done | bytes 65568 | tf_op jit(solution)/shard_map/ppermute | solution.py:59
  95.3 4.3 %inverse_factor.1.inverse = f32[128,128]{1,0:T(8,128)S(1)} custom-call(f32[128,128]{1,0:T(8,128)S(1)} %add.61.mine, f32[128,128]{1,0:T(8,128)S(1)} %collective-permute-done.15.theirs), custom_call_target="tpu_custom_call" | custom-call | flops 1000000 | bytes 100000 | tf_op jit(solution)/shard_map/inverse_factor/pallas_call | solution.py:215
  99.7 1.8 %basis.1 = f32[1536,128]{1,0:T(8,128)} custom-call(s32[4]{0:T(128)S(1)} %pad_add_fusion.place, f32[128,128]{1,0:T(8,128)S(1)} %inverse_factor.1.inverse, f32[128,384]{1,0:T(8,128)S(1)} %turn.1.refs_0_.ready, f32[128,384]{1,0:T(8,128)S(1)} %collective-permute-done.12.refs_1_, f32[128,384]{1,0:T(8,128)S(1)} %collective-permute-done.10.refs_0_.refs_2_, ...), custom_call_target="tpu_custom_call" | custom-call | flops 1000000 | bytes 100000 | tf_op jit(solution)/shard_map/basis/pallas_call | solution.py:364
  101.5 1.3 %finish.1 = f32[1536,128]{1,0:T(8,128)} custom-call(f32[128,128]{1,0:T(8,128)S(1)} %inverse_factor.1.inverse, f32[128,1536]{1,0:T(8,128)S(1)} %collective-permute-done.16.far, f32[128,384]{1,0:T(8,128)S(1)} %get-tuple-element.36.refs_0_, f32[128,384]{1,0:T(8,128)S(1)} %get-tuple-element.37.refs_1_, f32[128,384]{1,0:T(8,128)S(1)} %get-tuple-element.38.refs_2_, ...), custom_call_target="tpu_custom_call" | custom-call | flops 1000000 | bytes 100000 | tf_op jit(solution)/shard_map/finish/pallas_call | solution.py:377
  (41 shorter events, 10.2 us)
Async XLA Ops:
  0.8 1.4 %copy-start = (bf16[6144,128]{1,0:T(8,128)(2,1)S(1)}, bf16[6144,128]{1,0:T(8,128)(2,1)}, u32[]{:S(2)}) copy-start(bf16[6144,128]{1,0:T(8,128)(2,1)} %test.1) | copy-start | bytes 4718596
  2.2 0.7 copy-start.1
  16.0 7.7 %collective-permute-start = (f32[384,128]{1,0:T(8,128)S(1)}, f32[384,128]{1,0:T(8,128)S(1)}, u32[]{:S(2)}, u32[]{:S(2)}) collective-permute-start(f32[384,128]{1,0:T(8,128)S(1)} %get-tuple-element.24), channel_id=1, source_target_pairs={{0,32},{1,97},{2,34},{3,99},{4,36},{5,101},{6,38},{7,103},{8,40},{... | collective-permute-start | bytes 589832 | tf_op jit(solution)/shard_map/ppermute | solution.py:59
  20.6 5.9 %collective-permute-start.1 = (f32[384,128]{1,0:T(8,128)S(1)}, f32[384,128]{1,0:T(8,128)S(1)}, u32[]{:S(2)}, u32[]{:S(2)}) collective-permute-start(f32[384,128]{1,0:T(8,128)S(1)} %get-tuple-element.25), channel_id=1, source_target_pairs={{0,4},{1,13},{2,6},{3,15},{4,0},{5,9},{6,2},{7,11},{8,12},{9,5},{1... | collective-permute-start | bytes 589832 | tf_op jit(solution)/shard_map/ppermute | solution.py:59
  23.4 7.8 %collective-permute-start.2 = (f32[384,128]{1,0:T(8,128)S(1)}, f32[384,128]{1,0:T(8,128)S(1)}, u32[]{:S(2)}, u32[]{:S(2)}) collective-permute-start(f32[384,128]{1,0:T(8,128)S(1)} %get-tuple-element.26), channel_id=1, source_target_pairs={{0,36},{1,109},{2,38},{3,111},{4,32},{5,105},{6,34},{7,107},{8,44}... | collective-permute-start | bytes 589832 | tf_op jit(solution)/shard_map/ppermute | solution.py:59
  31.3 3.0 %collective-permute-start.3 = (f32[96,128]{1,0:T(8,128)S(1)}, f32[96,128]{1,0:T(8,128)S(1)}, u32[]{:S(2)}, u32[]{:S(2)}) collective-permute-start(f32[96,128]{1,0:T(8,128)S(1)} %get-tuple-element.44), channel_id=1, source_target_pairs={{0,96},{1,33},{2,98},{3,35},{4,100},{5,37},{6,102},{7,39},{8,104},... | collective-permute-start | bytes 147464 | tf_op jit(solution)/shard_map/ppermute | solution.py:59
  31.4 3.0 %collective-permute-start.4 = (f32[96,128]{1,0:T(8,128)S(1)}, f32[96,128]{1,0:T(8,128)S(1)}, u32[]{:S(2)}, u32[]{:S(2)}) collective-permute-start(f32[96,128]{1,0:T(8,128)S(1)} %get-tuple-element.46), channel_id=1, source_target_pairs={{0,12},{1,5},{2,14},{3,7},{4,8},{5,1},{6,10},{7,3},{8,4},{9,13},{1... | collective-permute-start | bytes 147464 | tf_op jit(solution)/shard_map/ppermute | solution.py:59
  31.4 4.5 %collective-permute-start.5 = (f32[96,128]{1,0:T(8,128)S(1)}, f32[96,128]{1,0:T(8,128)S(1)}, u32[]{:S(2)}, u32[]{:S(2)}) collective-permute-start(f32[96,128]{1,0:T(8,128)S(1)} %get-tuple-element.45), channel_id=1, source_target_pairs={{0,108},{1,37},{2,110},{3,39},{4,104},{5,33},{6,106},{7,35},{8,100... | collective-permute-start | bytes 147464 | tf_op jit(solution)/shard_map/ppermute | solution.py:59
  36.0 4.8 %collective-permute-start.6 = (f32[96,128]{1,0:T(8,128)S(1)}, f32[96,128]{1,0:T(8,128)S(1)}, u32[]{:S(2)}, u32[]{:S(2)}) collective-permute-start(f32[96,128]{1,0:T(8,128)S(1)} %fusion.1), channel_id=1, source_target_pairs={{0,16},{1,17},{2,18},{3,19},{4,20},{5,21},{6,22},{7,23},{8,24},{9,... | collective-permute-start | bytes 147464 | tf_op jit(solution)/shard_map/ppermute | solution.py:59
  40.8 3.0 %collective-permute-start.7 = (f32[96,128]{1,0:T(8,128)S(1)}, f32[96,128]{1,0:T(8,128)S(1)}, u32[]{:S(2)}, u32[]{:S(2)}) collective-permute-start(f32[96,128]{1,0:T(8,128)S(1)} %add.59.refs_0_), channel_id=1, source_target_pairs={{0,96},{1,33},{2,98},{3,35},{4,100},{5,37},{6,102},{7,39},{8,104},... | collective-permute-start | bytes 147464 | tf_op jit(solution)/shard_map/ppermute | solution.py:59
  41.3 3.0 %collective-permute-start.8 = (f32[96,128]{1,0:T(8,128)S(1)}, f32[96,128]{1,0:T(8,128)S(1)}, u32[]{:S(2)}, u32[]{:S(2)}) collective-permute-start(f32[96,128]{1,0:T(8,128)S(1)} %add.59.refs_0_), channel_id=1, source_target_pairs={{0,12},{1,5},{2,14},{3,7},{4,8},{5,1},{6,10},{7,3},{8,4},{9,13},{1... | collective-permute-start | bytes 147464 | tf_op jit(solution)/shard_map/ppermute | solution.py:59
  42.8 3.9 %collective-permute-start.9 = (f32[96,128]{1,0:T(8,128)S(1)}, f32[96,128]{1,0:T(8,128)S(1)}, u32[]{:S(2)}, u32[]{:S(2)}) collective-permute-start(f32[96,128]{1,0:T(8,128)S(1)} %add.59.refs_0_), channel_id=1, source_target_pairs={{0,108},{1,37},{2,110},{3,39},{4,104},{5,33},{6,106},{7,35},{8,100... | collective-permute-start | bytes 147464 | tf_op jit(solution)/shard_map/ppermute | solution.py:59
  47.4 11.9 %copy-start.2 = (s32[12,48]{1,0:T(8,128)S(1)}, s32[12,48]{1,0:T(8,128)}, u32[]{:S(2)}) copy-start(s32[12,48]{1,0:T(8,128)} %keep.5) | copy-start | bytes 6916
  47.4 9.6 %collective-permute-start.12 = (f32[128,384]{1,0:T(8,128)S(1)}, f32[128,384]{1,0:T(8,128)S(1)}, u32[]{:S(2)}, u32[]{:S(2)}) collective-permute-start(f32[128,384]{1,0:T(8,128)S(1)} %turn.1.refs_0_.ready), channel_id=1, source_target_pairs={{0,32},{1,97},{2,34},{3,99},{4,36},{5,101},{6,38},{7,103},{8,40},{... | collective-permute-start | bytes 589832 | tf_op jit(solution)/shard_map/ppermute | solution.py:59
  47.7 9.8 %collective-permute-start.10 = (f32[128,384]{1,0:T(8,128)S(1)}, f32[128,384]{1,0:T(8,128)S(1)}, u32[]{:S(2)}, u32[]{:S(2)}) collective-permute-start(f32[128,384]{1,0:T(8,128)S(1)} %turn.1.refs_0_.ready), channel_id=1, source_target_pairs={{0,4},{1,13},{2,6},{3,15},{4,0},{5,9},{6,2},{7,11},{8,12},{9,5},{1... | collective-permute-start | bytes 589832 | tf_op jit(solution)/shard_map/ppermute | solution.py:59
  50.3 8.4 %collective-permute-start.11 = (f32[128,384]{1,0:T(8,128)S(1)}, f32[128,384]{1,0:T(8,128)S(1)}, u32[]{:S(2)}, u32[]{:S(2)}) collective-permute-start(f32[128,384]{1,0:T(8,128)S(1)} %turn.1.refs_0_.ready), channel_id=1, source_target_pairs={{0,36},{1,109},{2,38},{3,111},{4,32},{5,105},{6,34},{7,107},{8,44}... | collective-permute-start | bytes 589832 | tf_op jit(solution)/shard_map/ppermute | solution.py:59
  63.7 10.0 %collective-permute-start.13 = (f32[128,1536]{1,0:T(8,128)S(1)}, f32[128,1536]{1,0:T(8,128)S(1)}, u32[]{:S(2)}, u32[]{:S(2)}) collective-permute-start(f32[128,1536]{1,0:T(8,128)S(1)} %get-tuple-element.32), channel_id=1, source_target_pairs={{0,1},{1,0},{2,3},{3,2},{4,5},{5,4},{6,7},{7,6},{8,9},{9,8},{10,11... | collective-permute-start | bytes 2359304 | tf_op jit(solution)/shard_map/ppermute | solution.py:59
  71.7 2.0 %collective-permute-start.14 = (f32[128,128]{1,0:T(8,128)S(1)}, f32[128,128]{1,0:T(8,128)S(1)}, u32[]{:S(2)}, u32[]{:S(2)}) collective-permute-start(f32[128,128]{1,0:T(8,128)S(1)} %gram.3), channel_id=1, source_target_pairs={{0,1},{1,0},{2,3},{3,2},{4,5},{5,4},{6,7},{7,6},{8,9},{9,8},{10,11... | collective-permute-start | bytes 196616 | tf_op jit(solution)/shard_map/ppermute | solution.py:59
  73.9 27.7 %collective-permute-start.16 = (f32[128,1536]{1,0:T(8,128)S(1)}, f32[128,1536]{1,0:T(8,128)S(1)}, u32[]{:S(2)}, u32[]{:S(2)}) collective-permute-start(f32[128,1536]{1,0:T(8,128)S(1)} %add.60), channel_id=1, source_target_pairs={{0,2},{1,3},{2,0},{3,1},{4,6},{5,7},{6,4},{7,5},{8,10},{9,11},{10,... | collective-permute-start | bytes 2359304 | tf_op jit(solution)/shard_map/ppermute | solution.py:59
  75.1 18.9 %collective-permute-start.15 = (f32[128,128]{1,0:T(8,128)S(1)}, f32[128,128]{1,0:T(8,128)S(1)}, u32[]{:S(2)}, u32[]{:S(2)}) collective-permute-start(f32[128,128]{1,0:T(8,128)S(1)} %add.61.mine), channel_id=1, source_target_pairs={{0,2},{1,3},{2,0},{3,1},{4,6},{5,7},{6,4},{7,5},{8,10},{9,11},{10,... | collective-permute-start | bytes 196616 | tf_op jit(solution)/shard_map/ppermute | solution.py:59
  82.4 19.0 %collective-permute-start.17 = (f32[128,384]{1,0:T(8,128)S(1)}, f32[128,384]{1,0:T(8,128)S(1)}, u32[]{:S(2)}, u32[]{:S(2)}) collective-permute-start(f32[128,384]{1,0:T(8,128)S(1)} %get-tuple-element.40), channel_id=1, source_target_pairs={{0,1},{1,0},{2,3},{3,2},{4,5},{5,4},{6,7},{7,6},{8,9},{9,8},{10,11... | collective-permute-start | bytes 589832 | tf_op jit(solution)/shard_map/ppermute | solution.py:59
  83.5 18.0 %collective-permute-start.18 = (f32[128,384]{1,0:T(8,128)S(1)}, f32[128,384]{1,0:T(8,128)S(1)}, u32[]{:S(2)}, u32[]{:S(2)}) collective-permute-start(f32[128,384]{1,0:T(8,128)S(1)} %get-tuple-element.41), channel_id=1, source_target_pairs={{0,1},{1,0},{2,3},{3,2},{4,5},{5,4},{6,7},{7,6},{8,9},{9,8},{10,11... | collective-permute-start | bytes 589832 | tf_op jit(solution)/shard_map/ppermute | solution.py:59
  83.6 17.9 %collective-permute-start.19 = (f32[128,384]{1,0:T(8,128)S(1)}, f32[128,384]{1,0:T(8,128)S(1)}, u32[]{:S(2)}, u32[]{:S(2)}) collective-permute-start(f32[128,384]{1,0:T(8,128)S(1)} %get-tuple-element.42), channel_id=1, source_target_pairs={{0,1},{1,0},{2,3},{3,2},{4,5},{5,4},{6,7},{7,6},{8,9},{9,8},{10,11... | collective-permute-start | bytes 589832 | tf_op jit(solution)/shard_map/ppermute | solution.py:59
  94.1 7.4 %collective-permute-start.20 = (f32[128,384]{1,0:T(8,128)S(1)}, f32[128,384]{1,0:T(8,128)S(1)}, u32[]{:S(2)}, u32[]{:S(2)}) collective-permute-start(f32[128,384]{1,0:T(8,128)S(1)} %get-tuple-element.43), channel_id=1, source_target_pairs={{0,1},{1,0},{2,3},{3,2},{4,5},{5,4},{6,7},{7,6},{8,9},{9,8},{10,11... | collective-permute-start | bytes 589832 | tf_op jit(solution)/shard_map/ppermute | solution.py:59

commit v3 on v2

v3 whole, which is shorter than its diff:
```python
import itertools
import math

import jax
import jax.numpy as jnp
from jax import lax
from jax.experimental import pallas as pl
from jax.experimental.pallas import tpu as pltpu
from jax.sharding import PartitionSpec as P

D = 6144
K = 128
BLOCK = 128
ROWS = 1536
WIDTH = 6144
QUARTER = ROWS // 4
PANEL = 1536
CHUNK = WIDTH // 8
MIB = 2**20
AXES = ("shard", "rep")
HIGHEST = lax.Precision.HIGHEST
SCALARS = pl.BlockSpec(memory_space=pltpu.SMEM)
WHOLE = pl.BlockSpec(memory_space=pltpu.VMEM)
FAR = pl.BlockSpec(memory_space=pltpu.HBM)
SMALL = pl.CostEstimate(flops=10**6, bytes_accessed=10**5, transcendentals=0)

FOLD_A, FOLD_B = (1, 0, 3, 2), (3, 2, 1, 0)
LABEL_A, LABEL_B = (0, 1, 1, 0), (0, 0, 1, 1)


def device(z, x_hi, y, x_lo, core):
    return ((z * 2 + x_hi) * 4 + y) * 4 + x_lo * 2 + core


PLACES = list(itertools.product(range(4), range(2), range(4), range(2), range(2)))


def pairs(partner):
    return [(device(*place), device(*partner(*place))) for place in PLACES]


def square(first, bits):
    def partner(z, x_hi, y, x_lo, core):
        fold = FOLD_A if (core == 0) == first else FOLD_B
        return (fold[z] if bits & 1 else z, x_hi, fold[y] if bits & 2 else y, x_lo, core)

    return pairs(partner)


ACROSS = pairs(lambda z, x_hi, y, x_lo, core: (z, 1 - x_hi, y, x_lo, core))
CORES = pairs(lambda z, x_hi, y, x_lo, core: (z, x_hi, y, x_lo, 1 - core))
CHIPS = pairs(lambda z, x_hi, y, x_lo, core: (z, x_hi, y, 1 - x_lo, core))


def swap(value, perm):
    return lax.ppermute(value, AXES, perm)


def label(table, place):
    return sum(jnp.where(place == i, v, 0) for i, v in enumerate(table) if v)


def position():
    shard, rep = lax.axis_index("shard"), lax.axis_index("rep")
    y, z = lax.rem(shard, 4), shard // 8
    core, x_lo = lax.rem(rep, 2), rep // 2
    a = 2 * label(LABEL_A, y) + label(LABEL_A, z)
    b = 2 * label(LABEL_B, y) + label(LABEL_B, z)
    return jnp.stack([jnp.where(core == 0, a, b), jnp.where(core == 0, b, a), x_lo, core]).astype(jnp.int32)


def masked(tile, keep, row_block, col_block):
    rows, cols = tile.shape
    return jnp.concatenate(
        [
            jnp.concatenate(
                [
                    tile[r * BLOCK : (r + 1) * BLOCK, c * BLOCK : (c + 1) * BLOCK]
                    * keep[row_block + r, col_block + c].astype(jnp.float32).astype(tile.dtype)
                    for c in range(cols // BLOCK)
                ],
                axis=1,
            )
            for r in range(rows // BLOCK)
        ],
        axis=0,
    )


def sketch_kernel(ks, pieces, fetch, place, keep_mask, weights, test, *refs):
    outs, refs = refs[:pieces], refs[pieces:]
    if fetch:
        right, test_sems, refs = refs[0], refs[-1], refs[1:-1]
    else:
        right = test
    keep, tiles, total, keep_sem, tile_sems = refs

    def copies(p):
        at = pl.ds(p * PANEL, PANEL)
        every = [pltpu.make_async_copy(test.at[at, :], right.at[at, :], test_sems.at[p])] if fetch else []
        for i, k in enumerate(ks):
            rows = pl.ds(pl.multiple_of((place[0] ^ k) * QUARTER, QUARTER), QUARTER)
            every.append(pltpu.make_async_copy(weights.at[rows, at], tiles.at[i, :, at], tile_sems.at[p, i]))
        return every

    keep_copy = pltpu.make_async_copy(keep_mask, keep, keep_sem)
    keep_copy.start()
    for p in range(WIDTH // PANEL):
        for copy in copies(p):
            copy.start()
    keep_copy.wait()
    height = QUARTER if len(ks) > 1 else BLOCK
    for p in range(WIDTH // PANEL):
        for copy in copies(p):
            copy.wait()
        at = slice(p * PANEL, (p + 1) * PANEL)
        for i, k in enumerate(ks):
            for r in range(0, QUARTER, height):
                rows = slice(r, r + height)
                row_block = (place[0] ^ k) * (QUARTER // BLOCK) + r // BLOCK
                tile = masked(tiles[i, rows, at], keep, row_block, p * (PANEL // BLOCK))
                part = jnp.dot(tile, right[at, :], preferred_element_type=jnp.float32)
                total[i, rows, :] = part if p == 0 else total[i, rows, :] + part
    for i, out in enumerate(outs):
        first = i * out.shape[0]
        out[...] = total[first // QUARTER, first % QUARTER : first % QUARTER + out.shape[0], :]


def sketch_parts(ks, pieces, place, keep_mask, weights, test_matrix, fetch=False):
    panels = WIDTH // PANEL
    scratch = [
        pltpu.SMEM((ROWS // BLOCK, WIDTH // BLOCK), jnp.int32),
        pltpu.VMEM((len(ks), QUARTER, WIDTH), jnp.bfloat16),
        pltpu.VMEM((len(ks), QUARTER, K), jnp.float32),
        pltpu.SemaphoreType.DMA,
        pltpu.SemaphoreType.DMA((panels, len(ks))),
    ]
    outs = [jax.ShapeDtypeStruct((QUARTER * len(ks) // pieces, K), jnp.float32)] * pieces
    if fetch:
        scratch.append(pltpu.SemaphoreType.DMA((panels,)))
        outs.append(jax.ShapeDtypeStruct((WIDTH, K), jnp.bfloat16))
    return pl.pallas_call(
        lambda *refs: sketch_kernel(ks, pieces, fetch, *refs),
        in_specs=[SCALARS, FAR, FAR, FAR if fetch else WHOLE],
        out_specs=[WHOLE] * len(outs),
        scratch_shapes=scratch,
        out_shape=outs,
        compiler_params=pltpu.CompilerParams(vmem_limit_bytes=52 * MIB),
        cost_estimate=SMALL,
        name="sketch",
    )(place, keep_mask, weights, test_matrix)


def turn_kernel(rows, out):
    out[...] = rows[...].T


def turn(quarter):
    return pl.pallas_call(
        turn_kernel,
        in_specs=[WHOLE],
        out_specs=WHOLE,
        out_shape=jax.ShapeDtypeStruct((K, QUARTER), jnp.float32),
        compiler_params=pltpu.CompilerParams(vmem_limit_bytes=4 * MIB),
        cost_estimate=SMALL,
        name="turn",
    )(quarter)


def gram_pair(first, second):
    def square_of(piece):
        return lax.dot_general(
            piece[...], piece[...], (((1,), (1,)), ((), ())), precision=HIGHEST, preferred_element_type=jnp.float32
        )

    return square_of(first) + square_of(second)


def inverse_factor_kernel(mine, theirs, out, step=4):
    gram = mine[:, CHUNK:] + theirs[:, CHUNK:]
    lanes = lax.broadcasted_iota(jnp.int32, (K, K), 1)
    rows = lax.broadcasted_iota(jnp.int32, (K, K), 0)
    unit = jnp.where(lanes == rows, 1.0, 0.0).astype(jnp.float32)
    for top in range(0, K, step):
        left = K - top
        column = [jnp.broadcast_to(gram[:, top + i : top + i + 1], (left, K)) for i in range(step)]
        row = [gram[i : i + 1, :] for i in range(step)]
        side = [unit[i : i + 1, :] for i in range(step)]
        for i in range(step):
            pivot = column[i][i : i + 1, :]
            inverse = 1.0 / pivot
            for m in range(i + 1, step):
                factor = column[i][m : m + 1, :] * inverse
                column[m] = column[m] - column[i] * factor
                row[m] = row[m] - row[i] * factor
                side[m] = side[m] - side[i] * factor
            out[top + i : top + i + 1, :] = side[i] * lax.rsqrt(pivot)
            row[i] = row[i] * inverse
            side[i] = side[i] * inverse
        if left > step:
            gram, unit = gram[step:], unit[step:]
            for i in range(step):
                gram = gram - column[i][step:] * row[i]
                unit = unit - column[i][step:] * side[i]


def inverse_factor(mine, theirs):
    return pl.pallas_call(
        inverse_factor_kernel,
        in_specs=[WHOLE] * 2,
        out_specs=WHOLE,
        out_shape=jax.ShapeDtypeStruct((K, K), jnp.float32),
        compiler_params=pltpu.CompilerParams(vmem_limit_bytes=8 * MIB),
        cost_estimate=SMALL,
        name="inverse_factor",
    )(mine, theirs)


def quarter_column(place, near, own):
    chip = place[2] if near else 1 - place[2]
    core = place[3] if own else 1 - place[3]
    return (chip * 2 + core) * (WIDTH // 4 // BLOCK)


def quarter_copies(place, near, own, weights, tile, sems):
    copies = []
    for k in range(4):
        columns = pl.ds(pl.multiple_of(quarter_column(place, near, own) * BLOCK, BLOCK), WIDTH // 4)
        rows = pl.ds(pl.multiple_of((place[0] ^ k) * QUARTER, QUARTER), QUARTER)
        at = pl.ds(k * QUARTER, QUARTER)
        copies.append(pltpu.make_async_copy(weights.at[rows, columns], tile.at[at, :], sems.at[k]))
    return copies


def kept(place, near, own, k, tile, keep):
    rows = slice(k * QUARTER, (k + 1) * QUARTER)
    return masked(tile[rows, :], keep, (place[0] ^ k) * (QUARTER // BLOCK), quarter_column(place, near, own))


def stage_kernel(own, place, keep_mask, weights, ready, out, keep, keep_sem, sems):
    keep_copy = pltpu.make_async_copy(keep_mask, keep, keep_sem)
    keep_copy.start()
    copies = quarter_copies(place, False, own, weights, out, sems)
    for copy in copies:
        copy.start()
    keep_copy.wait()
    for k in range(4):
        copies[k].wait()
        out[k * QUARTER : (k + 1) * QUARTER, :] = kept(place, False, own, k, out, keep)


def stage(own, place, keep_mask, weights, ready):
    return pl.pallas_call(
        lambda *refs: stage_kernel(own, *refs),
        in_specs=[SCALARS, FAR, FAR, FAR],
        out_specs=WHOLE,
        out_shape=jax.ShapeDtypeStruct((ROWS, WIDTH // 4), jnp.bfloat16),
        scratch_shapes=[
            pltpu.SMEM((ROWS // BLOCK, WIDTH // BLOCK), jnp.int32),
            pltpu.SemaphoreType.DMA,
            pltpu.SemaphoreType.DMA((4,)),
        ],
        compiler_params=pltpu.CompilerParams(vmem_limit_bytes=46 * MIB),
        cost_estimate=SMALL,
        name="stage",
    )(place, keep_mask, weights, ready)


def two_terms(first, second, sketch):
    for k, part in enumerate((first, second)):
        at = slice(k * QUARTER, (k + 1) * QUARTER)
        high = part[...].astype(jnp.bfloat16)
        sketch[0:K, at] = high
        sketch[K : 2 * K, at] = (part[...] - high.astype(jnp.float32)).astype(jnp.bfloat16)


def project(sketch, tile):
    both = jnp.dot(sketch[...], tile, preferred_element_type=jnp.float32)
    return both[:K] + both[K:]


def begin_kernel(first, second, send_tile, stay_tile, gram, sketch, send, stay):
    two_terms(first, second, sketch)
    gram[...] = gram_pair(first, second)
    send[...] = project(sketch, send_tile[: 2 * QUARTER, :])
    stay[...] = project(sketch, stay_tile[: 2 * QUARTER, :])


def begin(first, second, send_tile, stay_tile):
    return pl.pallas_call(
        begin_kernel,
        in_specs=[WHOLE] * 4,
        out_specs=[WHOLE] * 4,
        out_shape=[
            jax.ShapeDtypeStruct((K, K), jnp.float32),
            jax.ShapeDtypeStruct((2 * K, 2 * QUARTER), jnp.bfloat16),
            jax.ShapeDtypeStruct((K, WIDTH // 4), jnp.float32),
            jax.ShapeDtypeStruct((K, WIDTH // 4), jnp.float32),
        ],
        compiler_params=pltpu.CompilerParams(vmem_limit_bytes=16 * MIB),
        cost_estimate=SMALL,
        name="begin",
    )(first, second, send_tile, stay_tile)


def first_kernel(first, second, gram, tile, before, out, sketch):
    two_terms(first, second, sketch)
    out[:, :CHUNK] = before[:, :CHUNK] + project(sketch, tile[2 * QUARTER :, :CHUNK])
    out[:, CHUNK:] = gram[...] + gram_pair(first, second)


def first_term(first, second, gram, tile, before):
    return pl.pallas_call(
        first_kernel,
        in_specs=[WHOLE] * 5,
        out_specs=[WHOLE] * 2,
        out_shape=[
            jax.ShapeDtypeStruct((K, CHUNK + K), jnp.float32),
            jax.ShapeDtypeStruct((2 * K, 2 * QUARTER), jnp.bfloat16),
        ],
        compiler_params=pltpu.CompilerParams(vmem_limit_bytes=16 * MIB),
        cost_estimate=SMALL,
        name="first",
    )(first, second, gram, tile, before)


def far_kernel(start, sketch, tile, before, out):
    at = slice(start, start + CHUNK)
    out[...] = before[:, at] + project(sketch, tile[2 * QUARTER :, at])


def far_term(start, sketch, tile, before):
    return pl.pallas_call(
        lambda *refs: far_kernel(start, *refs),
        in_specs=[WHOLE] * 3,
        out_specs=WHOLE,
        out_shape=jax.ShapeDtypeStruct((K, CHUNK), jnp.float32),
        compiler_params=pltpu.CompilerParams(vmem_limit_bytes=16 * MIB),
        cost_estimate=SMALL,
        name="far",
    )(sketch, tile, before)


def near_kernel(place, keep_mask, sketch_a, sketch_b, weights, *refs):
    outs, keep, tiles, keep_sem, sems = refs[:8], *refs[8:]
    keep_copy = pltpu.make_async_copy(keep_mask, keep, keep_sem)
    keep_copy.start()
    copies = [quarter_copies(place, True, i == 1, weights, tiles.at[i], sems.at[i]) for i in range(2)]
    for copy in copies[0] + copies[1]:
        copy.start()
    keep_copy.wait()
    for i in range(2):
        total = 0.0
        for k, sketch in enumerate((sketch_a, sketch_a, sketch_b, sketch_b)):
            copies[i][k].wait()
            at = slice(k % 2 * QUARTER, (k % 2 + 1) * QUARTER)
            total = total + project(sketch.at[:, at], kept(place, True, i == 1, k, tiles.at[i], keep))
        for t in range(4):
            outs[4 * i + t][...] = total[:, t * QUARTER : (t + 1) * QUARTER]


def near_terms(place, keep_mask, sketch_a, sketch_b, weights):
    return pl.pallas_call(
        near_kernel,
        in_specs=[SCALARS, FAR, WHOLE, WHOLE, FAR],
        out_specs=[WHOLE] * 8,
        scratch_shapes=[
            pltpu.SMEM((ROWS // BLOCK, WIDTH // BLOCK), jnp.int32),
            pltpu.VMEM((2, ROWS, WIDTH // 4), jnp.bfloat16),
            pltpu.SemaphoreType.DMA,
            pltpu.SemaphoreType.DMA((2, 4)),
        ],
        out_shape=[jax.ShapeDtypeStruct((K, QUARTER), jnp.float32)] * 8,
        compiler_params=pltpu.CompilerParams(vmem_limit_bytes=40 * MIB),
        cost_estimate=SMALL,
        name="near",
    )(place, keep_mask, sketch_a, sketch_b, weights)


def dot_split(left, right):
    def terms(x):
        high = x.astype(jnp.bfloat16)
        return high, (x - high.astype(jnp.float32)).astype(jnp.bfloat16)

    (a, b), (c, d) = terms(left), terms(right)
    return jnp.dot(
        jnp.concatenate([a, a, b], axis=1), jnp.concatenate([c, d, c], axis=0), preferred_element_type=jnp.float32
    )


def write_turned(inverse, columns, scale, out, held, sems):
    copies = []
    for t in range(4):
        value, place = columns(t)
        held[t] = (dot_split(inverse, value) * scale).T
        rows = pl.ds(pl.multiple_of(place * QUARTER, QUARTER), QUARTER)
        copies.append(pltpu.make_async_copy(held.at[t], out.at[rows, :], sems.at[t]))
        copies[-1].start()
    for copy in copies:
        copy.wait()


TURNED = dict(
    out_specs=FAR,
    out_shape=jax.ShapeDtypeStruct((ROWS, K), jnp.float32),
    scratch_shapes=[pltpu.VMEM((4, QUARTER, K), jnp.float32), pltpu.SemaphoreType.DMA((4,))],
    compiler_params=pltpu.CompilerParams(vmem_limit_bytes=16 * MIB),
    cost_estimate=SMALL,
)


def basis_kernel(place, inverse, *refs):
    parts, out, held, sems = refs[:4], *refs[4:]
    write_turned(inverse[...], lambda k: (parts[k][...], place[0] ^ k), math.sqrt(D), out, held, sems)


def range_basis_of(place, inverse, parts):
    return pl.pallas_call(basis_kernel, in_specs=[SCALARS] + [WHOLE] * 5, name="basis", **TURNED)(place, inverse, *parts)


def finish_kernel(inverse, far_a, far_b, *refs):
    terms, out, held, sems = refs[:8], *refs[8:]

    def columns(t):
        far = (far_a, far_b)[t * QUARTER // CHUNK]
        start = t * QUARTER % CHUNK
        return terms[t][...] + terms[t + 4][...] + far[:, start : start + QUARTER], t

    write_turned(inverse[...], columns, 1.0, out, held, sems)


def finish(inverse, far, here, core):
    return pl.pallas_call(finish_kernel, in_specs=[WHOLE] * 11, name="finish", **TURNED)(inverse, *far, *here, *core)


def shards(weights, keep_mask, test_matrix):
    place = position()

    two, three, test_matrix = sketch_parts((2, 3), 2, place, keep_mask, weights, test_matrix, fetch=True)
    two, three = swap(two, square(True, 2)), swap(three, square(True, 3))
    one = [swap(piece, square(True, 1)) for piece in sketch_parts((1,), 2, place, keep_mask, weights, test_matrix)]
    part = sketch_parts((0,), 1, place, keep_mask, weights, test_matrix)[0] + three + two + jnp.concatenate(one)
    part = part + swap(part, square(False, 2))
    sent = swap(part, square(False, 1))
    send_tile = stage(False, place, keep_mask, weights, part)
    part, send_tile = lax.optimization_barrier((part + sent, send_tile))
    sent = swap(part, ACROSS)
    stay_tile = stage(True, place, keep_mask, weights, part)
    part, stay_tile = lax.optimization_barrier((part + sent, stay_tile))

    mine = turn(part)
    one, two, three = (swap(mine, square(True, k)) for k in (1, 2, 3))

    gram, sketch_a, send_a, stay_a = begin(mine, one, send_tile, stay_tile)
    send, sketch_b = first_term(two, three, gram, send_tile, send_a)
    stay = jnp.concatenate([far_term(0, sketch_b, stay_tile, stay_a), send[:, CHUNK:]], axis=1)
    total = stay + swap(send, CORES)
    far_a = swap(total, CHIPS)
    send = far_term(CHUNK, sketch_b, send_tile, send_a)
    rest = far_term(CHUNK, sketch_b, stay_tile, stay_a) + swap(send, CORES)
    rest, sketch_b = lax.optimization_barrier((rest, sketch_b))
    far_b = swap(rest, CHIPS)
    terms = near_terms(place, keep_mask, sketch_a, sketch_b, weights)
    core = [swap(term, CORES) for term in terms[:4]]
    inverse = inverse_factor(total, far_a)
    basis = range_basis_of(place, inverse, (mine, one, two, three))
    return basis, finish(inverse, (far_a, far_b), terms[4:], core)


def solution(mesh):
    placed = (P("rep", "shard"), P("rep", "shard"), P("shard", None))
    return jax.shard_map(
        shards,
        mesh=mesh,
        in_specs=placed,
        out_specs=(P("rep", None), P(("shard", "rep"), None)),
        check_vma=False,
    )
```

time: 103 us -> 77.7 us (0.75)
  waiting for transfers between devices: 28.2 us -> 12.9 us
  starting transfers between devices: 33.2 us -> 25 us
  local copies, waits for them, and re-layouts: 2.12 us -> 0.71 us
    ppermute x21 -> x18, waiting for transfers between devices: 28.2 us -> 12.9 us  [swap(): return lax.ppermute(value, AXES, perm)]
    ppermute x21 -> x18, starting transfers between devices: 33.2 us -> 25 us  [swap(): return lax.ppermute(value, AXES, perm)]
    unnamed x6 -> x4, local copies, waits for them, and re-layouts: 2.11 us -> 0.7 us
    pallas_call x8 -> x13, Pallas kernels: 32 us -> 31.3 us  [the longest x3 13.5 us: sketch_parts(): pl.pallas_call(lambda *refs: sketch_kernel(ks, pieces, fetch, *refs), in_...]
  transfers between devices with their start and end apart: 21 -> 18, of which waited for: 13 -> 9; matrix products, arithmetic and copies ran while one was open for 0% -> 0% of each run, Pallas kernels for 18% -> 38%
where the time goes in v3:
time: 77.7 us; the launch traced here: 77.5 us
  Pallas kernels  37.5 us (48%)
  starting transfers between devices  25 us (32%)
  waiting for transfers between devices  12.9 us (17%)
  between operations  1.1 us (1%)
    ppermute x18, starting transfers between devices, swap(): return lax.ppermute(value, AXES, perm)  25 us
    pallas_call x3, Pallas kernels, sketch_parts(): pl.pallas_call(lambda *refs: sketch_kernel(ks, pieces, fetch, *refs), in_...  13.5 us
    ppermute x18, waiting for transfers between devices, swap(): return lax.ppermute(value, AXES, perm)  12.9 us
    pallas_call x2, Pallas kernels, stage(): pl.pallas_call(lambda *refs: stage_kernel(own, *refs), in_specs=[SCALARS,...  6.25 us
    pallas_call x1, Pallas kernels, near_terms(): pl.pallas_call(near_kernel, in_specs=[SCALARS, FAR, WHOLE, WHOLE, FAR], o...  5.98 us
    pallas_call x1, Pallas kernels, inverse_factor(): pl.pallas_call(inverse_factor_kernel, in_specs=[WHOLE] * 2, out_specs=WHO...  4.34 us
    pallas_call x1, Pallas kernels, begin(): pl.pallas_call(begin_kernel, in_specs=[WHOLE] * 4, out_specs=[WHOLE] * 4,...  1.83 us
    pallas_call x1, Pallas kernels, range_basis_of(): pl.pallas_call(basis_kernel, in_specs=[SCALARS] + [WHOLE] * 5, name='basi...  1.81 us
  transfers between devices with their start and end apart: 18, of which 9 were waited for; matrix products, arithmetic and copies ran while one was open for 0% of the time, Pallas kernels for 38%

profile of v3, /device:TPU:1, one launch (start us, length us, event | category | flops | bytes accessed | tf_op | source)
XLA Modules:
  0.0 77.5 jit_solution(8732634512348454022)
XLA Ops:
  1.5 5.9 %sketch.3 = (f32[384,128]{1,0:T(8,128)S(1)}, f32[384,128]{1,0:T(8,128)S(1)}, bf16[6144,128]{1,0:T(8,128)(2,1)S(1)}) custom-call(s32[4]{0:T(128)S(1)} %pad_add_fusion.refs_0_.place, s32[12,48]{1,0:T(8,128)S(1)} %copy-done, bf16[1536,6144]{1,0:T(8,128)(2,1)} %weights.1, bf16[6144,128]{1,0:T(8,128)(2,1)} %refs_3_.1), custom_call_target="tpu_custom_call" | custom-call | flops 1000000 | bytes 100000 | tf_op jit(solution)/shard_map/sketch/pallas_call | solution.py:142
  7.3 7.1 %collective-permute-start = (f32[384,128]{1,0:T(8,128)S(1)}, f32[384,128]{1,0:T(8,128)S(1)}, u32[]{:S(2)}, u32[]{:S(2)}) collective-permute-start(f32[384,128]{1,0:T(8,128)S(1)} %get-tuple-element.28), channel_id=1, source_target_pairs={{0,36},{1,109},{2,38},{3,111},{4,32},{5,105},{6,34},{7,107},{8,44}... | collective-permute-start | bytes 589832 | tf_op jit(solution)/shard_map/ppermute | solution.py:56
  14.5 3.8 %sketch.5 = (f32[192,128]{1,0:T(8,128)S(1)}, f32[192,128]{1,0:T(8,128)S(1)}) custom-call(s32[4]{0:T(128)S(1)} %pad_add_fusion.refs_0_.place, s32[12,48]{1,0:T(8,128)S(1)} %copy-done, bf16[1536,6144]{1,0:T(8,128)(2,1)} %weights.1, bf16[6144,128]{1,0:T(8,128)(2,1)S(1)} %get-tuple-element.27.refs_3_), custom_call_target="tpu_custom_call" | custom-call | flops 1000000 | bytes 100000 | tf_op jit(solution)/shard_map/sketch/pallas_call | solution.py:142
  18.7 2.3 %collective-permute-start.3 = (f32[192,128]{1,0:T(8,128)S(1)}, f32[192,128]{1,0:T(8,128)S(1)}, u32[]{:S(2)}, u32[]{:S(2)}) collective-permute-start(f32[192,128]{1,0:T(8,128)S(1)} %get-tuple-element.31), channel_id=1, source_target_pairs={{0,32},{1,97},{2,34},{3,99},{4,36},{5,101},{6,38},{7,103},{8,40},{... | collective-permute-start | bytes 294920 | tf_op jit(solution)/shard_map/ppermute | solution.py:56
  21.0 3.8 %sketch.4 = f32[384,128]{1,0:T(8,128)S(1)} custom-call(s32[4]{0:T(128)S(1)} %pad_add_fusion.refs_0_.place, s32[12,48]{1,0:T(8,128)S(1)} %copy-done, bf16[1536,6144]{1,0:T(8,128)(2,1)} %weights.1, bf16[6144,128]{1,0:T(8,128)(2,1)S(1)} %get-tuple-element.27.refs_3_), custom_call_target="tpu_custom_call" | custom-call | flops 1000000 | bytes 100000 | tf_op jit(solution)/shard_map/sketch/pallas_call | solution.py:142
  25.1 4.5 %collective-permute-done.4 = f32[384,128]{1,0:T(8,128)S(1)} collective-permute-done((f32[384,128]{1,0:T(8,128)S(1)}, f32[384,128]{1,0:T(8,128)S(1)}, u32[]{:S(2)}, u32[]{:S(2)}) %collective-permute-start.4) | collective-permute-done | bytes 196640 | tf_op jit(solution)/shard_map/ppermute | solution.py:56
  29.7 3.1 %stage.2.send_tile.tile.refs_1_ = bf16[1536,1536]{1,0:T(8,128)(2,1)S(1)} custom-call(s32[4]{0:T(128)S(1)} %pad_add_fusion.refs_0_.place, s32[12,48]{1,0:T(8,128)S(1)} %copy-done.1, bf16[1536,6144]{1,0:T(8,128)(2,1)} %weights.1, f32[384,128]{1,0:T(8,128)S(1)} %add.53.refs_3_), custom_call_target="tpu_custom_call" | custom-call | flops 1000000 | bytes 100000 | tf_op jit(solution)/shard_map/stage/pallas_call | solution.py:253
  32.8 1.7 %collective-permute-done.5 = f32[384,128]{1,0:T(8,128)S(1)} collective-permute-done((f32[384,128]{1,0:T(8,128)S(1)}, f32[384,128]{1,0:T(8,128)S(1)}, u32[]{:S(2)}, u32[]{:S(2)}) %collective-permute-start.5) | collective-permute-done | bytes 196640 | tf_op jit(solution)/shard_map/ppermute | solution.py:56
  34.5 2.8 %collective-permute-start.6 = (f32[384,128]{1,0:T(8,128)S(1)}, f32[384,128]{1,0:T(8,128)S(1)}, u32[]{:S(2)}, u32[]{:S(2)}) collective-permute-start(f32[384,128]{1,0:T(8,128)S(1)} %add.54.refs_3_), channel_id=1, source_target_pairs={{0,16},{1,17},{2,18},{3,19},{4,20},{5,21},{6,22},{7,23},{8,24},{9,... | collective-permute-start | bytes 589832 | tf_op jit(solution)/shard_map/ppermute | solution.py:56
  37.3 3.1 %stage.3.stay_tile.refs_1_ = bf16[1536,1536]{1,0:T(8,128)(2,1)S(1)} custom-call(s32[4]{0:T(128)S(1)} %pad_add_fusion.refs_0_.place, s32[12,48]{1,0:T(8,128)S(1)} %copy-done.1, bf16[1536,6144]{1,0:T(8,128)(2,1)} %weights.1, f32[384,128]{1,0:T(8,128)S(1)} %add.54.refs_3_), custom_call_target="tpu_custom_call" | custom-call | flops 1000000 | bytes 100000 | tf_op jit(solution)/shard_map/stage/pallas_call | solution.py:253
  41.7 4.3 %collective-permute-start.8 = (f32[128,384]{1,0:T(8,128)S(1)}, f32[128,384]{1,0:T(8,128)S(1)}, u32[]{:S(2)}, u32[]{:S(2)}) collective-permute-start(f32[128,384]{1,0:T(8,128)S(1)} %turn.1.first.refs_0_), channel_id=1, source_target_pairs={{0,36},{1,109},{2,38},{3,111},{4,32},{5,105},{6,34},{7,107},{8,44}... | collective-permute-start | bytes 589832 | tf_op jit(solution)/shard_map/ppermute | solution.py:56
  46.6 1.8 %begin.1 = (f32[128,128]{1,0:T(8,128)S(1)}, bf16[256,768]{1,0:T(8,128)(2,1)S(1)}, f32[128,1536]{1,0:T(8,128)S(1)}, f32[128,1536]{1,0:T(8,128)S(1)}) custom-call(f32[128,384]{1,0:T(8,128)S(1)} %turn.1.first.refs_0_, f32[128,384]{1,0:T(8,128)S(1)} %collective-permute-done.9.second.refs_1_, bf16[1536,1536]{1,0:T(8,128)(2,1)S(1)} %stage.2.send_tile.tile.refs_1_, ...), custom_call_target="tpu_custom_call" | custom-call | flops 1000000 | bytes 100000 | tf_op jit(solution)/shard_map/begin/pallas_call | solution.py:290
  48.4 1.1 %collective-permute-done.8.second.refs_3_ = f32[128,384]{1,0:T(8,128)S(1)} collective-permute-done((f32[128,384]{1,0:T(8,128)S(1)}, f32[128,384]{1,0:T(8,128)S(1)}, u32[]{:S(2)}, u32[]{:S(2)}) %collective-permute-start.8) | collective-permute-done | bytes 196640 | tf_op jit(solution)/shard_map/ppermute | solution.py:56
  49.5 2.1 %collective-permute-done.7.first.refs_2_ = f32[128,384]{1,0:T(8,128)S(1)} collective-permute-done((f32[128,384]{1,0:T(8,128)S(1)}, f32[128,384]{1,0:T(8,128)S(1)}, u32[]{:S(2)}, u32[]{:S(2)}) %collective-permute-start.7) | collective-permute-done | bytes 196640 | tf_op jit(solution)/shard_map/ppermute | solution.py:56
  51.7 0.9 %first.1 = (f32[128,896]{1,0:T(8,128)S(1)}, bf16[256,768]{1,0:T(8,128)(2,1)S(1)}) custom-call(f32[128,384]{1,0:T(8,128)S(1)} %collective-permute-done.7.first.refs_2_, f32[128,384]{1,0:T(8,128)S(1)} %collective-permute-done.8.second.refs_3_, f32[128,128]{1,0:T(8,128)S(1)} %get-tuple-element.36.gram, bf16[1536,1536]{1,0:T(8,128)(2,1)S(1)} %stage.2.send_tile.tile.refs_1_, ...), custom_call_target="tpu_custom_call" | custom-call | flops 1000000 | bytes 100000 | tf_op jit(solution)/shard_map/first/pallas_call | solution.py:313
  52.6 1.7 %collective-permute-start.10 = (f32[128,896]{1,0:T(8,128)S(1)}, f32[128,896]{1,0:T(8,128)S(1)}, u32[]{:S(2)}, u32[]{:S(2)}) collective-permute-start(f32[128,896]{1,0:T(8,128)S(1)} %get-tuple-element.40), channel_id=1, source_target_pairs={{0,1},{1,0},{2,3},{3,2},{4,5},{5,4},{6,7},{7,6},{8,9},{9,8},{10,11... | collective-permute-start | bytes 1376264 | tf_op jit(solution)/shard_map/ppermute | solution.py:56
  55.8 1.3 %collective-permute-start.11 = (f32[128,896]{1,0:T(8,128)S(1)}, f32[128,896]{1,0:T(8,128)S(1)}, u32[]{:S(2)}, u32[]{:S(2)}) collective-permute-start(f32[128,896]{1,0:T(8,128)S(1)} %maximum_add_fusion.mine), channel_id=1, source_target_pairs={{0,2},{1,3},{2,0},{3,1},{4,6},{5,7},{6,4},{7,5},{8,10},{9,11},{10,... | collective-permute-start | bytes 1376264 | tf_op jit(solution)/shard_map/ppermute | solution.py:56
  58.0 6.0 %near.1 = (f32[128,384]{1,0:T(8,128)S(1)}, f32[128,384]{1,0:T(8,128)S(1)}, f32[128,384]{1,0:T(8,128)S(1)}, f32[128,384]{1,0:T(8,128)S(1)}, f32[128,384]{1,0:T(8,...) custom-call(s32[4]{0:T(128)S(1)} %pad_add_fusion.refs_0_.place, ...), custom_call_target="tpu_custom_call" | custom-call | flops 1000000 | bytes 100000 | tf_op jit(solution)/shard_map/near/pallas_call | solution.py:363
  64.0 1.0 %collective-permute-start.14 = (f32[128,384]{1,0:T(8,128)S(1)}, f32[128,384]{1,0:T(8,128)S(1)}, u32[]{:S(2)}, u32[]{:S(2)}) collective-permute-start(f32[128,384]{1,0:T(8,128)S(1)} %get-tuple-element.48), channel_id=1, source_target_pairs={{0,1},{1,0},{2,3},{3,2},{4,5},{5,4},{6,7},{7,6},{8,9},{9,8},{10,11... | collective-permute-start | bytes 589832 | tf_op jit(solution)/shard_map/ppermute | solution.py:56
  65.5 2.1 %collective-permute-done.11.theirs.far_a = f32[128,896]{1,0:T(8,128)S(1)} collective-permute-done((f32[128,896]{1,0:T(8,128)S(1)}, f32[128,896]{1,0:T(8,128)S(1)}, u32[]{:S(2)}, u32[]{:S(2)}) %collective-permute-start.11) | collective-permute-done | bytes 458784 | tf_op jit(solution)/shard_map/ppermute | solution.py:56
  67.6 2.0 %collective-permute-start.17 = (f32[128,384]{1,0:T(8,128)S(1)}, f32[128,384]{1,0:T(8,128)S(1)}, u32[]{:S(2)}, u32[]{:S(2)}) collective-permute-start(f32[128,384]{1,0:T(8,128)S(1)} %get-tuple-element.51), channel_id=1, source_target_pairs={{0,1},{1,0},{2,3},{3,2},{4,5},{5,4},{6,7},{7,6},{8,9},{9,8},{10,11... | collective-permute-start | bytes 589832 | tf_op jit(solution)/shard_map/ppermute | solution.py:56
  69.6 4.3 %inverse_factor.1.inverse = f32[128,128]{1,0:T(8,128)S(1)} custom-call(f32[128,896]{1,0:T(8,128)S(1)} %maximum_add_fusion.mine, f32[128,896]{1,0:T(8,128)S(1)} %collective-permute-done.11.theirs.far_a), custom_call_target="tpu_custom_call" | custom-call | flops 1000000 | bytes 100000 | tf_op jit(solution)/shard_map/inverse_factor/pallas_call | solution.py:208
  74.0 1.8 %basis.1 = f32[1536,128]{1,0:T(8,128)} custom-call(s32[4]{0:T(128)S(1)} %pad_add_fusion.refs_0_.place, f32[128,128]{1,0:T(8,128)S(1)} %inverse_factor.1.inverse, f32[128,384]{1,0:T(8,128)S(1)} %turn.1.first.refs_0_, f32[128,384]{1,0:T(8,128)S(1)} %collective-permute-done.9.second.refs_1_, f32[128,384]{1,0:T(8,128)S(1)} %collective-permute-done.7.first.refs_2_, ...), custom_call_target="tpu_custom_call" | custom-call | flops 1000000 | bytes 100000 | tf_op jit(solution)/shard_map/basis/pallas_call | solution.py:418
  76.1 1.3 %finish.1 = f32[1536,128]{1,0:T(8,128)} custom-call(f32[128,128]{1,0:T(8,128)S(1)} %inverse_factor.1.inverse, f32[128,896]{1,0:T(8,128)S(1)} %collective-permute-done.11.theirs.far_a, f32[128,768]{1,0:T(8,128)S(1)} %collective-permute-done.13.far_b, f32[128,384]{1,0:T(8,128)S(1)} %get-tuple-element.44.refs_0_, f32[128,384]{1,0:T(8,128)S(1)} %get-tuple-element.45.refs_1_, ...), custom_call_target="tpu_custom_call" | custom-call | flops 1000000 | bytes 100000 | tf_op jit(solution)/shard_map/finish/pallas_call | solution.py:433
  (39 shorter events, 6.5 us)
Async XLA Ops:
  0.8 0.7 copy-start
  7.3 17.5 %collective-permute-start = (f32[384,128]{1,0:T(8,128)S(1)}, f32[384,128]{1,0:T(8,128)S(1)}, u32[]{:S(2)}, u32[]{:S(2)}) collective-permute-start(f32[384,128]{1,0:T(8,128)S(1)} %get-tuple-element.28), channel_id=1, source_target_pairs={{0,36},{1,109},{2,38},{3,111},{4,32},{5,105},{6,34},{7,107},{8,44}... | collective-permute-start | bytes 589832 | tf_op jit(solution)/shard_map/ppermute | solution.py:56
  14.5 10.4 %collective-permute-start.1 = (f32[384,128]{1,0:T(8,128)S(1)}, f32[384,128]{1,0:T(8,128)S(1)}, u32[]{:S(2)}, u32[]{:S(2)}) collective-permute-start(f32[384,128]{1,0:T(8,128)S(1)} %get-tuple-element.29), channel_id=1, source_target_pairs={{0,4},{1,13},{2,6},{3,15},{4,0},{5,9},{6,2},{7,11},{8,12},{9,5},{1... | collective-permute-start | bytes 589832 | tf_op jit(solution)/shard_map/ppermute | solution.py:56
  18.3 6.6 %collective-permute-start.2 = (f32[192,128]{1,0:T(8,128)S(1)}, f32[192,128]{1,0:T(8,128)S(1)}, u32[]{:S(2)}, u32[]{:S(2)}) collective-permute-start(f32[192,128]{1,0:T(8,128)S(1)} %get-tuple-element.30), channel_id=1, source_target_pairs={{0,32},{1,97},{2,34},{3,99},{4,36},{5,101},{6,38},{7,103},{8,40},{... | collective-permute-start | bytes 294920 | tf_op jit(solution)/shard_map/ppermute | solution.py:56
  18.7 10.9 %copy-start.1 = (s32[12,48]{1,0:T(8,128)S(1)}, s32[12,48]{1,0:T(8,128)}, u32[]{:S(2)}) copy-start(s32[12,48]{1,0:T(8,128)} %keep_mask.1) | copy-start | bytes 6916
  18.7 6.1 %collective-permute-start.3 = (f32[192,128]{1,0:T(8,128)S(1)}, f32[192,128]{1,0:T(8,128)S(1)}, u32[]{:S(2)}, u32[]{:S(2)}) collective-permute-start(f32[192,128]{1,0:T(8,128)S(1)} %get-tuple-element.31), channel_id=1, source_target_pairs={{0,32},{1,97},{2,34},{3,99},{4,36},{5,101},{6,38},{7,103},{8,40},{... | collective-permute-start | bytes 294920 | tf_op jit(solution)/shard_map/ppermute | solution.py:56
  25.0 4.6 %collective-permute-start.4 = (f32[384,128]{1,0:T(8,128)S(1)}, f32[384,128]{1,0:T(8,128)S(1)}, u32[]{:S(2)}, u32[]{:S(2)}) collective-permute-start(f32[384,128]{1,0:T(8,128)S(1)} %maximum_add_fusion.1), channel_id=1, source_target_pairs={{0,12},{1,5},{2,14},{3,7},{4,8},{5,1},{6,10},{7,3},{8,4},{9,13},{1... | collective-permute-start | bytes 589832 | tf_op jit(solution)/shard_map/ppermute | solution.py:56
  29.6 4.9 %collective-permute-start.5 = (f32[384,128]{1,0:T(8,128)S(1)}, f32[384,128]{1,0:T(8,128)S(1)}, u32[]{:S(2)}, u32[]{:S(2)}) collective-permute-start(f32[384,128]{1,0:T(8,128)S(1)} %add.53.refs_3_), channel_id=1, source_target_pairs={{0,96},{1,33},{2,98},{3,35},{4,100},{5,37},{6,102},{7,39},{8,104},... | collective-permute-start | bytes 589832 | tf_op jit(solution)/shard_map/ppermute | solution.py:56
  34.5 6.1 %collective-permute-start.6 = (f32[384,128]{1,0:T(8,128)S(1)}, f32[384,128]{1,0:T(8,128)S(1)}, u32[]{:S(2)}, u32[]{:S(2)}) collective-permute-start(f32[384,128]{1,0:T(8,128)S(1)} %add.54.refs_3_), channel_id=1, source_target_pairs={{0,16},{1,17},{2,18},{3,19},{4,20},{5,21},{6,22},{7,23},{8,24},{9,... | collective-permute-start | bytes 589832 | tf_op jit(solution)/shard_map/ppermute | solution.py:56
  40.8 5.8 %collective-permute-start.9 = (f32[128,384]{1,0:T(8,128)S(1)}, f32[128,384]{1,0:T(8,128)S(1)}, u32[]{:S(2)}, u32[]{:S(2)}) collective-permute-start(f32[128,384]{1,0:T(8,128)S(1)} %turn.1.first.refs_0_), channel_id=1, source_target_pairs={{0,32},{1,97},{2,34},{3,99},{4,36},{5,101},{6,38},{7,103},{8,40},{... | collective-permute-start | bytes 589832 | tf_op jit(solution)/shard_map/ppermute | solution.py:56
  41.7 7.8 %collective-permute-start.8 = (f32[128,384]{1,0:T(8,128)S(1)}, f32[128,384]{1,0:T(8,128)S(1)}, u32[]{:S(2)}, u32[]{:S(2)}) collective-permute-start(f32[128,384]{1,0:T(8,128)S(1)} %turn.1.first.refs_0_), channel_id=1, source_target_pairs={{0,36},{1,109},{2,38},{3,111},{4,32},{5,105},{6,34},{7,107},{8,44}... | collective-permute-start | bytes 589832 | tf_op jit(solution)/shard_map/ppermute | solution.py:56
  45.9 5.7 %collective-permute-start.7 = (f32[128,384]{1,0:T(8,128)S(1)}, f32[128,384]{1,0:T(8,128)S(1)}, u32[]{:S(2)}, u32[]{:S(2)}) collective-permute-start(f32[128,384]{1,0:T(8,128)S(1)} %turn.1.first.refs_0_), channel_id=1, source_target_pairs={{0,4},{1,13},{2,6},{3,15},{4,0},{5,9},{6,2},{7,11},{8,12},{9,5},{1... | collective-permute-start | bytes 589832 | tf_op jit(solution)/shard_map/ppermute | solution.py:56
  52.6 3.2 %collective-permute-start.10 = (f32[128,896]{1,0:T(8,128)S(1)}, f32[128,896]{1,0:T(8,128)S(1)}, u32[]{:S(2)}, u32[]{:S(2)}) collective-permute-start(f32[128,896]{1,0:T(8,128)S(1)} %get-tuple-element.40), channel_id=1, source_target_pairs={{0,1},{1,0},{2,3},{3,2},{4,5},{5,4},{6,7},{7,6},{8,9},{9,8},{10,11... | collective-permute-start | bytes 1376264 | tf_op jit(solution)/shard_map/ppermute | solution.py:56
  54.8 2.8 %collective-permute-start.12 = (f32[128,768]{1,0:T(8,128)S(1)}, f32[128,768]{1,0:T(8,128)S(1)}, u32[]{:S(2)}, u32[]{:S(2)}) collective-permute-start(f32[128,768]{1,0:T(8,128)S(1)} %far.5), channel_id=1, source_target_pairs={{0,1},{1,0},{2,3},{3,2},{4,5},{5,4},{6,7},{7,6},{8,9},{9,8},{10,11... | collective-permute-start | bytes 1179656 | tf_op jit(solution)/shard_map/ppermute | solution.py:56
  55.8 11.8 %collective-permute-start.11 = (f32[128,896]{1,0:T(8,128)S(1)}, f32[128,896]{1,0:T(8,128)S(1)}, u32[]{:S(2)}, u32[]{:S(2)}) collective-permute-start(f32[128,896]{1,0:T(8,128)S(1)} %maximum_add_fusion.mine), channel_id=1, source_target_pairs={{0,2},{1,3},{2,0},{3,1},{4,6},{5,7},{6,4},{7,5},{8,10},{9,11},{10,... | collective-permute-start | bytes 1376264 | tf_op jit(solution)/shard_map/ppermute | solution.py:56
  57.7 18.4 %collective-permute-start.13 = (f32[128,768]{1,0:T(8,128)S(1)}, f32[128,768]{1,0:T(8,128)S(1)}, u32[]{:S(2)}, u32[]{:S(2)}) collective-permute-start(f32[128,768]{1,0:T(8,128)S(1)} %add.57), channel_id=1, source_target_pairs={{0,2},{1,3},{2,0},{3,1},{4,6},{5,7},{6,4},{7,5},{8,10},{9,11},{10,... | collective-permute-start | bytes 1179656 | tf_op jit(solution)/shard_map/ppermute | solution.py:56
  64.0 11.8 %collective-permute-start.14 = (f32[128,384]{1,0:T(8,128)S(1)}, f32[128,384]{1,0:T(8,128)S(1)}, u32[]{:S(2)}, u32[]{:S(2)}) collective-permute-start(f32[128,384]{1,0:T(8,128)S(1)} %get-tuple-element.48), channel_id=1, source_target_pairs={{0,1},{1,0},{2,3},{3,2},{4,5},{5,4},{6,7},{7,6},{8,9},{9,8},{10,11... | collective-permute-start | bytes 589832 | tf_op jit(solution)/shard_map/ppermute | solution.py:56
  65.0 10.8 %collective-permute-start.15 = (f32[128,384]{1,0:T(8,128)S(1)}, f32[128,384]{1,0:T(8,128)S(1)}, u32[]{:S(2)}, u32[]{:S(2)}) collective-permute-start(f32[128,384]{1,0:T(8,128)S(1)} %get-tuple-element.49), channel_id=1, source_target_pairs={{0,1},{1,0},{2,3},{3,2},{4,5},{5,4},{6,7},{7,6},{8,9},{9,8},{10,11... | collective-permute-start | bytes 589832 | tf_op jit(solution)/shard_map/ppermute | solution.py:56
  65.1 10.7 %collective-permute-start.16 = (f32[128,384]{1,0:T(8,128)S(1)}, f32[128,384]{1,0:T(8,128)S(1)}, u32[]{:S(2)}, u32[]{:S(2)}) collective-permute-start(f32[128,384]{1,0:T(8,128)S(1)} %get-tuple-element.50), channel_id=1, source_target_pairs={{0,1},{1,0},{2,3},{3,2},{4,5},{5,4},{6,7},{7,6},{8,9},{9,8},{10,11... | collective-permute-start | bytes 589832 | tf_op jit(solution)/shard_map/ppermute | solution.py:56
  67.6 8.2 %collective-permute-start.17 = (f32[128,384]{1,0:T(8,128)S(1)}, f32[128,384]{1,0:T(8,128)S(1)}, u32[]{:S(2)}, u32[]{:S(2)}) collective-permute-start(f32[128,384]{1,0:T(8,128)S(1)} %get-tuple-element.51), channel_id=1, source_target_pairs={{0,1},{1,0},{2,3},{3,2},{4,5},{5,4},{6,7},{7,6},{8,9},{9,8},{10,11... | collective-permute-start | bytes 589832 | tf_op jit(solution)/shard_map/ppermute | solution.py:56

commit v4 on v3

--- a/solution.py
+++ b/solution.py
@@ -16,6 +16,7 @@
 QUARTER = ROWS // 4
 PANEL = 1536
 CHUNK = WIDTH // 8
+ORDER = (0, 3, 1, 2)
 MIB = 2**20
 AXES = ("shard", "rep")
 HIGHEST = lax.Precision.HIGHEST
@@ -39,10 +40,14 @@
     return [(device(*place), device(*partner(*place))) for place in PLACES]
 
 
+def folds(first, core):
+    return (FOLD_A, FOLD_A) if (core == 0) == first else (FOLD_B, FOLD_B)
+
+
 def square(first, bits):
     def partner(z, x_hi, y, x_lo, core):
-        fold = FOLD_A if (core == 0) == first else FOLD_B
-        return (fold[z] if bits & 1 else z, x_hi, fold[y] if bits & 2 else y, x_lo, core)
+        fold_y, fold_z = folds(first, core)
+        return (fold_z[z] if bits & 1 else z, x_hi, fold_y[y] if bits & 2 else y, x_lo, core)
 
     return pairs(partner)
 
@@ -64,9 +69,9 @@
     shard, rep = lax.axis_index("shard"), lax.axis_index("rep")
     y, z = lax.rem(shard, 4), shard // 8
     core, x_lo = lax.rem(rep, 2), rep // 2
-    a = 2 * label(LABEL_A, y) + label(LABEL_A, z)
-    b = 2 * label(LABEL_B, y) + label(LABEL_B, z)
-    return jnp.stack([jnp.where(core == 0, a, b), jnp.where(core == 0, b, a), x_lo, core]).astype(jnp.int32)
+    even = 2 * label(LABEL_A, y) + label(LABEL_A, z)
+    odd = 2 * label(LABEL_B, y) + label(LABEL_B, z)
+    return jnp.stack([jnp.where(core == 0, even, odd), x_lo, core]).astype(jnp.int32)
 
 
 def masked(tile, keep, row_block, col_block):
@@ -87,17 +92,12 @@
     )
 
 
-def sketch_kernel(ks, pieces, fetch, place, keep_mask, weights, test, *refs):
-    outs, refs = refs[:pieces], refs[pieces:]
-    if fetch:
-        right, test_sems, refs = refs[0], refs[-1], refs[1:-1]
-    else:
-        right = test
-    keep, tiles, total, keep_sem, tile_sems = refs
+def sketch_kernel(ks, place, keep_mask, weights, right, *refs):
+    outs, keep, tiles, total, keep_sem, tile_sems = refs[: len(ks)], *refs[len(ks) :]
 
     def copies(p):
         at = pl.ds(p * PANEL, PANEL)
-        every = [pltpu.make_async_copy(test.at[at, :], right.at[at, :], test_sems.at[p])] if fetch else []
+        every = []
         for i, k in enumerate(ks):
             rows = pl.ds(pl.multiple_of((place[0] ^ k) * QUARTER, QUARTER), QUARTER)
             every.append(pltpu.make_async_copy(weights.at[rows, at], tiles.at[i, :, at], tile_sems.at[p, i]))
@@ -109,24 +109,22 @@
         for copy in copies(p):
             copy.start()
     keep_copy.wait()
-    height = QUARTER if len(ks) > 1 else BLOCK
     for p in range(WIDTH // PANEL):
         for copy in copies(p):
             copy.wait()
         at = slice(p * PANEL, (p + 1) * PANEL)
         for i, k in enumerate(ks):
-            for r in range(0, QUARTER, height):
-                rows = slice(r, r + height)
+            for r in range(0, QUARTER, BLOCK):
+                rows = slice(r, r + BLOCK)
                 row_block = (place[0] ^ k) * (QUARTER // BLOCK) + r // BLOCK
                 tile = masked(tiles[i, rows, at], keep, row_block, p * (PANEL // BLOCK))
                 part = jnp.dot(tile, right[at, :], preferred_element_type=jnp.float32)
                 total[i, rows, :] = part if p == 0 else total[i, rows, :] + part
     for i, out in enumerate(outs):
-        first = i * out.shape[0]
-        out[...] = total[first // QUARTER, first % QUARTER : first % QUARTER + out.shape[0], :]
-
-
-def sketch_parts(ks, pieces, place, keep_mask, weights, test_matrix, fetch=False):
+        out[...] = total[i]
+
+
+def sketch_parts(ks, place, keep_mask, weights, test_matrix):
     panels = WIDTH // PANEL
     scratch = [
         pltpu.SMEM((ROWS // BLOCK, WIDTH // BLOCK), jnp.int32),
@@ -135,17 +133,14 @@
         pltpu.SemaphoreType.DMA,
         pltpu.SemaphoreType.DMA((panels, len(ks))),
     ]
-    outs = [jax.ShapeDtypeStruct((QUARTER * len(ks) // pieces, K), jnp.float32)] * pieces
-    if fetch:
-        scratch.append(pltpu.SemaphoreType.DMA((panels,)))
-        outs.append(jax.ShapeDtypeStruct((WIDTH, K), jnp.bfloat16))
-    return pl.pallas_call(
-        lambda *refs: sketch_kernel(ks, pieces, fetch, *refs),
-        in_specs=[SCALARS, FAR, FAR, FAR if fetch else WHOLE],
+    outs = [jax.ShapeDtypeStruct((QUARTER, K), jnp.float32)] * len(ks)
+    return pl.pallas_call(
+        lambda *refs: sketch_kernel(ks, *refs),
+        in_specs=[SCALARS, FAR, FAR, WHOLE],
         out_specs=[WHOLE] * len(outs),
         scratch_shapes=scratch,
         out_shape=outs,
-        compiler_params=pltpu.CompilerParams(vmem_limit_bytes=52 * MIB),
+        compiler_params=pltpu.CompilerParams(vmem_limit_bytes=51 * MIB),
         cost_estimate=SMALL,
         name="sketch",
     )(place, keep_mask, weights, test_matrix)
@@ -217,8 +212,8 @@
 
 
 def quarter_column(place, near, own):
-    chip = place[2] if near else 1 - place[2]
-    core = place[3] if own else 1 - place[3]
+    chip = place[1] if near else 1 - place[1]
+    core = place[2] if own else 1 - place[2]
     return (chip * 2 + core) * (WIDTH // 4 // BLOCK)
 
 
@@ -226,7 +221,7 @@
     copies = []
     for k in range(4):
         columns = pl.ds(pl.multiple_of(quarter_column(place, near, own) * BLOCK, BLOCK), WIDTH // 4)
-        rows = pl.ds(pl.multiple_of((place[0] ^ k) * QUARTER, QUARTER), QUARTER)
+        rows = pl.ds(pl.multiple_of((place[0] ^ ORDER[k]) * QUARTER, QUARTER), QUARTER)
         at = pl.ds(k * QUARTER, QUARTER)
         copies.append(pltpu.make_async_copy(weights.at[rows, columns], tile.at[at, :], sems.at[k]))
     return copies
@@ -234,7 +229,7 @@
 
 def kept(place, near, own, k, tile, keep):
     rows = slice(k * QUARTER, (k + 1) * QUARTER)
-    return masked(tile[rows, :], keep, (place[0] ^ k) * (QUARTER // BLOCK), quarter_column(place, near, own))
+    return masked(tile[rows, :], keep, (place[0] ^ ORDER[k]) * (QUARTER // BLOCK), quarter_column(place, near, own))
 
 
 def stage_kernel(own, place, keep_mask, weights, ready, out, keep, keep_sem, sems):
@@ -266,8 +261,8 @@
     )(place, keep_mask, weights, ready)
 
 
-def two_terms(first, second, sketch):
-    for k, part in enumerate((first, second)):
+def two_terms(parts, sketch):
+    for k, part in enumerate(parts):
         at = slice(k * QUARTER, (k + 1) * QUARTER)
         high = part[...].astype(jnp.bfloat16)
         sketch[0:K, at] = high
@@ -279,14 +274,14 @@
     return both[:K] + both[K:]
 
 
-def begin_kernel(first, second, send_tile, stay_tile, gram, sketch, send, stay):
-    two_terms(first, second, sketch)
-    gram[...] = gram_pair(first, second)
+def begin_kernel(mine, three, send_tile, stay_tile, gram, sketch, send, stay):
+    two_terms((mine, three), sketch)
+    gram[...] = gram_pair(mine, three)
     send[...] = project(sketch, send_tile[: 2 * QUARTER, :])
     stay[...] = project(sketch, stay_tile[: 2 * QUARTER, :])
 
 
-def begin(first, second, send_tile, stay_tile):
+def begin(mine, three, send_tile, stay_tile):
     return pl.pallas_call(
         begin_kernel,
         in_specs=[WHOLE] * 4,
@@ -300,16 +295,16 @@
         compiler_params=pltpu.CompilerParams(vmem_limit_bytes=16 * MIB),
         cost_estimate=SMALL,
         name="begin",
-    )(first, second, send_tile, stay_tile)
-
-
-def first_kernel(first, second, gram, tile, before, out, sketch):
-    two_terms(first, second, sketch)
+    )(mine, three, send_tile, stay_tile)
+
+
+def first_kernel(one, two, gram, tile, before, out, sketch):
+    two_terms((one, two), sketch)
     out[:, :CHUNK] = before[:, :CHUNK] + project(sketch, tile[2 * QUARTER :, :CHUNK])
-    out[:, CHUNK:] = gram[...] + gram_pair(first, second)
-
-
-def first_term(first, second, gram, tile, before):
+    out[:, CHUNK:] = gram[...] + gram_pair(one, two)
+
+
+def first_term(one, two, gram, tile, before):
     return pl.pallas_call(
         first_kernel,
         in_specs=[WHOLE] * 5,
@@ -321,7 +316,7 @@
         compiler_params=pltpu.CompilerParams(vmem_limit_bytes=16 * MIB),
         cost_estimate=SMALL,
         name="first",
-    )(first, second, gram, tile, before)
+    )(one, two, gram, tile, before)
 
 
 def far_kernel(start, sketch, tile, before, out):
@@ -351,10 +346,10 @@
     keep_copy.wait()
     for i in range(2):
         total = 0.0
-        for k, sketch in enumerate((sketch_a, sketch_a, sketch_b, sketch_b)):
+        for k in range(4):
             copies[i][k].wait()
-            at = slice(k % 2 * QUARTER, (k % 2 + 1) * QUARTER)
-            total = total + project(sketch.at[:, at], kept(place, True, i == 1, k, tiles.at[i], keep))
+            sketch = (sketch_a, sketch_b)[k // 2].at[:, k % 2 * QUARTER : (k % 2 + 1) * QUARTER]
+            total = total + project(sketch, kept(place, True, i == 1, k, tiles.at[i], keep))
         for t in range(4):
             outs[4 * i + t][...] = total[:, t * QUARTER : (t + 1) * QUARTER]
 
@@ -436,14 +431,12 @@
 def shards(weights, keep_mask, test_matrix):
     place = position()
 
-    two, three, test_matrix = sketch_parts((2, 3), 2, place, keep_mask, weights, test_matrix, fetch=True)
-    two, three = swap(two, square(True, 2)), swap(three, square(True, 3))
-    one = [swap(piece, square(True, 1)) for piece in sketch_parts((1,), 2, place, keep_mask, weights, test_matrix)]
-    part = sketch_parts((0,), 1, place, keep_mask, weights, test_matrix)[0] + three + two + jnp.concatenate(one)
-    part = part + swap(part, square(False, 2))
-    sent = swap(part, square(False, 1))
+    one, two, three = sketch_parts((1, 2, 3), place, keep_mask, weights, test_matrix)
+    three, two, one = swap(three, square(True, 3)), swap(two, square(True, 2)), swap(one, square(True, 1))
+    part = sketch_parts((0,), place, keep_mask, weights, test_matrix)[0] + three + two + one
+    one, two, three = (swap(part, square(False, k)) for k in (1, 2, 3))
     send_tile = stage(False, place, keep_mask, weights, part)
-    part, send_tile = lax.optimization_barrier((part + sent, send_tile))
+    part, send_tile = lax.optimization_barrier(((part + two) + (one + three), send_tile))
     sent = swap(part, ACROSS)
     stay_tile = stage(True, place, keep_mask, weights, part)
     part, stay_tile = lax.optimization_barrier((part + sent, stay_tile))
@@ -451,8 +444,8 @@
     mine = turn(part)
     one, two, three = (swap(mine, square(True, k)) for k in (1, 2, 3))
 
-    gram, sketch_a, send_a, stay_a = begin(mine, one, send_tile, stay_tile)
-    send, sketch_b = first_term(two, three, gram, send_tile, send_a)
+    gram, sketch_a, send_a, stay_a = begin(mine, three, send_tile, stay_tile)
+    send, sketch_b = first_term(one, two, gram, send_tile, send_a)
     stay = jnp.concatenate([far_term(0, sketch_b, stay_tile, stay_a), send[:, CHUNK:]], axis=1)
     total = stay + swap(send, CORES)
     far_a = swap(total, CHIPS)

time: 77.7 us -> 74.5 us (0.959)
  waiting for transfers between devices: 12.9 us -> 8.78 us
  Pallas kernels: 37.5 us -> 35.1 us
  starting transfers between devices: 25 us -> 27 us
  local copies, waits for them, and re-layouts: 0.71 us -> 2.11 us
    ppermute x18, waiting for transfers between devices: 12.9 us -> 8.78 us  [swap(): return lax.ppermute(value, AXES, perm)]
    pallas_call x3 -> x2, Pallas kernels: 13.5 us -> 11.1 us  [sketch_parts(): pl.pallas_call(lambda *refs: sketch_kernel(ks, *refs), in_specs=[SCALARS,...]
    ppermute x18, starting transfers between devices: 25 us -> 27 us  [swap(): return lax.ppermute(value, AXES, perm)]
    unnamed x4 -> x6, local copies, waits for them, and re-layouts: 0.7 us -> 2.11 us
  transfers between devices with their start and end apart: 18 -> 18, of which waited for: 9 -> 8; matrix products, arithmetic and copies ran while one was open for 0% -> 0% of each run, Pallas kernels for 38% -> 34%
where the time goes in v4:
time: 74.5 us; the launch traced here: 74.3 us
  Pallas kernels  35.1 us (47%)
  starting transfers between devices  27 us (36%)
  waiting for transfers between devices  8.78 us (12%)
  local copies, waits for them, and re-layouts  2.11 us (3%)
  between operations  1.06 us (1%)
    ppermute x18, starting transfers between devices, swap(): return lax.ppermute(value, AXES, perm)  27 us
    pallas_call x2, Pallas kernels, sketch_parts(): pl.pallas_call(lambda *refs: sketch_kernel(ks, *refs), in_specs=[SCALARS,...  11.1 us
    ppermute x18, waiting for transfers between devices, swap(): return lax.ppermute(value, AXES, perm)  8.78 us
    pallas_call x2, Pallas kernels, stage(): pl.pallas_call(lambda *refs: stage_kernel(own, *refs), in_specs=[SCALARS,...  6.25 us
    pallas_call x1, Pallas kernels, near_terms(): pl.pallas_call(near_kernel, in_specs=[SCALARS, FAR, WHOLE, WHOLE, FAR], o...  5.98 us
    pallas_call x1, Pallas kernels, inverse_factor(): pl.pallas_call(inverse_factor_kernel, in_specs=[WHOLE] * 2, out_specs=WHO...  4.34 us
    unnamed x6, local copies, waits for them, and re-layouts  2.11 us
    pallas_call x1, Pallas kernels, begin(): pl.pallas_call(begin_kernel, in_specs=[WHOLE] * 4, out_specs=[WHOLE] * 4,...  1.82 us
  transfers between devices with their start and end apart: 18, of which 8 were waited for; matrix products, arithmetic and copies ran while one was open for 0% of the time, Pallas kernels for 34%

profile of v4, /device:TPU:1, one launch (start us, length us, event | category | flops | bytes accessed | tf_op | source)
XLA Modules:
  0.0 74.3 jit_solution(2795084182707058321)
XLA Ops:
  0.8 1.4 %copy-done = bf16[6144,128]{1,0:T(8,128)(2,1)S(1)} copy-done((bf16[6144,128]{1,0:T(8,128)(2,1)S(1)}, bf16[6144,128]{1,0:T(8,128)(2,1)}, u32[]{:S(2)}) %copy-start) | copy-done | bytes 1572888
  2.9 7.3 %sketch.3 = (f32[384,128]{1,0:T(8,128)S(1)}, f32[384,128]{1,0:T(8,128)S(1)}, f32[384,128]{1,0:T(8,128)S(1)}) custom-call(s32[3]{0:T(128)S(1)} %pad_add_fusion.refs_0_.place, s32[12,48]{1,0:T(8,128)S(1)} %copy-done.1, bf16[1536,6144]{1,0:T(8,128)(2,1)} %weights.1, bf16[6144,128]{1,0:T(8,128)(2,1)S(1)} %copy-done), custom_call_target="tpu_custom_call" | custom-call | flops 1000000 | bytes 100000 | tf_op jit(solution)/shard_map/sketch/pallas_call | solution.py:137
  10.2 7.1 %collective-permute-start = (f32[384,128]{1,0:T(8,128)S(1)}, f32[384,128]{1,0:T(8,128)S(1)}, u32[]{:S(2)}, u32[]{:S(2)}) collective-permute-start(f32[384,128]{1,0:T(8,128)S(1)} %get-tuple-element.25), channel_id=1, source_target_pairs={{0,36},{1,109},{2,38},{3,111},{4,32},{5,105},{6,34},{7,107},{8,44}... | collective-permute-start | bytes 589832 | tf_op jit(solution)/shard_map/ppermute | solution.py:61
  17.7 3.8 %sketch.2 = f32[384,128]{1,0:T(8,128)S(1)} custom-call(s32[3]{0:T(128)S(1)} %pad_add_fusion.refs_0_.place, s32[12,48]{1,0:T(8,128)S(1)} %copy-done.1, bf16[1536,6144]{1,0:T(8,128)(2,1)} %weights.1, bf16[6144,128]{1,0:T(8,128)(2,1)S(1)} %copy-done), custom_call_target="tpu_custom_call" | custom-call | flops 1000000 | bytes 100000 | tf_op jit(solution)/shard_map/sketch/pallas_call | solution.py:137
  21.5 1.5 %collective-permute-done.1 = f32[384,128]{1,0:T(8,128)S(1)} collective-permute-done((f32[384,128]{1,0:T(8,128)S(1)}, f32[384,128]{1,0:T(8,128)S(1)}, u32[]{:S(2)}, u32[]{:S(2)}) %collective-permute-start.1) | collective-permute-done | bytes 196640 | tf_op jit(solution)/shard_map/ppermute | solution.py:61
  23.1 1.2 %collective-permute-start.4 = (f32[384,128]{1,0:T(8,128)S(1)}, f32[384,128]{1,0:T(8,128)S(1)}, u32[]{:S(2)}, u32[]{:S(2)}) collective-permute-start(f32[384,128]{1,0:T(8,128)S(1)} %add_add_fusion.1.refs_3_), channel_id=1, source_target_pairs={{0,96},{1,33},{2,98},{3,35},{4,100},{5,37},{6,102},{7,39},{8,104},... | collective-permute-start | bytes 589832 | tf_op jit(solution)/shard_map/ppermute | solution.py:61
  24.3 1.4 %collective-permute-start.3 = (f32[384,128]{1,0:T(8,128)S(1)}, f32[384,128]{1,0:T(8,128)S(1)}, u32[]{:S(2)}, u32[]{:S(2)}) collective-permute-start(f32[384,128]{1,0:T(8,128)S(1)} %add_add_fusion.1.refs_3_), channel_id=1, source_target_pairs={{0,12},{1,5},{2,14},{3,7},{4,8},{5,1},{6,10},{7,3},{8,4},{9,13},{1... | collective-permute-start | bytes 589832 | tf_op jit(solution)/shard_map/ppermute | solution.py:61
  25.8 3.1 %stage.2.send_tile.tile.refs_1_ = bf16[1536,1536]{1,0:T(8,128)(2,1)S(1)} custom-call(s32[3]{0:T(128)S(1)} %pad_add_fusion.refs_0_.place, s32[12,48]{1,0:T(8,128)S(1)} %copy-done.2, bf16[1536,6144]{1,0:T(8,128)(2,1)} %weights.1, f32[384,128]{1,0:T(8,128)S(1)} %add_add_fusion.1.refs_3_), custom_call_target="tpu_custom_call" | custom-call | flops 1000000 | bytes 100000 | tf_op jit(solution)/shard_map/stage/pallas_call | solution.py:248
  28.9 1.2 %collective-permute-done.4 = f32[384,128]{1,0:T(8,128)S(1)} collective-permute-done((f32[384,128]{1,0:T(8,128)S(1)}, f32[384,128]{1,0:T(8,128)S(1)}, u32[]{:S(2)}, u32[]{:S(2)}) %collective-permute-start.4) | collective-permute-done | bytes 196640 | tf_op jit(solution)/shard_map/ppermute | solution.py:61
  30.2 2.8 %collective-permute-start.6 = (f32[384,128]{1,0:T(8,128)S(1)}, f32[384,128]{1,0:T(8,128)S(1)}, u32[]{:S(2)}, u32[]{:S(2)}) collective-permute-start(f32[384,128]{1,0:T(8,128)S(1)} %add_add_fusion.refs_3_), channel_id=1, source_target_pairs={{0,16},{1,17},{2,18},{3,19},{4,20},{5,21},{6,22},{7,23},{8,24},{9,... | collective-permute-start | bytes 589832 | tf_op jit(solution)/shard_map/ppermute | solution.py:61
  33.0 3.1 %stage.3.stay_tile.refs_1_ = bf16[1536,1536]{1,0:T(8,128)(2,1)S(1)} custom-call(s32[3]{0:T(128)S(1)} %pad_add_fusion.refs_0_.place, s32[12,48]{1,0:T(8,128)S(1)} %copy-done.2, bf16[1536,6144]{1,0:T(8,128)(2,1)} %weights.1, f32[384,128]{1,0:T(8,128)S(1)} %add_add_fusion.refs_3_), custom_call_target="tpu_custom_call" | custom-call | flops 1000000 | bytes 100000 | tf_op jit(solution)/shard_map/stage/pallas_call | solution.py:248
  36.5 4.3 %collective-permute-start.9 = (f32[128,384]{1,0:T(8,128)S(1)}, f32[128,384]{1,0:T(8,128)S(1)}, u32[]{:S(2)}, u32[]{:S(2)}) collective-permute-start(f32[128,384]{1,0:T(8,128)S(1)} %turn.1.mine.refs_0_), channel_id=1, source_target_pairs={{0,36},{1,109},{2,38},{3,111},{4,32},{5,105},{6,34},{7,107},{8,44}... | collective-permute-start | bytes 589832 | tf_op jit(solution)/shard_map/ppermute | solution.py:61
  41.6 2.8 %collective-permute-done.9.three.refs_3_ = f32[128,384]{1,0:T(8,128)S(1)} collective-permute-done((f32[128,384]{1,0:T(8,128)S(1)}, f32[128,384]{1,0:T(8,128)S(1)}, u32[]{:S(2)}, u32[]{:S(2)}) %collective-permute-start.9) | collective-permute-done | bytes 196640 | tf_op jit(solution)/shard_map/ppermute | solution.py:61
  44.4 1.8 %begin.1 = (f32[128,128]{1,0:T(8,128)S(1)}, bf16[256,768]{1,0:T(8,128)(2,1)S(1)}, f32[128,1536]{1,0:T(8,128)S(1)}, f32[128,1536]{1,0:T(8,128)S(1)}) custom-call(f32[128,384]{1,0:T(8,128)S(1)} %turn.1.mine.refs_0_, f32[128,384]{1,0:T(8,128)S(1)} %collective-permute-done.9.three.refs_3_, bf16[1536,1536]{1,0:T(8,128)(2,1)S(1)} %stage.2.send_tile.tile.refs_1_, ...), custom_call_target="tpu_custom_call" | custom-call | flops 1000000 | bytes 100000 | tf_op jit(solution)/shard_map/begin/pallas_call | solution.py:285
  46.6 0.9 %first.1 = (f32[128,896]{1,0:T(8,128)S(1)}, bf16[256,768]{1,0:T(8,128)(2,1)S(1)}) custom-call(f32[128,384]{1,0:T(8,128)S(1)} %collective-permute-done.7.one.refs_1_, f32[128,384]{1,0:T(8,128)S(1)} %collective-permute-done.8.two.refs_2_, f32[128,128]{1,0:T(8,128)S(1)} %get-tuple-element.32.gram, bf16[1536,1536]{1,0:T(8,128)(2,1)S(1)} %stage.2.send_tile.tile.refs_1_, ...), custom_call_target="tpu_custom_call" | custom-call | flops 1000000 | bytes 100000 | tf_op jit(solution)/shard_map/first/pallas_call | solution.py:308
  47.6 3.6 %collective-permute-start.10 = (f32[128,896]{1,0:T(8,128)S(1)}, f32[128,896]{1,0:T(8,128)S(1)}, u32[]{:S(2)}, u32[]{:S(2)}) collective-permute-start(f32[128,896]{1,0:T(8,128)S(1)} %get-tuple-element.36), channel_id=1, source_target_pairs={{0,1},{1,0},{2,3},{3,2},{4,5},{5,4},{6,7},{7,6},{8,9},{9,8},{10,11... | collective-permute-start | bytes 1376264 | tf_op jit(solution)/shard_map/ppermute | solution.py:61
  52.7 1.3 %collective-permute-start.11 = (f32[128,896]{1,0:T(8,128)S(1)}, f32[128,896]{1,0:T(8,128)S(1)}, u32[]{:S(2)}, u32[]{:S(2)}) collective-permute-start(f32[128,896]{1,0:T(8,128)S(1)} %maximum_add_fusion.mine), channel_id=1, source_target_pairs={{0,2},{1,3},{2,0},{3,1},{4,6},{5,7},{6,4},{7,5},{8,10},{9,11},{10,... | collective-permute-start | bytes 1376264 | tf_op jit(solution)/shard_map/ppermute | solution.py:61
  54.8 6.0 %near.1 = (f32[128,384]{1,0:T(8,128)S(1)}, f32[128,384]{1,0:T(8,128)S(1)}, f32[128,384]{1,0:T(8,128)S(1)}, f32[128,384]{1,0:T(8,128)S(1)}, f32[128,384]{1,0:T(8,...) custom-call(s32[3]{0:T(128)S(1)} %pad_add_fusion.refs_0_.place, ...), custom_call_target="tpu_custom_call" | custom-call | flops 1000000 | bytes 100000 | tf_op jit(solution)/shard_map/near/pallas_call | solution.py:358
  60.8 1.0 %collective-permute-start.14 = (f32[128,384]{1,0:T(8,128)S(1)}, f32[128,384]{1,0:T(8,128)S(1)}, u32[]{:S(2)}, u32[]{:S(2)}) collective-permute-start(f32[128,384]{1,0:T(8,128)S(1)} %get-tuple-element.44), channel_id=1, source_target_pairs={{0,1},{1,0},{2,3},{3,2},{4,5},{5,4},{6,7},{7,6},{8,9},{9,8},{10,11... | collective-permute-start | bytes 589832 | tf_op jit(solution)/shard_map/ppermute | solution.py:61
  62.4 2.1 %collective-permute-done.11.theirs.far_a = f32[128,896]{1,0:T(8,128)S(1)} collective-permute-done((f32[128,896]{1,0:T(8,128)S(1)}, f32[128,896]{1,0:T(8,128)S(1)}, u32[]{:S(2)}, u32[]{:S(2)}) %collective-permute-start.11) | collective-permute-done | bytes 458784 | tf_op jit(solution)/shard_map/ppermute | solution.py:61
  64.5 2.0 %collective-permute-start.17 = (f32[128,384]{1,0:T(8,128)S(1)}, f32[128,384]{1,0:T(8,128)S(1)}, u32[]{:S(2)}, u32[]{:S(2)}) collective-permute-start(f32[128,384]{1,0:T(8,128)S(1)} %get-tuple-element.47), channel_id=1, source_target_pairs={{0,1},{1,0},{2,3},{3,2},{4,5},{5,4},{6,7},{7,6},{8,9},{9,8},{10,11... | collective-permute-start | bytes 589832 | tf_op jit(solution)/shard_map/ppermute | solution.py:61
  66.5 4.3 %inverse_factor.1.inverse = f32[128,128]{1,0:T(8,128)S(1)} custom-call(f32[128,896]{1,0:T(8,128)S(1)} %maximum_add_fusion.mine, f32[128,896]{1,0:T(8,128)S(1)} %collective-permute-done.11.theirs.far_a), custom_call_target="tpu_custom_call" | custom-call | flops 1000000 | bytes 100000 | tf_op jit(solution)/shard_map/inverse_factor/pallas_call | solution.py:203
  70.8 1.8 %basis.1 = f32[1536,128]{1,0:T(8,128)} custom-call(s32[3]{0:T(128)S(1)} %pad_add_fusion.refs_0_.place, f32[128,128]{1,0:T(8,128)S(1)} %inverse_factor.1.inverse, f32[128,384]{1,0:T(8,128)S(1)} %turn.1.mine.refs_0_, f32[128,384]{1,0:T(8,128)S(1)} %collective-permute-done.7.one.refs_1_, f32[128,384]{1,0:T(8,128)S(1)} %collective-permute-done.8.two.refs_2_, ...), custom_call_target="tpu_custom_call" | custom-call | flops 1000000 | bytes 100000 | tf_op jit(solution)/shard_map/basis/pallas_call | solution.py:413
  72.9 1.3 %finish.1 = f32[1536,128]{1,0:T(8,128)} custom-call(f32[128,128]{1,0:T(8,128)S(1)} %inverse_factor.1.inverse, f32[128,896]{1,0:T(8,128)S(1)} %collective-permute-done.11.theirs.far_a, f32[128,768]{1,0:T(8,128)S(1)} %collective-permute-done.13.far_b, f32[128,384]{1,0:T(8,128)S(1)} %get-tuple-element.40.refs_0_, f32[128,384]{1,0:T(8,128)S(1)} %get-tuple-element.41.refs_1_, ...), custom_call_target="tpu_custom_call" | custom-call | flops 1000000 | bytes 100000 | tf_op jit(solution)/shard_map/finish/pallas_call | solution.py:428
  (39 shorter events, 6.0 us)
Async XLA Ops:
  0.8 1.4 %copy-start = (bf16[6144,128]{1,0:T(8,128)(2,1)S(1)}, bf16[6144,128]{1,0:T(8,128)(2,1)}, u32[]{:S(2)}) copy-start(bf16[6144,128]{1,0:T(8,128)(2,1)} %refs_3_.3) | copy-start | bytes 4718596
  2.2 0.7 copy-start.1
  10.2 11.3 %collective-permute-start = (f32[384,128]{1,0:T(8,128)S(1)}, f32[384,128]{1,0:T(8,128)S(1)}, u32[]{:S(2)}, u32[]{:S(2)}) collective-permute-start(f32[384,128]{1,0:T(8,128)S(1)} %get-tuple-element.25), channel_id=1, source_target_pairs={{0,36},{1,109},{2,38},{3,111},{4,32},{5,105},{6,34},{7,107},{8,44}... | collective-permute-start | bytes 589832 | tf_op jit(solution)/shard_map/ppermute | solution.py:61
  17.3 5.7 %collective-permute-start.1 = (f32[384,128]{1,0:T(8,128)S(1)}, f32[384,128]{1,0:T(8,128)S(1)}, u32[]{:S(2)}, u32[]{:S(2)}) collective-permute-start(f32[384,128]{1,0:T(8,128)S(1)} %get-tuple-element.26), channel_id=1, source_target_pairs={{0,4},{1,13},{2,6},{3,15},{4,0},{5,9},{6,2},{7,11},{8,12},{9,5},{1... | collective-permute-start | bytes 589832 | tf_op jit(solution)/shard_map/ppermute | solution.py:61
  17.3 8.5 %copy-start.2 = (s32[12,48]{1,0:T(8,128)S(1)}, s32[12,48]{1,0:T(8,128)}, u32[]{:S(2)}) copy-start(s32[12,48]{1,0:T(8,128)} %keep_mask.1) | copy-start | bytes 6916
  17.3 5.7 %collective-permute-start.2 = (f32[384,128]{1,0:T(8,128)S(1)}, f32[384,128]{1,0:T(8,128)S(1)}, u32[]{:S(2)}, u32[]{:S(2)}) collective-permute-start(f32[384,128]{1,0:T(8,128)S(1)} %get-tuple-element.27), channel_id=1, source_target_pairs={{0,32},{1,97},{2,34},{3,99},{4,36},{5,101},{6,38},{7,103},{8,40},{... | collective-permute-start | bytes 589832 | tf_op jit(solution)/shard_map/ppermute | solution.py:61
  23.1 5.9 %collective-permute-start.5 = (f32[384,128]{1,0:T(8,128)S(1)}, f32[384,128]{1,0:T(8,128)S(1)}, u32[]{:S(2)}, u32[]{:S(2)}) collective-permute-start(f32[384,128]{1,0:T(8,128)S(1)} %add_add_fusion.1.refs_3_), channel_id=1, source_target_pairs={{0,108},{1,37},{2,110},{3,39},{4,104},{5,33},{6,106},{7,35},{8,100... | collective-permute-start | bytes 589832 | tf_op jit(solution)/shard_map/ppermute | solution.py:61
  23.1 7.0 %collective-permute-start.4 = (f32[384,128]{1,0:T(8,128)S(1)}, f32[384,128]{1,0:T(8,128)S(1)}, u32[]{:S(2)}, u32[]{:S(2)}) collective-permute-start(f32[384,128]{1,0:T(8,128)S(1)} %add_add_fusion.1.refs_3_), channel_id=1, source_target_pairs={{0,96},{1,33},{2,98},{3,35},{4,100},{5,37},{6,102},{7,39},{8,104},... | collective-permute-start | bytes 589832 | tf_op jit(solution)/shard_map/ppermute | solution.py:61
  24.3 5.8 %collective-permute-start.3 = (f32[384,128]{1,0:T(8,128)S(1)}, f32[384,128]{1,0:T(8,128)S(1)}, u32[]{:S(2)}, u32[]{:S(2)}) collective-permute-start(f32[384,128]{1,0:T(8,128)S(1)} %add_add_fusion.1.refs_3_), channel_id=1, source_target_pairs={{0,12},{1,5},{2,14},{3,7},{4,8},{5,1},{6,10},{7,3},{8,4},{9,13},{1... | collective-permute-start | bytes 589832 | tf_op jit(solution)/shard_map/ppermute | solution.py:61
  30.2 6.1 %collective-permute-start.6 = (f32[384,128]{1,0:T(8,128)S(1)}, f32[384,128]{1,0:T(8,128)S(1)}, u32[]{:S(2)}, u32[]{:S(2)}) collective-permute-start(f32[384,128]{1,0:T(8,128)S(1)} %add_add_fusion.refs_3_), channel_id=1, source_target_pairs={{0,16},{1,17},{2,18},{3,19},{4,20},{5,21},{6,22},{7,23},{8,24},{9,... | collective-permute-start | bytes 589832 | tf_op jit(solution)/shard_map/ppermute | solution.py:61
  36.5 7.9 %collective-permute-start.9 = (f32[128,384]{1,0:T(8,128)S(1)}, f32[128,384]{1,0:T(8,128)S(1)}, u32[]{:S(2)}, u32[]{:S(2)}) collective-permute-start(f32[128,384]{1,0:T(8,128)S(1)} %turn.1.mine.refs_0_), channel_id=1, source_target_pairs={{0,36},{1,109},{2,38},{3,111},{4,32},{5,105},{6,34},{7,107},{8,44}... | collective-permute-start | bytes 589832 | tf_op jit(solution)/shard_map/ppermute | solution.py:61
  40.8 5.9 %collective-permute-start.8 = (f32[128,384]{1,0:T(8,128)S(1)}, f32[128,384]{1,0:T(8,128)S(1)}, u32[]{:S(2)}, u32[]{:S(2)}) collective-permute-start(f32[128,384]{1,0:T(8,128)S(1)} %turn.1.mine.refs_0_), channel_id=1, source_target_pairs={{0,4},{1,13},{2,6},{3,15},{4,0},{5,9},{6,2},{7,11},{8,12},{9,5},{1... | collective-permute-start | bytes 589832 | tf_op jit(solution)/shard_map/ppermute | solution.py:61
  40.8 5.9 %collective-permute-start.7 = (f32[128,384]{1,0:T(8,128)S(1)}, f32[128,384]{1,0:T(8,128)S(1)}, u32[]{:S(2)}, u32[]{:S(2)}) collective-permute-start(f32[128,384]{1,0:T(8,128)S(1)} %turn.1.mine.refs_0_), channel_id=1, source_target_pairs={{0,32},{1,97},{2,34},{3,99},{4,36},{5,101},{6,38},{7,103},{8,40},{... | collective-permute-start | bytes 589832 | tf_op jit(solution)/shard_map/ppermute | solution.py:61
  47.6 5.0 %collective-permute-start.10 = (f32[128,896]{1,0:T(8,128)S(1)}, f32[128,896]{1,0:T(8,128)S(1)}, u32[]{:S(2)}, u32[]{:S(2)}) collective-permute-start(f32[128,896]{1,0:T(8,128)S(1)} %get-tuple-element.36), channel_id=1, source_target_pairs={{0,1},{1,0},{2,3},{3,2},{4,5},{5,4},{6,7},{7,6},{8,9},{9,8},{10,11... | collective-permute-start | bytes 1376264 | tf_op jit(solution)/shard_map/ppermute | solution.py:61
  51.7 2.8 %collective-permute-start.12 = (f32[128,768]{1,0:T(8,128)S(1)}, f32[128,768]{1,0:T(8,128)S(1)}, u32[]{:S(2)}, u32[]{:S(2)}) collective-permute-start(f32[128,768]{1,0:T(8,128)S(1)} %far.5), channel_id=1, source_target_pairs={{0,1},{1,0},{2,3},{3,2},{4,5},{5,4},{6,7},{7,6},{8,9},{9,8},{10,11... | collective-permute-start | bytes 1179656 | tf_op jit(solution)/shard_map/ppermute | solution.py:61
  52.7 11.8 %collective-permute-start.11 = (f32[128,896]{1,0:T(8,128)S(1)}, f32[128,896]{1,0:T(8,128)S(1)}, u32[]{:S(2)}, u32[]{:S(2)}) collective-permute-start(f32[128,896]{1,0:T(8,128)S(1)} %maximum_add_fusion.mine), channel_id=1, source_target_pairs={{0,2},{1,3},{2,0},{3,1},{4,6},{5,7},{6,4},{7,5},{8,10},{9,11},{10,... | collective-permute-start | bytes 1376264 | tf_op jit(solution)/shard_map/ppermute | solution.py:61
  54.5 18.4 %collective-permute-start.13 = (f32[128,768]{1,0:T(8,128)S(1)}, f32[128,768]{1,0:T(8,128)S(1)}, u32[]{:S(2)}, u32[]{:S(2)}) collective-permute-start(f32[128,768]{1,0:T(8,128)S(1)} %add.61), channel_id=1, source_target_pairs={{0,2},{1,3},{2,0},{3,1},{4,6},{5,7},{6,4},{7,5},{8,10},{9,11},{10,... | collective-permute-start | bytes 1179656 | tf_op jit(solution)/shard_map/ppermute | solution.py:61
  60.8 11.8 %collective-permute-start.14 = (f32[128,384]{1,0:T(8,128)S(1)}, f32[128,384]{1,0:T(8,128)S(1)}, u32[]{:S(2)}, u32[]{:S(2)}) collective-permute-start(f32[128,384]{1,0:T(8,128)S(1)} %get-tuple-element.44), channel_id=1, source_target_pairs={{0,1},{1,0},{2,3},{3,2},{4,5},{5,4},{6,7},{7,6},{8,9},{9,8},{10,11... | collective-permute-start | bytes 589832 | tf_op jit(solution)/shard_map/ppermute | solution.py:61
  61.8 10.8 %collective-permute-start.15 = (f32[128,384]{1,0:T(8,128)S(1)}, f32[128,384]{1,0:T(8,128)S(1)}, u32[]{:S(2)}, u32[]{:S(2)}) collective-permute-start(f32[128,384]{1,0:T(8,128)S(1)} %get-tuple-element.45), channel_id=1, source_target_pairs={{0,1},{1,0},{2,3},{3,2},{4,5},{5,4},{6,7},{7,6},{8,9},{9,8},{10,11... | collective-permute-start | bytes 589832 | tf_op jit(solution)/shard_map/ppermute | solution.py:61
  61.9 10.7 %collective-permute-start.16 = (f32[128,384]{1,0:T(8,128)S(1)}, f32[128,384]{1,0:T(8,128)S(1)}, u32[]{:S(2)}, u32[]{:S(2)}) collective-permute-start(f32[128,384]{1,0:T(8,128)S(1)} %get-tuple-element.46), channel_id=1, source_target_pairs={{0,1},{1,0},{2,3},{3,2},{4,5},{5,4},{6,7},{7,6},{8,9},{9,8},{10,11... | collective-permute-start | bytes 589832 | tf_op jit(solution)/shard_map/ppermute | solution.py:61
  64.5 8.2 %collective-permute-start.17 = (f32[128,384]{1,0:T(8,128)S(1)}, f32[128,384]{1,0:T(8,128)S(1)}, u32[]{:S(2)}, u32[]{:S(2)}) collective-permute-start(f32[128,384]{1,0:T(8,128)S(1)} %get-tuple-element.47), channel_id=1, source_target_pairs={{0,1},{1,0},{2,3},{3,2},{4,5},{5,4},{6,7},{7,6},{8,9},{9,8},{10,11... | collective-permute-start | bytes 589832 | tf_op jit(solution)/shard_map/ppermute | solution.py:61

commit v5 on v4

--- a/solution.py
+++ b/solution.py
@@ -15,7 +15,7 @@
 WIDTH = 6144
 QUARTER = ROWS // 4
 PANEL = 1536
-CHUNK = WIDTH // 8
+CHUNK = 896
 ORDER = (0, 3, 1, 2)
 MIB = 2**20
 AXES = ("shard", "rep")
@@ -54,6 +54,7 @@
 
 ACROSS = pairs(lambda z, x_hi, y, x_lo, core: (z, 1 - x_hi, y, x_lo, core))
 CORES = pairs(lambda z, x_hi, y, x_lo, core: (z, x_hi, y, x_lo, 1 - core))
+OTHERS = pairs(lambda z, x_hi, y, x_lo, core: (z, 1 - x_hi, y, 1 - x_lo, core))
 CHIPS = pairs(lambda z, x_hi, y, x_lo, core: (z, x_hi, y, 1 - x_lo, core))
 
 
@@ -171,8 +172,8 @@
     return square_of(first) + square_of(second)
 
 
-def inverse_factor_kernel(mine, theirs, out, step=4):
-    gram = mine[:, CHUNK:] + theirs[:, CHUNK:]
+def inverse_factor_kernel(mine, theirs, out, step=8):
+    gram = mine[...] + theirs[...]
     lanes = lax.broadcasted_iota(jnp.int32, (K, K), 1)
     rows = lax.broadcasted_iota(jnp.int32, (K, K), 0)
     unit = jnp.where(lanes == rows, 1.0, 0.0).astype(jnp.float32)
@@ -319,17 +320,16 @@
     )(one, two, gram, tile, before)
 
 
-def far_kernel(start, sketch, tile, before, out):
-    at = slice(start, start + CHUNK)
+def far_kernel(at, sketch, tile, before, out):
     out[...] = before[:, at] + project(sketch, tile[2 * QUARTER :, at])
 
 
-def far_term(start, sketch, tile, before):
-    return pl.pallas_call(
-        lambda *refs: far_kernel(start, *refs),
+def far_term(at, sketch, tile, before):
+    return pl.pallas_call(
+        lambda *refs: far_kernel(at, *refs),
         in_specs=[WHOLE] * 3,
         out_specs=WHOLE,
-        out_shape=jax.ShapeDtypeStruct((K, CHUNK), jnp.float32),
+        out_shape=jax.ShapeDtypeStruct((K, at.stop - at.start), jnp.float32),
         compiler_params=pltpu.CompilerParams(vmem_limit_bytes=16 * MIB),
         cost_estimate=SMALL,
         name="far",
@@ -417,9 +417,10 @@
     terms, out, held, sems = refs[:8], *refs[8:]
 
     def columns(t):
-        far = (far_a, far_b)[t * QUARTER // CHUNK]
-        start = t * QUARTER % CHUNK
-        return terms[t][...] + terms[t + 4][...] + far[:, start : start + QUARTER], t
+        start, stop = t * QUARTER, (t + 1) * QUARTER
+        far = [far_a[:, start : min(stop, CHUNK)]] if start < CHUNK else []
+        far += [far_b[:, max(start, CHUNK) - CHUNK : stop - CHUNK]] if stop > CHUNK else []
+        return terms[t][...] + terms[t + 4][...] + (far[0] if len(far) == 1 else jnp.concatenate(far, axis=1)), t
 
     write_turned(inverse[...], columns, 1.0, out, held, sems)
 
@@ -446,16 +447,18 @@
 
     gram, sketch_a, send_a, stay_a = begin(mine, three, send_tile, stay_tile)
     send, sketch_b = first_term(one, two, gram, send_tile, send_a)
-    stay = jnp.concatenate([far_term(0, sketch_b, stay_tile, stay_a), send[:, CHUNK:]], axis=1)
-    total = stay + swap(send, CORES)
+    early, late = slice(0, CHUNK), slice(CHUNK, WIDTH // 4)
+    sent = swap(send, CORES)
+    total = far_term(early, sketch_b, stay_tile, stay_a) + sent[:, :CHUNK]
+    gram = send[:, CHUNK:] + sent[:, CHUNK:]
     far_a = swap(total, CHIPS)
-    send = far_term(CHUNK, sketch_b, send_tile, send_a)
-    rest = far_term(CHUNK, sketch_b, stay_tile, stay_a) + swap(send, CORES)
-    rest, sketch_b = lax.optimization_barrier((rest, sketch_b))
+    far_gram = swap(gram, OTHERS)
+    rest = far_term(late, sketch_b, stay_tile, stay_a) + swap(far_term(late, sketch_b, send_tile, send_a), CORES)
+    rest, gram, sketch_b = lax.optimization_barrier((rest, gram, sketch_b))
     far_b = swap(rest, CHIPS)
     terms = near_terms(place, keep_mask, sketch_a, sketch_b, weights)
     core = [swap(term, CORES) for term in terms[:4]]
-    inverse = inverse_factor(total, far_a)
+    inverse = inverse_factor(gram, far_gram)
     basis = range_basis_of(place, inverse, (mine, one, two, three))
     return basis, finish(inverse, (far_a, far_b), terms[4:], core)
 

time: 74.5 us -> 74.5 us (level)
  starting transfers between devices: 27 us -> 28.6 us
  waiting for transfers between devices: 8.78 us -> 7.85 us
    ppermute x18 -> x19, starting transfers between devices: 27 us -> 28.6 us  [swap(): return lax.ppermute(value, AXES, perm)]
    ppermute x18 -> x19, waiting for transfers between devices: 8.78 us -> 7.85 us  [swap(): return lax.ppermute(value, AXES, perm)]
    pallas_call x1, Pallas kernels: 4.34 us -> 3.5 us  [inverse_factor(): pl.pallas_call(inverse_factor_kernel, in_specs=[WHOLE] * 2, out_specs=WHO...]
  transfers between devices with their start and end apart: 18 -> 19, of which waited for: 8 -> 7; matrix products, arithmetic and copies ran while one was open for 0% -> 0% of each run, Pallas kernels for 34% -> 33%
where the time goes in v5:
time: 74.5 us; the launch traced here: 74.3 us
  Pallas kernels  34.4 us (46%)
  starting transfers between devices  28.6 us (38%)
  waiting for transfers between devices  7.85 us (11%)
  local copies, waits for them, and re-layouts  2.11 us (3%)
  between operations  1.06 us (1%)
    ppermute x19, starting transfers between devices, swap(): return lax.ppermute(value, AXES, perm)  28.6 us
    pallas_call x2, Pallas kernels, sketch_parts(): pl.pallas_call(lambda *refs: sketch_kernel(ks, *refs), in_specs=[SCALARS,...  11.1 us
    ppermute x19, waiting for transfers between devices, swap(): return lax.ppermute(value, AXES, perm)  7.85 us
    pallas_call x2, Pallas kernels, stage(): pl.pallas_call(lambda *refs: stage_kernel(own, *refs), in_specs=[SCALARS,...  6.25 us
    pallas_call x1, Pallas kernels, near_terms(): pl.pallas_call(near_kernel, in_specs=[SCALARS, FAR, WHOLE, WHOLE, FAR], o...  5.99 us
    pallas_call x1, Pallas kernels, inverse_factor(): pl.pallas_call(inverse_factor_kernel, in_specs=[WHOLE] * 2, out_specs=WHO...  3.5 us
    unnamed x6, local copies, waits for them, and re-layouts  2.11 us
    pallas_call x1, Pallas kernels, begin(): pl.pallas_call(begin_kernel, in_specs=[WHOLE] * 4, out_specs=[WHOLE] * 4,...  1.82 us
  transfers between devices with their start and end apart: 19, of which 7 were waited for; matrix products, arithmetic and copies ran while one was open for 0% of the time, Pallas kernels for 33%

profile of v5, /device:TPU:1, one launch (start us, length us, event | category | flops | bytes accessed | tf_op | source)
XLA Modules:
  0.0 74.3 jit_solution(15591224419425937417)
XLA Ops:
  0.8 1.4 %copy-done = bf16[6144,128]{1,0:T(8,128)(2,1)S(1)} copy-done((bf16[6144,128]{1,0:T(8,128)(2,1)S(1)}, bf16[6144,128]{1,0:T(8,128)(2,1)}, u32[]{:S(2)}) %copy-start) | copy-done | bytes 1572888
  2.9 7.3 %sketch.3 = (f32[384,128]{1,0:T(8,128)S(1)}, f32[384,128]{1,0:T(8,128)S(1)}, f32[384,128]{1,0:T(8,128)S(1)}) custom-call(s32[3]{0:T(128)S(1)} %pad_add_fusion.refs_0_.place, s32[12,48]{1,0:T(8,128)S(1)} %copy-done.1, bf16[1536,6144]{1,0:T(8,128)(2,1)} %weights.1, bf16[6144,128]{1,0:T(8,128)(2,1)S(1)} %copy-done), custom_call_target="tpu_custom_call" | custom-call | flops 1000000 | bytes 100000 | tf_op jit(solution)/shard_map/sketch/pallas_call | solution.py:138
  10.2 7.1 %collective-permute-start = (f32[384,128]{1,0:T(8,128)S(1)}, f32[384,128]{1,0:T(8,128)S(1)}, u32[]{:S(2)}, u32[]{:S(2)}) collective-permute-start(f32[384,128]{1,0:T(8,128)S(1)} %get-tuple-element.26), channel_id=1, source_target_pairs={{0,36},{1,109},{2,38},{3,111},{4,32},{5,105},{6,34},{7,107},{8,44}... | collective-permute-start | bytes 589832 | tf_op jit(solution)/shard_map/ppermute | solution.py:62
  17.7 3.8 %sketch.2 = f32[384,128]{1,0:T(8,128)S(1)} custom-call(s32[3]{0:T(128)S(1)} %pad_add_fusion.refs_0_.place, s32[12,48]{1,0:T(8,128)S(1)} %copy-done.1, bf16[1536,6144]{1,0:T(8,128)(2,1)} %weights.1, bf16[6144,128]{1,0:T(8,128)(2,1)S(1)} %copy-done), custom_call_target="tpu_custom_call" | custom-call | flops 1000000 | bytes 100000 | tf_op jit(solution)/shard_map/sketch/pallas_call | solution.py:138
  21.5 1.5 %collective-permute-done.1 = f32[384,128]{1,0:T(8,128)S(1)} collective-permute-done((f32[384,128]{1,0:T(8,128)S(1)}, f32[384,128]{1,0:T(8,128)S(1)}, u32[]{:S(2)}, u32[]{:S(2)}) %collective-permute-start.1) | collective-permute-done | bytes 196640 | tf_op jit(solution)/shard_map/ppermute | solution.py:62
  23.1 1.2 %collective-permute-start.4 = (f32[384,128]{1,0:T(8,128)S(1)}, f32[384,128]{1,0:T(8,128)S(1)}, u32[]{:S(2)}, u32[]{:S(2)}) collective-permute-start(f32[384,128]{1,0:T(8,128)S(1)} %add_add_fusion.1.refs_3_), channel_id=1, source_target_pairs={{0,96},{1,33},{2,98},{3,35},{4,100},{5,37},{6,102},{7,39},{8,104},... | collective-permute-start | bytes 589832 | tf_op jit(solution)/shard_map/ppermute | solution.py:62
  24.3 1.4 %collective-permute-start.3 = (f32[384,128]{1,0:T(8,128)S(1)}, f32[384,128]{1,0:T(8,128)S(1)}, u32[]{:S(2)}, u32[]{:S(2)}) collective-permute-start(f32[384,128]{1,0:T(8,128)S(1)} %add_add_fusion.1.refs_3_), channel_id=1, source_target_pairs={{0,12},{1,5},{2,14},{3,7},{4,8},{5,1},{6,10},{7,3},{8,4},{9,13},{1... | collective-permute-start | bytes 589832 | tf_op jit(solution)/shard_map/ppermute | solution.py:62
  25.8 3.1 %stage.2.send_tile.tile.refs_1_ = bf16[1536,1536]{1,0:T(8,128)(2,1)S(1)} custom-call(s32[3]{0:T(128)S(1)} %pad_add_fusion.refs_0_.place, s32[12,48]{1,0:T(8,128)S(1)} %copy-done.2, bf16[1536,6144]{1,0:T(8,128)(2,1)} %weights.1, f32[384,128]{1,0:T(8,128)S(1)} %add_add_fusion.1.refs_3_), custom_call_target="tpu_custom_call" | custom-call | flops 1000000 | bytes 100000 | tf_op jit(solution)/shard_map/stage/pallas_call | solution.py:249
  28.9 1.2 %collective-permute-done.4 = f32[384,128]{1,0:T(8,128)S(1)} collective-permute-done((f32[384,128]{1,0:T(8,128)S(1)}, f32[384,128]{1,0:T(8,128)S(1)}, u32[]{:S(2)}, u32[]{:S(2)}) %collective-permute-start.4) | collective-permute-done | bytes 196640 | tf_op jit(solution)/shard_map/ppermute | solution.py:62
  30.2 2.8 %collective-permute-start.6 = (f32[384,128]{1,0:T(8,128)S(1)}, f32[384,128]{1,0:T(8,128)S(1)}, u32[]{:S(2)}, u32[]{:S(2)}) collective-permute-start(f32[384,128]{1,0:T(8,128)S(1)} %add_add_fusion.refs_3_), channel_id=1, source_target_pairs={{0,16},{1,17},{2,18},{3,19},{4,20},{5,21},{6,22},{7,23},{8,24},{9,... | collective-permute-start | bytes 589832 | tf_op jit(solution)/shard_map/ppermute | solution.py:62
  33.0 3.1 %stage.3.stay_tile.refs_1_ = bf16[1536,1536]{1,0:T(8,128)(2,1)S(1)} custom-call(s32[3]{0:T(128)S(1)} %pad_add_fusion.refs_0_.place, s32[12,48]{1,0:T(8,128)S(1)} %copy-done.2, bf16[1536,6144]{1,0:T(8,128)(2,1)} %weights.1, f32[384,128]{1,0:T(8,128)S(1)} %add_add_fusion.refs_3_), custom_call_target="tpu_custom_call" | custom-call | flops 1000000 | bytes 100000 | tf_op jit(solution)/shard_map/stage/pallas_call | solution.py:249
  36.5 4.3 %collective-permute-start.9 = (f32[128,384]{1,0:T(8,128)S(1)}, f32[128,384]{1,0:T(8,128)S(1)}, u32[]{:S(2)}, u32[]{:S(2)}) collective-permute-start(f32[128,384]{1,0:T(8,128)S(1)} %turn.1.mine.refs_0_), channel_id=1, source_target_pairs={{0,36},{1,109},{2,38},{3,111},{4,32},{5,105},{6,34},{7,107},{8,44}... | collective-permute-start | bytes 589832 | tf_op jit(solution)/shard_map/ppermute | solution.py:62
  41.6 2.8 %collective-permute-done.9.three.refs_3_ = f32[128,384]{1,0:T(8,128)S(1)} collective-permute-done((f32[128,384]{1,0:T(8,128)S(1)}, f32[128,384]{1,0:T(8,128)S(1)}, u32[]{:S(2)}, u32[]{:S(2)}) %collective-permute-start.9) | collective-permute-done | bytes 196640 | tf_op jit(solution)/shard_map/ppermute | solution.py:62
  44.4 1.8 %begin.1 = (f32[128,128]{1,0:T(8,128)S(1)}, bf16[256,768]{1,0:T(8,128)(2,1)S(1)}, f32[128,1536]{1,0:T(8,128)S(1)}, f32[128,1536]{1,0:T(8,128)S(1)}) custom-call(f32[128,384]{1,0:T(8,128)S(1)} %turn.1.mine.refs_0_, f32[128,384]{1,0:T(8,128)S(1)} %collective-permute-done.9.three.refs_3_, bf16[1536,1536]{1,0:T(8,128)(2,1)S(1)} %stage.2.send_tile.tile.refs_1_, ...), custom_call_target="tpu_custom_call" | custom-call | flops 1000000 | bytes 100000 | tf_op jit(solution)/shard_map/begin/pallas_call | solution.py:286
  46.6 1.0 %first.1 = (f32[128,1024]{1,0:T(8,128)S(1)}, bf16[256,768]{1,0:T(8,128)(2,1)S(1)}) custom-call(f32[128,384]{1,0:T(8,128)S(1)} %collective-permute-done.7.one.refs_1_, f32[128,384]{1,0:T(8,128)S(1)} %collective-permute-done.8.two.refs_2_, f32[128,128]{1,0:T(8,128)S(1)} %get-tuple-element.33.gram, bf16[1536,1536]{1,0:T(8,128)(2,1)S(1)} %stage.2.send_tile.tile.refs_1_, ...), custom_call_target="tpu_custom_call" | custom-call | flops 1000000 | bytes 100000 | tf_op jit(solution)/shard_map/first/pallas_call | solution.py:309
  47.7 3.6 %collective-permute-start.11 = (f32[128,1024]{1,0:T(8,128)S(1)}, f32[128,1024]{1,0:T(8,128)S(1)}, u32[]{:S(2)}, u32[]{:S(2)}) collective-permute-start(f32[128,1024]{1,0:T(8,128)S(1)} %get-tuple-element.37), channel_id=1, source_target_pairs={{0,1},{1,0},{2,3},{3,2},{4,5},{5,4},{6,7},{7,6},{8,9},{9,8},{10,11... | collective-permute-start | bytes 1572872 | tf_op jit(solution)/shard_map/ppermute | solution.py:62
  53.5 1.3 %collective-permute-start.13 = (f32[128,896]{1,0:T(8,128)S(1)}, f32[128,896]{1,0:T(8,128)S(1)}, u32[]{:S(2)}, u32[]{:S(2)}) collective-permute-start(f32[128,896]{1,0:T(8,128)S(1)} %slice_add_fusion), channel_id=1, source_target_pairs={{0,2},{1,3},{2,0},{3,1},{4,6},{5,7},{6,4},{7,5},{8,10},{9,11},{10,... | collective-permute-start | bytes 1376264 | tf_op jit(solution)/shard_map/ppermute | solution.py:62
  54.9 6.0 %near.1 = (f32[128,384]{1,0:T(8,128)S(1)}, f32[128,384]{1,0:T(8,128)S(1)}, f32[128,384]{1,0:T(8,128)S(1)}, f32[128,384]{1,0:T(8,128)S(1)}, f32[128,384]{1,0:T(8,...) custom-call(s32[3]{0:T(128)S(1)} %pad_add_fusion.refs_0_.place, ...), custom_call_target="tpu_custom_call" | custom-call | flops 1000000 | bytes 100000 | tf_op jit(solution)/shard_map/near/pallas_call | solution.py:358
  61.7 2.5 %collective-permute-start.12 = (f32[128,128]{1,0:T(8,128)S(1)}, f32[128,128]{1,0:T(8,128)S(1)}, u32[]{:S(2)}, u32[]{:S(2)}) collective-permute-start(f32[128,128]{1,0:T(8,128)S(1)} %slice_add_fusion.1.mine), channel_id=1, source_target_pairs={{0,18},{1,19},{2,16},{3,17},{4,22},{5,23},{6,20},{7,21},{8,26},{9,... | collective-permute-start | bytes 196616 | tf_op jit(solution)/shard_map/ppermute | solution.py:62
  64.8 1.2 %collective-permute-done.12.theirs = f32[128,128]{1,0:T(8,128)S(1)} collective-permute-done((f32[128,128]{1,0:T(8,128)S(1)}, f32[128,128]{1,0:T(8,128)S(1)}, u32[]{:S(2)}, u32[]{:S(2)}) %collective-permute-start.12) | collective-permute-done | bytes 65568 | tf_op jit(solution)/shard_map/ppermute | solution.py:62
  66.0 1.5 %collective-permute-start.17 = (f32[128,384]{1,0:T(8,128)S(1)}, f32[128,384]{1,0:T(8,128)S(1)}, u32[]{:S(2)}, u32[]{:S(2)}) collective-permute-start(f32[128,384]{1,0:T(8,128)S(1)} %get-tuple-element.48), channel_id=1, source_target_pairs={{0,1},{1,0},{2,3},{3,2},{4,5},{5,4},{6,7},{7,6},{8,9},{9,8},{10,11... | collective-permute-start | bytes 589832 | tf_op jit(solution)/shard_map/ppermute | solution.py:62
  67.5 3.5 %inverse_factor.1.inverse = f32[128,128]{1,0:T(8,128)S(1)} custom-call(f32[128,128]{1,0:T(8,128)S(1)} %slice_add_fusion.1.mine, f32[128,128]{1,0:T(8,128)S(1)} %collective-permute-done.12.theirs), custom_call_target="tpu_custom_call" | custom-call | flops 1000000 | bytes 100000 | tf_op jit(solution)/shard_map/inverse_factor/pallas_call | solution.py:204
  71.0 1.8 %basis.1 = f32[1536,128]{1,0:T(8,128)} custom-call(s32[3]{0:T(128)S(1)} %pad_add_fusion.refs_0_.place, f32[128,128]{1,0:T(8,128)S(1)} %inverse_factor.1.inverse, f32[128,384]{1,0:T(8,128)S(1)} %turn.1.mine.refs_0_, f32[128,384]{1,0:T(8,128)S(1)} %collective-permute-done.7.one.refs_1_, f32[128,384]{1,0:T(8,128)S(1)} %collective-permute-done.8.two.refs_2_, ...), custom_call_target="tpu_custom_call" | custom-call | flops 1000000 | bytes 100000 | tf_op jit(solution)/shard_map/basis/pallas_call | solution.py:413
  72.9 1.3 %finish.1 = f32[1536,128]{1,0:T(8,128)} custom-call(f32[128,128]{1,0:T(8,128)S(1)} %inverse_factor.1.inverse, f32[128,896]{1,0:T(8,128)S(1)} %collective-permute-done.13.far_a, f32[128,640]{1,0:T(8,128)S(1)} %collective-permute-done.14.far_b, f32[128,384]{1,0:T(8,128)S(1)} %get-tuple-element.42.refs_0_, f32[128,384]{1,0:T(8,128)S(1)} %get-tuple-element.43.refs_1_, ...), custom_call_target="tpu_custom_call" | custom-call | flops 1000000 | bytes 100000 | tf_op jit(solution)/shard_map/finish/pallas_call | solution.py:429
  (41 shorter events, 6.7 us)
Async XLA Ops:
  0.8 1.4 %copy-start = (bf16[6144,128]{1,0:T(8,128)(2,1)S(1)}, bf16[6144,128]{1,0:T(8,128)(2,1)}, u32[]{:S(2)}) copy-start(bf16[6144,128]{1,0:T(8,128)(2,1)} %refs_3_.3) | copy-start | bytes 4718596
  2.2 0.7 copy-start.1
  10.2 11.3 %collective-permute-start = (f32[384,128]{1,0:T(8,128)S(1)}, f32[384,128]{1,0:T(8,128)S(1)}, u32[]{:S(2)}, u32[]{:S(2)}) collective-permute-start(f32[384,128]{1,0:T(8,128)S(1)} %get-tuple-element.26), channel_id=1, source_target_pairs={{0,36},{1,109},{2,38},{3,111},{4,32},{5,105},{6,34},{7,107},{8,44}... | collective-permute-start | bytes 589832 | tf_op jit(solution)/shard_map/ppermute | solution.py:62
  17.3 5.7 %collective-permute-start.1 = (f32[384,128]{1,0:T(8,128)S(1)}, f32[384,128]{1,0:T(8,128)S(1)}, u32[]{:S(2)}, u32[]{:S(2)}) collective-permute-start(f32[384,128]{1,0:T(8,128)S(1)} %get-tuple-element.27), channel_id=1, source_target_pairs={{0,4},{1,13},{2,6},{3,15},{4,0},{5,9},{6,2},{7,11},{8,12},{9,5},{1... | collective-permute-start | bytes 589832 | tf_op jit(solution)/shard_map/ppermute | solution.py:62
  17.3 8.5 %copy-start.2 = (s32[12,48]{1,0:T(8,128)S(1)}, s32[12,48]{1,0:T(8,128)}, u32[]{:S(2)}) copy-start(s32[12,48]{1,0:T(8,128)} %keep_mask.1) | copy-start | bytes 6916
  17.3 5.7 %collective-permute-start.2 = (f32[384,128]{1,0:T(8,128)S(1)}, f32[384,128]{1,0:T(8,128)S(1)}, u32[]{:S(2)}, u32[]{:S(2)}) collective-permute-start(f32[384,128]{1,0:T(8,128)S(1)} %get-tuple-element.28), channel_id=1, source_target_pairs={{0,32},{1,97},{2,34},{3,99},{4,36},{5,101},{6,38},{7,103},{8,40},{... | collective-permute-start | bytes 589832 | tf_op jit(solution)/shard_map/ppermute | solution.py:62
  23.1 5.9 %collective-permute-start.5 = (f32[384,128]{1,0:T(8,128)S(1)}, f32[384,128]{1,0:T(8,128)S(1)}, u32[]{:S(2)}, u32[]{:S(2)}) collective-permute-start(f32[384,128]{1,0:T(8,128)S(1)} %add_add_fusion.1.refs_3_), channel_id=1, source_target_pairs={{0,108},{1,37},{2,110},{3,39},{4,104},{5,33},{6,106},{7,35},{8,100... | collective-permute-start | bytes 589832 | tf_op jit(solution)/shard_map/ppermute | solution.py:62
  23.1 7.0 %collective-permute-start.4 = (f32[384,128]{1,0:T(8,128)S(1)}, f32[384,128]{1,0:T(8,128)S(1)}, u32[]{:S(2)}, u32[]{:S(2)}) collective-permute-start(f32[384,128]{1,0:T(8,128)S(1)} %add_add_fusion.1.refs_3_), channel_id=1, source_target_pairs={{0,96},{1,33},{2,98},{3,35},{4,100},{5,37},{6,102},{7,39},{8,104},... | collective-permute-start | bytes 589832 | tf_op jit(solution)/shard_map/ppermute | solution.py:62
  24.3 5.8 %collective-permute-start.3 = (f32[384,128]{1,0:T(8,128)S(1)}, f32[384,128]{1,0:T(8,128)S(1)}, u32[]{:S(2)}, u32[]{:S(2)}) collective-permute-start(f32[384,128]{1,0:T(8,128)S(1)} %add_add_fusion.1.refs_3_), channel_id=1, source_target_pairs={{0,12},{1,5},{2,14},{3,7},{4,8},{5,1},{6,10},{7,3},{8,4},{9,13},{1... | collective-permute-start | bytes 589832 | tf_op jit(solution)/shard_map/ppermute | solution.py:62
  30.2 6.1 %collective-permute-start.6 = (f32[384,128]{1,0:T(8,128)S(1)}, f32[384,128]{1,0:T(8,128)S(1)}, u32[]{:S(2)}, u32[]{:S(2)}) collective-permute-start(f32[384,128]{1,0:T(8,128)S(1)} %add_add_fusion.refs_3_), channel_id=1, source_target_pairs={{0,16},{1,17},{2,18},{3,19},{4,20},{5,21},{6,22},{7,23},{8,24},{9,... | collective-permute-start | bytes 589832 | tf_op jit(solution)/shard_map/ppermute | solution.py:62
  36.5 7.9 %collective-permute-start.9 = (f32[128,384]{1,0:T(8,128)S(1)}, f32[128,384]{1,0:T(8,128)S(1)}, u32[]{:S(2)}, u32[]{:S(2)}) collective-permute-start(f32[128,384]{1,0:T(8,128)S(1)} %turn.1.mine.refs_0_), channel_id=1, source_target_pairs={{0,36},{1,109},{2,38},{3,111},{4,32},{5,105},{6,34},{7,107},{8,44}... | collective-permute-start | bytes 589832 | tf_op jit(solution)/shard_map/ppermute | solution.py:62
  40.8 5.9 %collective-permute-start.8 = (f32[128,384]{1,0:T(8,128)S(1)}, f32[128,384]{1,0:T(8,128)S(1)}, u32[]{:S(2)}, u32[]{:S(2)}) collective-permute-start(f32[128,384]{1,0:T(8,128)S(1)} %turn.1.mine.refs_0_), channel_id=1, source_target_pairs={{0,4},{1,13},{2,6},{3,15},{4,0},{5,9},{6,2},{7,11},{8,12},{9,5},{1... | collective-permute-start | bytes 589832 | tf_op jit(solution)/shard_map/ppermute | solution.py:62
  40.8 5.9 %collective-permute-start.7 = (f32[128,384]{1,0:T(8,128)S(1)}, f32[128,384]{1,0:T(8,128)S(1)}, u32[]{:S(2)}, u32[]{:S(2)}) collective-permute-start(f32[128,384]{1,0:T(8,128)S(1)} %turn.1.mine.refs_0_), channel_id=1, source_target_pairs={{0,32},{1,97},{2,34},{3,99},{4,36},{5,101},{6,38},{7,103},{8,40},{... | collective-permute-start | bytes 589832 | tf_op jit(solution)/shard_map/ppermute | solution.py:62
  47.7 5.8 %collective-permute-start.11 = (f32[128,1024]{1,0:T(8,128)S(1)}, f32[128,1024]{1,0:T(8,128)S(1)}, u32[]{:S(2)}, u32[]{:S(2)}) collective-permute-start(f32[128,1024]{1,0:T(8,128)S(1)} %get-tuple-element.37), channel_id=1, source_target_pairs={{0,1},{1,0},{2,3},{3,2},{4,5},{5,4},{6,7},{7,6},{8,9},{9,8},{10,11... | collective-permute-start | bytes 1572872 | tf_op jit(solution)/shard_map/ppermute | solution.py:62
  51.7 1.7 %collective-permute-start.10 = (f32[128,640]{1,0:T(8,128)S(1)}, f32[128,640]{1,0:T(8,128)S(1)}, u32[]{:S(2)}, u32[]{:S(2)}) collective-permute-start(f32[128,640]{1,0:T(8,128)S(1)} %far.4), channel_id=1, source_target_pairs={{0,1},{1,0},{2,3},{3,2},{4,5},{5,4},{6,7},{7,6},{8,9},{9,8},{10,11... | collective-permute-start | bytes 983048 | tf_op jit(solution)/shard_map/ppermute | solution.py:62
  53.5 19.3 %collective-permute-start.13 = (f32[128,896]{1,0:T(8,128)S(1)}, f32[128,896]{1,0:T(8,128)S(1)}, u32[]{:S(2)}, u32[]{:S(2)}) collective-permute-start(f32[128,896]{1,0:T(8,128)S(1)} %slice_add_fusion), channel_id=1, source_target_pairs={{0,2},{1,3},{2,0},{3,1},{4,6},{5,7},{6,4},{7,5},{8,10},{9,11},{10,... | collective-permute-start | bytes 1376264 | tf_op jit(solution)/shard_map/ppermute | solution.py:62
  60.9 6.7 %collective-permute-start.15 = (f32[128,384]{1,0:T(8,128)S(1)}, f32[128,384]{1,0:T(8,128)S(1)}, u32[]{:S(2)}, u32[]{:S(2)}) collective-permute-start(f32[128,384]{1,0:T(8,128)S(1)} %get-tuple-element.46), channel_id=1, source_target_pairs={{0,1},{1,0},{2,3},{3,2},{4,5},{5,4},{6,7},{7,6},{8,9},{9,8},{10,11... | collective-permute-start | bytes 589832 | tf_op jit(solution)/shard_map/ppermute | solution.py:62
  61.4 11.5 %collective-permute-start.14 = (f32[128,640]{1,0:T(8,128)S(1)}, f32[128,640]{1,0:T(8,128)S(1)}, u32[]{:S(2)}, u32[]{:S(2)}) collective-permute-start(f32[128,640]{1,0:T(8,128)S(1)} %add.63), channel_id=1, source_target_pairs={{0,2},{1,3},{2,0},{3,1},{4,6},{5,7},{6,4},{7,5},{8,10},{9,11},{10,... | collective-permute-start | bytes 983048 | tf_op jit(solution)/shard_map/ppermute | solution.py:62
  61.7 4.3 %collective-permute-start.12 = (f32[128,128]{1,0:T(8,128)S(1)}, f32[128,128]{1,0:T(8,128)S(1)}, u32[]{:S(2)}, u32[]{:S(2)}) collective-permute-start(f32[128,128]{1,0:T(8,128)S(1)} %slice_add_fusion.1.mine), channel_id=1, source_target_pairs={{0,18},{1,19},{2,16},{3,17},{4,22},{5,23},{6,20},{7,21},{8,26},{9,... | collective-permute-start | bytes 196616 | tf_op jit(solution)/shard_map/ppermute | solution.py:62
  64.2 8.7 %collective-permute-start.16 = (f32[128,384]{1,0:T(8,128)S(1)}, f32[128,384]{1,0:T(8,128)S(1)}, u32[]{:S(2)}, u32[]{:S(2)}) collective-permute-start(f32[128,384]{1,0:T(8,128)S(1)} %get-tuple-element.47), channel_id=1, source_target_pairs={{0,1},{1,0},{2,3},{3,2},{4,5},{5,4},{6,7},{7,6},{8,9},{9,8},{10,11... | collective-permute-start | bytes 589832 | tf_op jit(solution)/shard_map/ppermute | solution.py:62
  66.0 6.8 %collective-permute-start.17 = (f32[128,384]{1,0:T(8,128)S(1)}, f32[128,384]{1,0:T(8,128)S(1)}, u32[]{:S(2)}, u32[]{:S(2)}) collective-permute-start(f32[128,384]{1,0:T(8,128)S(1)} %get-tuple-element.48), channel_id=1, source_target_pairs={{0,1},{1,0},{2,3},{3,2},{4,5},{5,4},{6,7},{7,6},{8,9},{9,8},{10,11... | collective-permute-start | bytes 589832 | tf_op jit(solution)/shard_map/ppermute | solution.py:62
  67.5 5.3 %collective-permute-start.18 = (f32[128,384]{1,0:T(8,128)S(1)}, f32[128,384]{1,0:T(8,128)S(1)}, u32[]{:S(2)}, u32[]{:S(2)}) collective-permute-start(f32[128,384]{1,0:T(8,128)S(1)} %get-tuple-element.49), channel_id=1, source_target_pairs={{0,1},{1,0},{2,3},{3,2},{4,5},{5,4},{6,7},{7,6},{8,9},{9,8},{10,11... | collective-permute-start | bytes 589832 | tf_op jit(solution)/shard_map/ppermute | solution.py:62
